TPU v7x, 128 devices: a whole 4x4x4 slice. The times are simulated.
128 devices in a mesh: space: 16 (over z, y), filt: 8 (over x, core).
Axes of the slice: x: 4, y: 4, z: 4, core: 2. Of those that a mesh axis runs over, the one named last changes fastest.
Arguments:
- volume: bfloat16 [16, 32, 4, 64, 256], P(None, 'space'), may hold values from -6 to 6
- weight_first: bfloat16 [27, 128, 64], P(None, 'filt'), may hold values from -0.15625 to 0.15625
- weight_second: bfloat16 [27, 256, 128], P(None, 'filt'), may hold values from -0.109375 to 0.109375
- cotangent: bfloat16 [16, 16, 2, 256, 128], P('space', None, None, 'filt'), may hold values from -0.09375 to 0.09375
Outputs:
- grad_first: float32 [27, 128, 64], P(None, 'filt')
- grad_second: float32 [27, 256, 128], P(None, 'filt')
All inputs are finite; a program needn't handle non-finite values.
Results may differ from a plain program's by a relative error of at most 0.0045.
Values may be sent and summed in bfloat16 or wider, within the bound.
No kernel may reach another device: no remote copies, remote signals or barrier semaphores. Data moves between devices by JAX's collectives and lax.ppermute only.
A program may use at most 384 MiB of HBM per device.

v0:
```python
import jax
import jax.numpy as jnp
from jax import lax
from jax.sharding import PartitionSpec as P


def with_halo(cells, sides, width):
    for axis, dim in sides:
        count = lax.axis_size(axis)
        ends = count - 1
        head = lax.slice_in_dim(cells, 0, width, axis=dim)
        tail = lax.slice_in_dim(cells, cells.shape[dim] - width, cells.shape[dim], axis=dim)
        cells = jnp.concatenate(
            [
                lax.ppermute(tail, axis, [(i, (i + 1) % count) for i in range(ends)]),
                cells,
                lax.ppermute(head, axis, [((i + 1) % count, i) for i in range(ends)]),
            ],
            axis=dim,
        )
    return cells


def pad_cells(field):
    return jnp.pad(field, ((0, 0), (1, 1), (1, 1), (0, 0), (1, 1)))


def convolve(padded, weight, depth, height, width):
    summed = None
    for offset in range(27):
        shift_depth, shift_rows, shift_cols = (offset // 9, offset // 3 % 3, offset % 3)
        window = padded[
            :,
            shift_depth : shift_depth + depth,
            shift_rows : shift_rows + height,
            :,
            shift_cols : shift_cols + width,
        ]
        product = jnp.einsum(
            "oc,szycx->szyox", weight[offset], window, preferred_element_type=jnp.float32
        )
        summed = product if summed is None else summed + product
    return summed


def weight_gradient(grads, padded, depth, height, width):
    parts = []
    for offset in range(27):
        shift_depth, shift_rows, shift_cols = (offset // 9, offset // 3 % 3, offset % 3)
        window = padded[
            :,
            shift_depth : shift_depth + depth,
            shift_rows : shift_rows + height,
            :,
            shift_cols : shift_cols + width,
        ]
        parts.append(
            jnp.einsum("szyox,szycx->oc", grads, window, preferred_element_type=jnp.float32)
        )
    return jnp.stack(parts)


def transpose_conv(padded_grad, weight, depth, height, width):
    summed = None
    for offset in range(27):
        shift_depth, shift_rows, shift_cols = (offset // 9, offset // 3 % 3, offset % 3)
        window = padded_grad[
            :,
            2 - shift_depth : 2 - shift_depth + depth,
            2 - shift_rows : 2 - shift_rows + height,
            :,
            2 - shift_cols : 2 - shift_cols + width,
        ]
        product = jnp.einsum(
            "oc,szyox->szycx", weight[offset], window, preferred_element_type=jnp.float32
        )
        summed = product if summed is None else summed + product
    return summed


def per_device(volume, weight_first, weight_second, cotangent):
    samples, depth_rows, height_cells, channels_in, width_cells = volume.shape
    mid_local = weight_first.shape[1]
    space_count = lax.axis_size("space")
    depth_pool, height_pool, width_half = (depth_rows // 2, height_cells // 2, width_cells // 2)
    depth_full = depth_pool * space_count
    with_faces = with_halo(volume, (("space", 1),), 1)
    padded_in = jnp.pad(with_faces, ((0, 0), (0, 0), (1, 1), (0, 0), (1, 1)))
    pre_first = convolve(padded_in, weight_first, depth_rows, height_cells, width_cells)
    activated, pull_first = jax.vjp(jax.nn.gelu, pre_first)
    pooled = (
        activated.reshape(samples, depth_pool, 2, height_pool, 2, mid_local, width_half, 2)
        .mean(axis=(2, 4, 7))
        .astype(jnp.bfloat16)
    )
    moved = lax.all_to_all(pooled, "space", split_axis=0, concat_axis=1, tiled=True)
    gathered = lax.all_gather(moved, "filt", axis=3, tiled=True)
    padded_pool = pad_cells(gathered)
    pre_second = convolve(padded_pool, weight_second, depth_full, height_pool, width_half)
    unused, pull_second = jax.vjp(jax.nn.gelu, pre_second)
    grad_out = pull_second(cotangent.astype(jnp.float32))[0].astype(jnp.bfloat16)
    second_terms = weight_gradient(grad_out, padded_pool, depth_full, height_pool, width_half)
    grad_second = lax.psum(second_terms, "space")
    partial_in = transpose_conv(
        pad_cells(grad_out), weight_second, depth_full, height_pool, width_half
    )
    input_grad = lax.psum_scatter(partial_in, "filt", scatter_dimension=3, tiled=True)
    returned = lax.all_to_all(input_grad, "space", split_axis=1, concat_axis=0, tiled=True)
    returned = (
        returned.reshape(samples, depth_pool, 1, height_pool, 1, mid_local, width_half, 1) / 8.0
    )
    upsampled = jnp.broadcast_to(
        returned, (samples, depth_pool, 2, height_pool, 2, mid_local, width_half, 2)
    ).reshape(pre_first.shape)
    inner_grad = pull_first(upsampled)[0].astype(jnp.bfloat16)
    first_terms = weight_gradient(inner_grad, padded_in, depth_rows, height_cells, width_cells)
    grad_first = lax.psum(first_terms, "space")
    return (grad_first, grad_second)


def solution(mesh):
    return jax.shard_map(
        per_device,
        mesh=mesh,
        in_specs=(
            P(None, "space", None, None, None),
            P(None, "filt", None),
            P(None, "filt", None),
            P("space", None, None, "filt", None),
        ),
        out_specs=(P(None, "filt", None), P(None, "filt", None)),
        check_vma=False,
    )
```

profile of v0, /device:TPU:0, one launch (start us, length us, event | category | flops | bytes accessed | tf_op | source)
XLA Modules:
  0.0 592.7 jit_solution(4452080812312901290)
XLA Ops:
  7.2 2.7 fusion.736
  9.9 3.7 collective-permute-start
  16.9 41.4 %collective-permute-done = bf16[16,1,4,64,256]{4,3,2,1,0:T(8,128)(2,1)S(1)} collective-permute-done((bf16[16,1,4,64,256]{4,3,2,1,0:T(8,128)(2,1)S(1)}, bf16[16,1,4,64,256]{4,3,2,1,0:T(8,128)(2,1)S(1)}, u32[]{:S(2)}, u32[]{:S(2)}) %collective-permute-start) | collective-permute-done | bytes 2097184 | tf_op jit(solution)/shard_map/ppermute | solution.py:15
  58.3 4.2 collective-permute-done.1
  62.6 17.3 %select_maximum_fusion = bf16[16,4,6,64,258]{4,3,2,1,0:T(8,128)(2,1)S(1)} fusion(bf16[16,1,4,64,256]{4,3,2,1,0:T(8,128)(2,1)S(1)} %collective-permute-done.1, bf16[16,2,4,64,256]{4,3,2,1,0:T(8,128)(2,1)S(1)} %copy-done.2, bf16[16,1,4,64,256]{4,3,2,1,0:T(8,128)(2,1)S(1)} %collective-permute-done), kind=kLoop, calls=%fused_computation.33 | loop fusion | flops 120471552 | bytes 21069824 | tf_op jit(solution)/shard_map/concatenate | solution.py:13
  79.9 3.3 fusion.523
  83.2 2.8 fusion.573
  86.0 2.7 fusion.571
  88.7 2.7 fusion.569
  93.5 2.7 fusion.563
  98.2 2.7 fusion.559
  100.9 2.7 fusion.557
  105.6 2.7 fusion.553
  108.4 3.2 fusion.551
  113.6 2.7 fusion.545
  118.3 2.7 fusion.541
  121.0 2.7 fusion.539
  125.7 2.7 fusion.535
  128.4 2.7 fusion.533
  133.2 2.7 fusion.527
  135.9 2.2 fusion.525
  138.1 2.3 pad_maximum_fusion.1
  140.4 5.7 fusion.565
  146.1 2.2 fusion.529
  148.3 17.8 %fusion.68 = (f32[16,4,16,256]{3,2,1,0:T(8,128)S(1)}, f32[16,2,4,16,256]{4,3,2,1,0:T(8,128)S(1)}) fusion(bf16[16,4,6,64,258]{4,3,2,1,0:T(8,128)(2,1)S(1)} %select_maximum_fusion, bf16[27,16,64]{2,1,0:T(8,128)(2,1)S(1)} %copy-done.58, f32[16,2,4,256,16]{3,4,2,1,0:T(8,128)} %fusion.523, f32[16,2,4,256,16]{3,4,2,1,0:T(8,128)} %fusion.525, ...), kind=kOutput, calls=%fused_computation.153 | convolution fusion | flops 85196800 | bytes 61870080 | tf_op jit(solution)/shard_map/oc,szycx->szyox/dot_general | solution.py:39
  166.1 6.1 %copy.226 = f32[16,4,16,256]{2,0,3,1:T(8,128)} copy(f32[16,4,16,256]{3,2,1,0:T(8,128)S(1)} %get-tuple-element.58) | data formatting | bytes 2097152 | tf_op jit(solution)/shard_map/reduce_sum | solution.py:93
  172.2 6.2 %reduce_sum.18 = f32[16,2,16,128]{2,0,3,1:T(8,128)} reduce(f32[16,2,2,16,128,2]{3,0,5,4,2,1:T(8,128)} %bitcast.1333, f32[]{:T(128)} %constant.5.clone.1), dimensions={2,5}, to_apply=%region_1.2 | reduce | flops 196608 | bytes 1310724 | tf_op jit(solution)/shard_map/reduce_sum | solution.py:93
  181.6 9.4 %all-to-all-start = ((bf16[16,1,2,16,128]{4,3,2,1,0:T(8,128)(2,1)}), bf16[16,1,2,16,128]{4,3,2,1,0:T(8,128)(2,1)S(1)}, u32[]{:S(2)}, u32[]{:S(2)}) async-start(bf16[16,1,2,16,128]{4,3,2,1,0:T(8,128)(2,1)} %copy.227), calls=%async_computation | async-start | bytes 262144 | tf_op jit(solution)/shard_map/all_to_all | solution.py:96
  191.1 16.8 %fusion.735 = (bf16[16,2,4,64,256]{4,3,2,1,0:T(8,128)(2,1)}, bf16[16,2,4,64,256]{4,3,2,1,0:T(8,128)(2,1)}, bf16[16,2,4,64,256]{4,3,2,1,0:T(8,128)(2,1)}, bf16[16...) fusion(bf16[16,4,6,64,258]{4,3,2,1,0:T(8,128)(2,1)} %copy-done), kind=kLoop, calls=%fused_computation.719 | loop fusion | bytes 41943040 | tf_op jit(solution)/shard_map/slice | solution.py:32
  208.7 62.5 %fusion.734 = (bf16[16,2,4,64,256]{4,3,2,1,0:T(8,128)(2,1)}, bf16[16,2,4,64,256]{4,3,2,1,0:T(8,128)(2,1)}, bf16[16,2,4,64,256]{4,3,2,1,0:T(8,128)(2,1)}, bf16[16...) fusion(bf16[16,4,6,64,258]{4,3,2,1,0:T(8,128)(2,1)} %copy-done), kind=kLoop, calls=%fused_computation.718 | loop fusion | bytes 159383552 | tf_op jit(solution)/shard_map/slice | solution.py:32
  300.9 2.0 fusion.363
  333.7 3.9 fusion.296
  337.6 9.5 %fusion.297 = (bf16[16,2,128,128]{3,2,1,0:T(8,128)(2,1)}, bf16[16,2,128,128]{3,2,1,0:T(8,128)(2,1)}, bf16[16,2,128,128]{3,2,1,0:T(8,128)(2,1)}, bf16[16,2,128,12...) fusion(bf16[1,16,2,128,128]{4,3,2,1,0:T(8,128)(2,1)S(1)} %bitca, ...), kind=kLoop, calls=%fused_computation.328 | loop fusion | bytes 20971520 | tf_op jit(solution)/shard_map/reshape.59
  347.1 19.8 %bitcast_add_fusion = f32[1,16,2,128,128]{3,4,2,1,0:T(8,128)} fusion(f32[16,2,128,128]{3,2,1,0:T(8,128)} %fusion.408, f32[16,2,128,128]{3,2,1,0:T(8,128)} %fusion.405, f32[16,2,128,128]{3,2,1,0:T(8,128)} %fusion.402, f32[16,2,128,128]{3,2,1,0:T(8,128)} %fusion.399, f32[16,2,128,128]{3,2,1,0:T(8,128)} %fusion.396, f32[16,2,128,128]{3,2,1,0:T(8,128)} %fusion.393, ...), kind=kOutput, calls=%fused_computation.130 | convolution fusion | flops 47185920 | bytes 56893440 | tf_op jit(solution)/shard_map/oc,szyox->szycx/dot_general | solution.py:74
  366.9 3.3 copy.229
  370.3 2.4 fusion.108
  372.7 2.4 fusion.107
  375.1 2.4 fusion.106
  401.8 3.7 reduce-scatter.2.cloned.1.call-done
  407.4 7.0 %all-to-all-start.1 = ((f32[1,16,2,16,128]{4,3,2,0,1:T(8,128)}), f32[1,16,2,16,128]{4,3,2,0,1:T(8,128)}, u32[]{:S(2)}, u32[]{:S(2)}) async-start(f32[1,16,2,16,128]{4,3,2,0,1:T(8,128)} %copy.230), calls=%async_computation.2 | async-start | bytes 524288 | tf_op jit(solution)/shard_map/all_to_all | solution.py:108
  415.5 7.6 %all-to-all-done.1 = f32[1,16,2,16,128]{4,3,2,0,1:T(8,128)} async-done(((f32[1,16,2,16,128]{4,3,2,0,1:T(8,128)}), f32[1,16,2,16,128]{4,3,2,0,1:T(8,128)}, u32[]{:S(2)}, u32[]{:S(2)}) %all-to-all-start.1) | async-done | bytes 262176 | tf_op jit(solution)/shard_map/all_to_all | solution.py:108
  424.1 2.0 copy.231
  426.2 5.6 broadcast_in_dim.9
  431.8 5.1 copy.233
  436.9 7.3 %broadcast_multiply_fusion = f32[16,4,16,256]{2,0,3,1:T(8,128)} fusion(f32[16,4,16,256]{2,0,3,1:T(8,128)} %bitcast.1332), kind=kLoop, calls=%fused_computation.120 | loop fusion | flops 262144 | bytes 2097152 | tf_op jit(solution)/shard_map/transpose(jvp())/mul | solution.py:90
  444.2 6.2 %copy.232 = f32[16,4,16,256]{3,2,1,0:T(8,128)} copy(f32[16,4,16,256]{2,0,3,1:T(8,128)} %broadcast_multiply_fusion) | data formatting | bytes 2097152 | tf_op jit(solution)/shard_map/transpose(jvp())/mul | solution.py:90
  450.5 2.7 fusion.66
  501.6 81.0 %all-reduce.6.cloned.1.call-done = (f32[27,16,64]{2,1,0:T(8,128)}, f32[27,32,128]{2,1,0:T(8,128)}) async-done(((f32[27,16,64]{2,1,0:T(8,128)}, f32[27,32,128]{2,1,0:T(8,128)}), (f32[27,16,64]{2,1,0:T(8,128)}, f32[27,32,128]{2,1,0:T(8,128)})) %all-reduce.6.cloned.1.call-update) | async-done | bytes 552976 | tf_op jit(solution)/shard_map/psum | solution.py:117
  (246 shorter events, 161.9 us)
Async XLA Ops:
  7.2 7.7 %copy-start.2 = (bf16[16,2,4,64,256]{4,3,2,1,0:T(8,128)(2,1)S(1)}, bf16[16,2,4,64,256]{4,3,2,1,0:T(8,128)(2,1)}, u32[]{:S(2)}) copy-start(bf16[16,2,4,64,256]{4,3,2,1,0:T(8,128)(2,1)} %param.4) | copy-start | bytes 12582916
  7.2 7.7 %copy-start.58 = (bf16[27,16,64]{2,1,0:T(8,128)(2,1)S(1)}, bf16[27,16,64]{2,1,0:T(8,128)(2,1)}, u32[]{:S(2)}) copy-start(bf16[27,16,64]{2,1,0:T(8,128)(2,1)} %param.5) | copy-start | bytes 165892
  9.9 48.4 %collective-permute-start = (bf16[16,1,4,64,256]{4,3,2,1,0:T(8,128)(2,1)S(1)}, bf16[16,1,4,64,256]{4,3,2,1,0:T(8,128)(2,1)S(1)}, u32[]{:S(2)}, u32[]{:S(2)}) collective-permute-start(bf16[16,1,4,64,256]{4,3,2,1,0:T(8,128)(2,1)S(1)} %get-tuple-element.30), channel_id=1, source_target_pairs={{0,8},{8,16},{16,24},{24,32},{32,40},{40,48},{48,56},{56,64},{64,7... | collective-permute-start | bytes 6291464 | tf_op jit(solution)/shard_map/ppermute | solution.py:15
  13.6 49.0 %collective-permute-start.1 = (bf16[16,1,4,64,256]{4,3,2,1,0:T(8,128)(2,1)S(1)}, bf16[16,1,4,64,256]{4,3,2,1,0:T(8,128)(2,1)S(1)}, u32[]{:S(2)}, u32[]{:S(2)}) collective-permute-start(bf16[16,1,4,64,256]{4,3,2,1,0:T(8,128)(2,1)S(1)} %get-tuple-element.31), channel_id=1, source_target_pairs={{8,0},{16,8},{24,16},{32,24},{40,32},{48,40},{56,48},{64,56},{72,6... | collective-permute-start | bytes 6291464 | tf_op jit(solution)/shard_map/ppermute | solution.py:17
  79.9 68.4 %copy-start = (bf16[16,4,6,64,258]{4,3,2,1,0:T(8,128)(2,1)}, bf16[16,4,6,64,258]{4,3,2,1,0:T(8,128)(2,1)S(1)}, u32[]{:S(2)}) copy-start(bf16[16,4,6,64,258]{4,3,2,1,0:T(8,128)(2,1)S(1)} %select_maximum_fusion) | copy-start | bytes 38043652
  140.4 5.7 copy-start.4
  181.6 26.3 %all-to-all-start = ((bf16[16,1,2,16,128]{4,3,2,1,0:T(8,128)(2,1)}), bf16[16,1,2,16,128]{4,3,2,1,0:T(8,128)(2,1)S(1)}, u32[]{:S(2)}, u32[]{:S(2)}) async-start(bf16[16,1,2,16,128]{4,3,2,1,0:T(8,128)(2,1)} %copy.227), calls=%async_computation | async-start | bytes 262144 | tf_op jit(solution)/shard_map/all_to_all | solution.py:96
  191.0 80.1 %all-gather.3.cloned.1.call-start = ((), (), s32[]{:S(2)}) async-start(), calls=%async_computation.4 | async-start | bytes 1179648 | tf_op jit(solution)/shard_map/all_gather | solution.py:97
  208.6 62.6 %copy-start.54 = (bf16[27,32,128]{2,1,0:T(8,128)(2,1)S(1)}, bf16[27,32,128]{2,1,0:T(8,128)(2,1)}, u32[]{:S(2)}) copy-start(bf16[27,32,128]{2,1,0:T(8,128)(2,1)} %param.6) | copy-start | bytes 663556
  208.6 196.9 %reduce-scatter.2.cloned.1.call-start = ((), (), s32[]{:S(2)}) async-start(), calls=%async_computation.3 | async-start | bytes 2359296 | tf_op jit(solution)/shard_map/reduce_scatter | solution.py:107
  271.2 4.1 copy-start.1
  370.3 7.2 %copy-start.47 = (bf16[16,2,128,128]{3,2,1,0:T(8,128)(2,1)S(1)}, bf16[16,2,128,128]{3,2,1,0:T(8,128)(2,1)}, u32[]{:S(2)}) copy-start(bf16[16,2,128,128]{3,2,1,0:T(8,128)(2,1)} %get-tuple-element.35) | copy-start | bytes 3145732
  370.3 8.3 %copy-start.46 = (bf16[16,2,128,128]{3,2,1,0:T(8,128)(2,1)S(1)}, bf16[16,2,128,128]{3,2,1,0:T(8,128)(2,1)}, u32[]{:S(2)}) copy-start(bf16[16,2,128,128]{3,2,1,0:T(8,128)(2,1)} %get-tuple-element.36) | copy-start | bytes 3145732
  370.3 9.3 %copy-start.45 = (bf16[16,2,128,128]{3,2,1,0:T(8,128)(2,1)S(1)}, bf16[16,2,128,128]{3,2,1,0:T(8,128)(2,1)}, u32[]{:S(2)}) copy-start(bf16[16,2,128,128]{3,2,1,0:T(8,128)(2,1)} %get-tuple-element.37) | copy-start | bytes 3145732
  370.3 10.4 %copy-start.44 = (bf16[16,2,128,128]{3,2,1,0:T(8,128)(2,1)S(1)}, bf16[16,2,128,128]{3,2,1,0:T(8,128)(2,1)}, u32[]{:S(2)}) copy-start(bf16[16,2,128,128]{3,2,1,0:T(8,128)(2,1)} %get-tuple-element.38) | copy-start | bytes 3145732
  372.7 9.0 %copy-start.43 = (bf16[16,2,128,128]{3,2,1,0:T(8,128)(2,1)S(1)}, bf16[16,2,128,128]{3,2,1,0:T(8,128)(2,1)}, u32[]{:S(2)}) copy-start(bf16[16,2,128,128]{3,2,1,0:T(8,128)(2,1)} %get-tuple-element.39) | copy-start | bytes 3145732
  375.1 7.7 %copy-start.42 = (bf16[16,2,128,128]{3,2,1,0:T(8,128)(2,1)S(1)}, bf16[16,2,128,128]{3,2,1,0:T(8,128)(2,1)}, u32[]{:S(2)}) copy-start(bf16[16,2,128,128]{3,2,1,0:T(8,128)(2,1)} %get-tuple-element.40) | copy-start | bytes 3145732
  377.5 6.4 %copy-start.41 = (bf16[16,2,128,128]{3,2,1,0:T(8,128)(2,1)S(1)}, bf16[16,2,128,128]{3,2,1,0:T(8,128)(2,1)}, u32[]{:S(2)}) copy-start(bf16[16,2,128,128]{3,2,1,0:T(8,128)(2,1)} %get-tuple-element.41) | copy-start | bytes 3145732
  378.5 6.4 %copy-start.40 = (bf16[16,2,128,128]{3,2,1,0:T(8,128)(2,1)S(1)}, bf16[16,2,128,128]{3,2,1,0:T(8,128)(2,1)}, u32[]{:S(2)}) copy-start(bf16[16,2,128,128]{3,2,1,0:T(8,128)(2,1)} %get-tuple-element.42) | copy-start | bytes 3145732
  379.6 6.4 %copy-start.39 = (bf16[16,2,128,128]{3,2,1,0:T(8,128)(2,1)S(1)}, bf16[16,2,128,128]{3,2,1,0:T(8,128)(2,1)}, u32[]{:S(2)}) copy-start(bf16[16,2,128,128]{3,2,1,0:T(8,128)(2,1)} %get-tuple-element.43) | copy-start | bytes 3145732
  380.7 6.4 %copy-start.38 = (bf16[16,2,128,128]{3,2,1,0:T(8,128)(2,1)S(1)}, bf16[16,2,128,128]{3,2,1,0:T(8,128)(2,1)}, u32[]{:S(2)}) copy-start(bf16[16,2,128,128]{3,2,1,0:T(8,128)(2,1)} %get-tuple-element.44) | copy-start | bytes 3145732
  382.8 6.4 %copy-start.37 = (bf16[16,2,128,128]{3,2,1,0:T(8,128)(2,1)S(1)}, bf16[16,2,128,128]{3,2,1,0:T(8,128)(2,1)}, u32[]{:S(2)}) copy-start(bf16[16,2,128,128]{3,2,1,0:T(8,128)(2,1)} %get-tuple-element.45) | copy-start | bytes 3145732
  383.8 6.4 %copy-start.36 = (bf16[16,2,128,128]{3,2,1,0:T(8,128)(2,1)S(1)}, bf16[16,2,128,128]{3,2,1,0:T(8,128)(2,1)}, u32[]{:S(2)}) copy-start(bf16[16,2,128,128]{3,2,1,0:T(8,128)(2,1)} %get-tuple-element.46) | copy-start | bytes 3145732
  384.9 6.4 %copy-start.35 = (bf16[16,2,128,128]{3,2,1,0:T(8,128)(2,1)S(1)}, bf16[16,2,128,128]{3,2,1,0:T(8,128)(2,1)}, u32[]{:S(2)}) copy-start(bf16[16,2,128,128]{3,2,1,0:T(8,128)(2,1)} %get-tuple-element.47) | copy-start | bytes 3145732
  386.0 6.4 %copy-start.34 = (bf16[16,2,128,128]{3,2,1,0:T(8,128)(2,1)S(1)}, bf16[16,2,128,128]{3,2,1,0:T(8,128)(2,1)}, u32[]{:S(2)}) copy-start(bf16[16,2,128,128]{3,2,1,0:T(8,128)(2,1)} %get-tuple-element.48) | copy-start | bytes 3145732
  387.0 6.4 %copy-start.33 = (bf16[16,2,128,128]{3,2,1,0:T(8,128)(2,1)S(1)}, bf16[16,2,128,128]{3,2,1,0:T(8,128)(2,1)}, u32[]{:S(2)}) copy-start(bf16[16,2,128,128]{3,2,1,0:T(8,128)(2,1)} %get-tuple-element.49) | copy-start | bytes 3145732
  388.1 6.4 %copy-start.32 = (bf16[16,2,128,128]{3,2,1,0:T(8,128)(2,1)S(1)}, bf16[16,2,128,128]{3,2,1,0:T(8,128)(2,1)}, u32[]{:S(2)}) copy-start(bf16[16,2,128,128]{3,2,1,0:T(8,128)(2,1)} %get-tuple-element.50) | copy-start | bytes 3145732
  389.1 6.4 %copy-start.53 = (bf16[16,2,128,128]{3,2,1,0:T(8,128)(2,1)S(1)}, bf16[16,2,128,128]{3,2,1,0:T(8,128)(2,1)}, u32[]{:S(2)}) copy-start(bf16[16,2,128,128]{3,2,1,0:T(8,128)(2,1)} %get-tuple-element.52) | copy-start | bytes 3145732
  390.2 6.4 %copy-start.52 = (bf16[16,2,128,128]{3,2,1,0:T(8,128)(2,1)S(1)}, bf16[16,2,128,128]{3,2,1,0:T(8,128)(2,1)}, u32[]{:S(2)}) copy-start(bf16[16,2,128,128]{3,2,1,0:T(8,128)(2,1)} %get-tuple-element.53) | copy-start | bytes 3145732
  391.3 6.4 %copy-start.51 = (bf16[16,2,128,128]{3,2,1,0:T(8,128)(2,1)S(1)}, bf16[16,2,128,128]{3,2,1,0:T(8,128)(2,1)}, u32[]{:S(2)}) copy-start(bf16[16,2,128,128]{3,2,1,0:T(8,128)(2,1)} %get-tuple-element.54) | copy-start | bytes 3145732
  392.3 6.4 %copy-start.50 = (bf16[16,2,128,128]{3,2,1,0:T(8,128)(2,1)S(1)}, bf16[16,2,128,128]{3,2,1,0:T(8,128)(2,1)}, u32[]{:S(2)}) copy-start(bf16[16,2,128,128]{3,2,1,0:T(8,128)(2,1)} %get-tuple-element.55) | copy-start | bytes 3145732
  393.4 6.4 %copy-start.49 = (bf16[16,2,128,128]{3,2,1,0:T(8,128)(2,1)S(1)}, bf16[16,2,128,128]{3,2,1,0:T(8,128)(2,1)}, u32[]{:S(2)}) copy-start(bf16[16,2,128,128]{3,2,1,0:T(8,128)(2,1)} %get-tuple-element.56) | copy-start | bytes 3145732
  394.4 6.4 %copy-start.48 = (bf16[16,2,128,128]{3,2,1,0:T(8,128)(2,1)S(1)}, bf16[16,2,128,128]{3,2,1,0:T(8,128)(2,1)}, u32[]{:S(2)}) copy-start(bf16[16,2,128,128]{3,2,1,0:T(8,128)(2,1)} %get-tuple-element.51) | copy-start | bytes 3145732
  396.6 17.9 %copy-start.31 = (bf16[16,2,128,128]{3,2,1,0:T(8,128)(2,1)S(1)}, bf16[16,2,128,128]{3,2,1,0:T(8,128)(2,1)}, u32[]{:S(2)}) copy-start(bf16[16,2,128,128]{3,2,1,0:T(8,128)(2,1)} %get-tuple-element.32) | copy-start | bytes 3145732
  407.4 15.8 %all-to-all-start.1 = ((f32[1,16,2,16,128]{4,3,2,0,1:T(8,128)}), f32[1,16,2,16,128]{4,3,2,0,1:T(8,128)}, u32[]{:S(2)}, u32[]{:S(2)}) async-start(f32[1,16,2,16,128]{4,3,2,0,1:T(8,128)} %copy.230), calls=%async_computation.2 | async-start | bytes 524288 | tf_op jit(solution)/shard_map/all_to_all | solution.py:108
  414.4 168.1 %all-reduce.6.cloned.1.call-start = ((), (), s32[]{:S(2)}) async-start(), calls=%async_computation.5 | async-start | bytes 1327104 | tf_op jit(solution)/shard_map/psum | solution.py:117
  450.4 2.7 copy-start.28
  450.5 3.9 copy-start.26
  455.6 2.5 copy-start.22
  461.2 2.5 copy-start.30
  464.9 2.4 copy-start.27
  468.5 2.4 copy-start.23
  477.4 2.5 copy-start.17
  481.1 2.4 copy-start.15
  484.6 2.4 copy-start.13
  490.0 2.4 copy-start.5
  493.6 2.5 copy-start.9
  497.3 2.4 copy-start.7
  (19 other events, 38.2 us)
Sparse Core Ops, SparseCore 0:
  208.7 24.8 all-gather.2
  370.4 35.1 reduce-scatter.1
  501.7 80.7 all-reduce.5
where the time goes:
time: 597 us; the launch traced here: 593 us
  matrix products  233 us (39%)
  local copies, waits for them, and re-layouts  148 us (25%)
  waiting for transfers between devices  138 us (23%)
  other arithmetic  38.5 us (6%)
  starting transfers between devices  21.5 us (4%)
  between operations  14.3 us (2%)
    dot_general x54, matrix products, convolve(): jnp.einsum('oc,szycx->szyox', weight[offset], window, preferred_element_t...  98.5 us
    psum x1, waiting for transfers between devices, per_device(): grad_first = lax.psum(first_terms, 'space')  81 us
    slice x2, local copies, waits for them, and re-layouts, convolve(): padded[:, shift_depth:shift_depth + depth, shift_rows:shift_rows + height...  79.3 us
    dot_general x27, matrix products, transpose_conv(): jnp.einsum('oc,szyox->szycx', weight[offset], window, preferred_element_t...  69.5 us
    dot_general x54, matrix products, weight_gradient(): jnp.einsum('szyox,szycx->oc', grads, window, preferred_element_type=jnp.f...  64.7 us
    ppermute x1, waiting for transfers between devices, with_halo(): lax.ppermute(tail, axis, [(i, (i + 1) % count) for i in range(ends)])  41.4 us
    unnamed x122, local copies, waits for them, and re-layouts  20.4 us
    concatenate x2, other arithmetic, with_halo(): jnp.concatenate([lax.ppermute(tail, axis, [(i, (i + 1) % count) for i in...  19.6 us
  transfers between devices with their start and end apart: 7, of which 5 were waited for; matrix products, arithmetic and copies ran while one was open for 19% of the time, Pallas kernels for 0%

commit v1 on v0

v1 whole, which is shorter than its diff:
```python
import functools

import jax
import jax.numpy as jnp
from jax import lax
from jax.experimental import pallas as pl
from jax.experimental.pallas import tpu as pltpu
from jax.sharding import PartitionSpec as P

BF = jnp.bfloat16
F32 = jnp.float32
ROOT = 0.7978845608028654
CUBE = 0.044715


def dot(a, b):
    return lax.dot_general(a, b, (((1,), (0,)), ((), ())), preferred_element_type=F32)


def dot_nt(a, b):
    return lax.dot_general(a, b, (((1,), (1,)), ((), ())), preferred_element_type=F32)


def dot_tn(a, b):
    return lax.dot_general(a, b, (((0,), (0,)), ((), ())), preferred_element_type=F32)


def gelu_and_slope(v):
    square = v * v
    t = jnp.tanh(ROOT * v * (1.0 + CUBE * square))
    half = 0.5 * (1.0 + t)
    slope = half + 0.5 * v * (1.0 - t * t) * (ROOT * (1.0 + 3.0 * CUBE * square))
    return v * half, slope


def split_shift(e):
    row = lax.broadcasted_iota(jnp.int32, (256, 256), 0)
    col = lax.broadcasted_iota(jnp.int32, (256, 256), 1)
    source = 2 * (col & 127) + (col >> 7) + (e - 1)
    return jnp.where(row == source, 1.0, 0.0).astype(BF)


def pair_shift(e):
    row = lax.broadcasted_iota(jnp.int32, (256, 256), 0)
    col = lax.broadcasted_iota(jnp.int32, (256, 256), 1)
    same = (row >> 7) == (col >> 7)
    return jnp.where(same & ((row & 127) == (col & 127) + (e - 1)), 1.0, 0.0).astype(BF)


def first_forward(own, low, high, weight, taps, slope, pooled):
    shifts = [split_shift(e) for e in range(3)]

    @pl.loop(0, 2)
    def _(s):
        for depth in range(4):
            if depth == 0:
                cells = low[s]
            elif depth == 3:
                cells = high[s]
            else:
                cells = own[s, depth - 1]
            cells = cells.reshape(256, 256)
            for e in range(3):
                taps[s, depth, :, e * 64 : (e + 1) * 64, :] = (
                    dot(cells, shifts[e]).astype(BF).reshape(4, 64, 256)
                )
        for pair in range(2):
            total = None
            for z in range(2):
                for y in (2 * pair, 2 * pair + 1):
                    first, last = max(y - 1, 0), min(y + 2, 4)
                    left = (first - y + 1) * 192
                    size = (last - first) * 192
                    pre = None
                    for a in range(3):
                        w = weight[:, a].reshape(128, 576)[:, left : left + size]
                        part = dot(w, taps[s, z + a, first:last].reshape(size, 256))
                        pre = part if pre is None else pre + part
                    value, rate = gelu_and_slope(pre)
                    slope[s, z, y] = rate
                    total = value if total is None else total + value
            pooled[s, pair] = ((total[:, :128] + total[:, 128:]) * 0.125).astype(BF)


def second_layer(parity, own, low, high, weight, cot_a, cot_b, grads, taps, mid, down, up, spread):
    left, right = pair_shift(0), pair_shift(2)
    for a, field in enumerate((low, own, high)):
        for y in range(2):
            cells = jnp.concatenate([field[0, y], field[1, y]], axis=1)
            taps[a, y, 0:128] = dot(cells, left).astype(BF)
            taps[a, y, 128:256] = cells
            taps[a, y, 256:384] = dot(cells, right).astype(BF)
    even = parity[0] == 0
    for y in range(2):
        pre = None
        for a in range(3):
            base = 9 * a + 3 * (1 - y)
            w = jnp.concatenate([weight[:, base + j].reshape(256, 128) for j in range(6)], axis=1)
            part = dot(w, taps[a].reshape(768, 256))
            pre = part if pre is None else pre + part
        _, rate = gelu_and_slope(pre)
        one = cot_a[:, y].reshape(256, 128).astype(F32)
        two = cot_b[:, y].reshape(256, 128).astype(F32)
        cot = jnp.concatenate([jnp.where(even, one, two), jnp.where(even, two, one)], axis=1)
        grad = (cot * rate).astype(BF)
        grads[y] = grad
        spread[y, 0] = dot(grad, right).astype(BF)
        spread[y, 1] = grad
        spread[y, 2] = dot(grad, left).astype(BF)
    for a, out in enumerate((down, mid, up)):
        for y in range(2):
            total = None
            for source in range(2):
                base = 9 * a + 3 * (y - source + 1)
                w = jnp.concatenate([weight[:, base + e].reshape(256, 128) for e in range(3)], axis=0)
                part = dot_tn(w, spread[source].reshape(768, 256))
                total = part if total is None else total + part
            out[y] = total.astype(out.dtype)


def second_weights(grads, taps, out):
    for a in range(3):
        for b in range(3):
            total = None
            for y in range(2):
                row = y + b - 1
                if 0 <= row < 2:
                    part = dot_nt(grads[y], taps[a, row])
                    total = part if total is None else total + part
            k = (3 * a + b) * 384
            out[:, k : k + 384] = total.astype(BF)


def first_weights(taps, slope, mid, low, high, out, total):
    total[...] = jnp.zeros_like(total)

    @pl.loop(0, 2)
    def _(s):
        for pair in range(2):
            lanes = pl.ds(pl.multiple_of(s * 128, 128), 128)
            back = (
                mid[pair, :, lanes]
                + low[pair, :, lanes].astype(F32)
                + high[pair, :, lanes].astype(F32)
            ) * 0.125
            back = jnp.concatenate([back, back], axis=1)
            for z in range(2):
                for y in (2 * pair, 2 * pair + 1):
                    inner = (slope[s, z, y] * back).astype(BF)
                    first, last = max(y - 1, 0), min(y + 2, 4)
                    left = (first - y + 1) * 192
                    size = (last - first) * 192
                    for a in range(3):
                        total[a, :, left : left + size] += dot_nt(
                            inner, taps[s, z + a, first:last].reshape(size, 256)
                        )

    out[...] = jnp.concatenate([total[a] for a in range(3)], axis=1).astype(BF)


VMEM = pl.BlockSpec(memory_space=pltpu.VMEM)
SMEM = pl.BlockSpec(memory_space=pltpu.SMEM)


def call(kernel, ins, outs, scratch, flops, name):
    shapes = [jax.ShapeDtypeStruct(s, d) for s, d in outs]
    size = sum(x.size * x.dtype.itemsize for x in list(ins) + shapes)
    return pl.pallas_call(
        kernel,
        out_shape=shapes,
        in_specs=[SMEM if x.dtype == jnp.int32 else VMEM for x in ins],
        out_specs=[VMEM] * len(outs),
        scratch_shapes=scratch,
        compiler_params=pltpu.CompilerParams(vmem_limit_bytes=48 * 1024 * 1024),
        cost_estimate=pl.CostEstimate(flops=flops, bytes_accessed=size, transcendentals=0),
        name=name,
    )(*ins)


def per_device(volume, weight_first, weight_second, cotangent):
    space, filt = lax.axis_index("space"), lax.axis_index("filt")
    ns, nf = lax.axis_size("space"), lax.axis_size("filt")
    upward = [(i, i + 1) for i in range(ns - 1)]
    downward = [(i + 1, i) for i in range(ns - 1)]

    own = lax.dynamic_slice_in_dim(volume, 2 * filt, 2, axis=0)
    low = lax.ppermute(own[:, 1], "space", upward)
    high = lax.ppermute(own[:, 0], "space", downward)

    piece = weight_first.reshape(3, 9, 16, 64).transpose(0, 2, 1, 3).reshape(3, 16, 576)
    whole_first = lax.all_to_all(
        jnp.broadcast_to(piece[None], (nf,) + piece.shape), "filt", 0, 0, tiled=True
    )
    whole_second = lax.all_gather(weight_second, "filt", axis=0, tiled=False)

    cot = lax.all_to_all(cotangent.reshape(nf, 2, 2, 32, 128), "filt", 0, 0, tiled=True)
    parity = space % 2
    same = [
        (s * nf + f, (2 * f + s % 2) * nf + s // 2) for s in range(ns) for f in range(nf)
    ]
    other = [
        (s * nf + f, (2 * f + 1 - s % 2) * nf + s // 2) for s in range(ns) for f in range(nf)
    ]
    cot_a = lax.ppermute(
        lax.dynamic_index_in_dim(cot, parity, axis=1, keepdims=False), ("space", "filt"), same
    )
    cot_b = lax.ppermute(
        lax.dynamic_index_in_dim(cot, 1 - parity, axis=1, keepdims=False), ("space", "filt"), other
    )

    taps, slope, pooled = call(
        first_forward,
        (own, low, high, whole_first),
        (((2, 4, 4, 192, 256), BF), ((2, 2, 4, 128, 256), F32), ((2, 2, 128, 128), BF)),
        [],
        2_600_000_000,
        "first_forward",
    )
    pool_low = lax.ppermute(pooled, "space", upward)
    pool_high = lax.ppermute(pooled, "space", downward)

    parity_ref = parity.astype(jnp.int32).reshape(1)
    grads, taps_second, mid, down, up = call(
        second_layer,
        (parity_ref, pooled, pool_low, pool_high, whole_second, cot_a, cot_b),
        (
            ((2, 256, 256), BF),
            ((3, 2, 384, 256), BF),
            ((2, 128, 256), F32),
            ((2, 128, 256), BF),
            ((2, 128, 256), BF),
        ),
        [pltpu.VMEM((2, 3, 256, 256), BF)],
        2_000_000_000,
        "second_layer",
    )
    from_high = lax.ppermute(down, "space", downward)
    from_low = lax.ppermute(up, "space", upward)
    (terms_second,) = call(
        second_weights,
        (grads, taps_second),
        (((256, 3456), BF),),
        [],
        900_000_000,
        "second_weights",
    )
    (terms_first,) = call(
        first_weights,
        (taps, slope, mid, from_low, from_high),
        (((128, 1728), BF),),
        [pltpu.VMEM((3, 128, 576), F32)],
        1_800_000_000,
        "first_weights",
    )

    def reduce(terms, rows):
        count = ns * nf
        got = lax.all_to_all(
            terms.reshape(count, rows, -1), ("filt", "space"), 0, 0, tiled=True
        )
        return jnp.sum(got.astype(F32), axis=0)

    mine_second = reduce(terms_second, 2)
    mine_first = reduce(terms_first, 1)
    mine = jnp.concatenate([mine_first.reshape(-1), mine_second.reshape(-1)])
    both = lax.all_to_all(
        jnp.broadcast_to(mine[None], (ns,) + mine.shape), "space", 0, 0, tiled=True
    )
    grad_first = both[:, :1728].reshape(16, 27, 64).transpose(1, 0, 2)
    grad_second = both[:, 1728:].reshape(32, 27, 128).transpose(1, 0, 2)
    return (grad_first, grad_second)


def solution(mesh):
    return jax.shard_map(
        per_device,
        mesh=mesh,
        in_specs=(
            P(None, "space", None, None, None),
            P(None, "filt", None),
            P(None, "filt", None),
            P("space", None, None, "filt", None),
        ),
        out_specs=(P(None, "filt", None), P(None, "filt", None)),
        check_vma=False,
    )
```

time: 597 us -> 176 us (0.29)
  matrix products: 233 us -> 0 us
  local copies, waits for them, and re-layouts: 148 us -> 16.1 us
  waiting for transfers between devices: 138 us -> 55.3 us
  starting transfers between devices: 21.5 us -> 58.1 us
  other arithmetic: 38.5 us -> 3.3 us
  blocking collectives: 0 us -> 15 us
  Pallas kernels: 0 us -> 13 us
    dot_general x135 -> x0, matrix products: 233 us -> none  [the longest x54 98.5 us: convolve(): jnp.einsum('oc,szycx->szyox', weight[offset], window, preferred_element_t...]
    slice x3 -> x2, local copies, waits for them, and re-layouts: 82 us -> 0.19 us  [the longest x1 0.18 us: per_device(): grad_second = both[:, 1728:].reshape(32, 27, 128).transpose(1, 0, 2)]
    psum x1 -> x0, waiting for transfers between devices: 81 us -> none  [per_device(): grad_first = lax.psum(first_terms, 'space')]
    all_to_all x2 -> x4, waiting for transfers between devices: 7.63 us -> 38.5 us  [the longest x2 32.1 us: reduce(): lax.all_to_all(terms.reshape(count, rows, -1), ('filt', 'space'), 0, 0, t...]
    ppermute x2 -> x8, waiting for transfers between devices: 45.6 us -> 16.1 us  [the longest x1 4.36 us: per_device(): from_high = lax.ppermute(down, 'space', downward)]
    all_to_all x2 -> x4, starting transfers between devices: 16.4 us -> 39.6 us  [the longest x2 31.7 us: reduce(): lax.all_to_all(terms.reshape(count, rows, -1), ('filt', 'space'), 0, 0, t...]
    concatenate x2 -> x1, other arithmetic: 19.6 us -> 0.08 us  [per_device(): mine = jnp.concatenate([mine_first.reshape(-1), mine_second.reshape(-1)])]
    all_to_all x0 -> x1, blocking collectives: none -> 15 us  [per_device(): lax.all_to_all(jnp.broadcast_to(mine[None], (ns,) + mine.shape), 'space',...]
  transfers between devices with their start and end apart: 7 -> 13, of which waited for: 5 -> 9; matrix products, arithmetic and copies ran while one was open for 19% -> 6% of each run, Pallas kernels for 0% -> 3%
where the time goes in v1:
time: 176 us; the launch traced here: 175 us
  starting transfers between devices  58.1 us (33%)
  waiting for transfers between devices  55.3 us (31%)
  local copies, waits for them, and re-layouts  16.1 us (9%)
  blocking collectives  15 us (9%)
  between operations  14.2 us (8%)
  Pallas kernels  13 us (7%)
  other arithmetic  3.3 us (2%)
    all_to_all x2, waiting for transfers between devices, reduce(): lax.all_to_all(terms.reshape(count, rows, -1), ('filt', 'space'), 0, 0, t...  32.1 us
    all_to_all x2, starting transfers between devices, reduce(): lax.all_to_all(terms.reshape(count, rows, -1), ('filt', 'space'), 0, 0, t...  31.7 us
    all_to_all x1, blocking collectives, per_device(): lax.all_to_all(jnp.broadcast_to(mine[None], (ns,) + mine.shape), 'space',...  15 us
    pallas_call x4, Pallas kernels, call(): pl.pallas_call(kernel, out_shape=shapes, in_specs=[SMEM if x.dtype == jnp...  13 us
    unnamed x13, local copies, waits for them, and re-layouts  9.11 us
    all_to_all x1, waiting for transfers between devices, per_device(): lax.all_to_all(cotangent.reshape(nf, 2, 2, 32, 128), 'filt', 0, 0, tiled=...  6.43 us
    all_to_all x1, starting transfers between devices, per_device(): lax.all_to_all(cotangent.reshape(nf, 2, 2, 32, 128), 'filt', 0, 0, tiled=...  4.4 us
    ppermute x1, waiting for transfers between devices, per_device(): from_high = lax.ppermute(down, 'space', downward)  4.36 us
  transfers between devices with their start and end apart: 13, of which 9 were waited for; matrix products, arithmetic and copies ran while one was open for 6% of the time, Pallas kernels for 3%

profile of v1, /device:TPU:0, one launch (start us, length us, event | category | flops | bytes accessed | tf_op | source)
XLA Modules:
  0.0 175.0 jit_solution(7993516824362212030)
XLA Ops:
  7.2 0.7 all-gather.3.cloned.1.call-update
  7.9 4.4 %all-to-all-start.1 = ((bf16[8,2,2,32,128]{4,3,2,1,0:T(8,128)(2,1)}), bf16[8,2,2,32,128]{4,3,2,1,0:T(8,128)(2,1)S(1)}, u32[]{:S(2)}, u32[]{:S(2)}) async-start(bf16[8,2,2,32,128]{4,3,2,1,0:T(8,128)(2,1)} %bitcast.32), calls=%async_computation.1 | async-start | bytes 524288 | tf_op jit(solution)/shard_map/all_to_all | solution.py:196
  12.3 0.9 copy.29
  13.2 0.2 broadcast_in_dim.6
  13.4 6.4 %all-to-all-done.1 = bf16[8,2,2,32,128]{4,3,2,1,0:T(8,128)(2,1)S(1)} async-done(((bf16[8,2,2,32,128]{4,3,2,1,0:T(8,128)(2,1)}), bf16[8,2,2,32,128]{4,3,2,1,0:T(8,128)(2,1)S(1)}, u32[]{:S(2)}, u32[]{:S(2)}) %all-to-all-start.1) | async-done | bytes 262176 | tf_op jit(solution)/shard_map/all_to_all | solution.py:196
  19.8 0.8 broadcast_in_dim.14
  20.7 3.5 %all-to-all-start = ((bf16[8,3,16,576]{3,2,1,0:T(8,128)(2,1)}), bf16[8,3,16,576]{3,2,1,0:T(8,128)(2,1)S(1)}, u32[]{:S(2)}, u32[]{:S(2)}) async-start(bf16[8,3,16,576]{3,2,1,0:T(8,128)(2,1)} %broadcast_in_dim.14), calls=%async_computation | async-start | bytes 983040 | tf_op jit(solution)/shard_map/all_to_all | solution.py:191
  24.2 1.1 dynamic-slice_bitcast_fusion
  25.2 3.5 %collective-permute-start = (bf16[2,4,64,256]{3,2,1,0:T(8,128)(2,1)S(1)}, bf16[2,4,64,256]{3,2,1,0:T(8,128)(2,1)S(1)}, u32[]{:S(2)}, u32[]{:S(2)}) collective-permute-start(bf16[2,4,64,256]{3,2,1,0:T(8,128)(2,1)S(1)} %get-tuple-element.23), channel_id=1, source_target_pairs={{0,8},{8,16},{16,24},{24,32},{32,40},{40,48},{48,56},{56,64},{64,7... | collective-permute-start | bytes 786440 | tf_op jit(solution)/shard_map/ppermute | solution.py:187
  28.8 1.3 collective-permute-start.1
  30.1 1.1 constant_dynamic-slice_fusion.own
  31.2 0.7 collective-permute-start.4
  31.9 2.7 %collective-permute-start.5 = (bf16[8,2,32,128]{3,2,1,0:T(8,128)(2,1)S(1)}, bf16[8,2,32,128]{3,2,1,0:T(8,128)(2,1)S(1)}, u32[]{:S(2)}, u32[]{:S(2)}) collective-permute-start(bf16[8,2,32,128]{3,2,1,0:T(8,128)(2,1)S(1)} %get-tuple-element.24), channel_id=1, source_target_pairs={{0,8},{1,24},{2,40},{3,56},{4,72},{5,88},{6,104},{7,120},{8,0},{9,... | collective-permute-start | bytes 393224 | tf_op jit(solution)/shard_map/ppermute | solution.py:207
  34.6 0.2 collective-permute-done.low
  34.8 4.1 %collective-permute-done.1.high = bf16[2,4,64,256]{3,2,1,0:T(8,128)(2,1)S(1)} collective-permute-done((bf16[2,4,64,256]{3,2,1,0:T(8,128)(2,1)S(1)}, bf16[2,4,64,256]{3,2,1,0:T(8,128)(2,1)S(1)}, u32[]{:S(2)}, u32[]{:S(2)}) %collective-permute-start.1) | collective-permute-done | bytes 262176 | tf_op jit(solution)/shard_map/ppermute | solution.py:188
  39.0 5.0 %first_forward.1 = (bf16[2,4,4,192,256]{4,3,2,1,0:T(8,128)(2,1)}, f32[2,2,4,128,256]{4,3,2,1,0:T(8,128)S(1)}, bf16[2,2,128,128]{3,2,1,0:T(8,128)(2,1)S(1)}) custom-call(bf16[2,2,4,64,256]{4,3,2,1,0:T(8,128)(2,1)S(1)} %constant_dynamic-slice_fusion.own, bf16[2,4,64,256]{3,2,1,0:T(8,128)(2,1)S(1)} %collective-permute-done.low, ...), custom_call_target="tpu_custom_call" | custom-call | flops 2600000000 | bytes 6864896 | tf_op jit(solution)/shard_map/first_forward/pallas_call | solution.py:168
  43.9 1.4 copy-done.2
  45.3 3.5 %collective-permute-start.2 = (bf16[2,2,128,128]{3,2,1,0:T(8,128)(2,1)S(1)}, bf16[2,2,128,128]{3,2,1,0:T(8,128)(2,1)S(1)}, u32[]{:S(2)}, u32[]{:S(2)}) collective-permute-start(bf16[2,2,128,128]{3,2,1,0:T(8,128)(2,1)S(1)} %get-tuple-element.12.own), channel_id=1, source_target_pairs={{0,8},{8,16},{16,24},{24,32},{32,40},{40,48},{48,56},{56,64},{64,7... | collective-permute-start | bytes 393224 | tf_op jit(solution)/shard_map/ppermute | solution.py:219
  48.8 1.3 collective-permute-start.3
  50.1 3.7 %collective-permute-done.2.low = bf16[2,2,128,128]{3,2,1,0:T(8,128)(2,1)S(1)} collective-permute-done((bf16[2,2,128,128]{3,2,1,0:T(8,128)(2,1)S(1)}, bf16[2,2,128,128]{3,2,1,0:T(8,128)(2,1)S(1)}, u32[]{:S(2)}, u32[]{:S(2)}) %collective-permute-start.2) | collective-permute-done | bytes 131104 | tf_op jit(solution)/shard_map/ppermute | solution.py:219
  53.8 2.4 %collective-permute-done.3.high = bf16[2,2,128,128]{3,2,1,0:T(8,128)(2,1)S(1)} collective-permute-done((bf16[2,2,128,128]{3,2,1,0:T(8,128)(2,1)S(1)}, bf16[2,2,128,128]{3,2,1,0:T(8,128)(2,1)S(1)}, u32[]{:S(2)}, u32[]{:S(2)}) %collective-permute-start.3) | collective-permute-done | bytes 131104 | tf_op jit(solution)/shard_map/ppermute | solution.py:220
  56.2 1.5 copy-done
  57.7 3.0 %second_layer.1 = (bf16[2,256,256]{2,1,0:T(8,128)(2,1)S(1)}, bf16[3,2,384,256]{3,2,1,0:T(8,128)(2,1)S(1)}, f32[2,128,256]{2,1,0:T(8,128)S(1)}, bf16[2,128,256]{2,1,0:T(8,128)(2,1)S(1)}, bf16[2,128,256]{2,1,0:T(8,128)(2,1)S(1)}) custom-call(s32[1]{0:T(128)} %bitcast.4.parity, bf16[2,2,128,128]{3,2,1,0:T(8,128)(2,1)S(1)} %get-tuple-element.12.own, ...), custom_call_target="tpu_custom_call" | custom-call | flops 2000000000 | bytes 4390916 | tf_op jit(solution)/shard_map/second_layer/pallas_call | solution.py:168
  60.7 4.3 %collective-permute-start.6 = (bf16[2,128,256]{2,1,0:T(8,128)(2,1)S(1)}, bf16[2,128,256]{2,1,0:T(8,128)(2,1)S(1)}, u32[]{:S(2)}, u32[]{:S(2)}) collective-permute-start(bf16[2,128,256]{2,1,0:T(8,128)(2,1)S(1)} %get-tuple-element.14), channel_id=1, source_target_pairs={{0,8},{8,16},{16,24},{24,32},{32,40},{40,48},{48,56},{56,64},{64,7... | collective-permute-start | bytes 393224 | tf_op jit(solution)/shard_map/ppermute | solution.py:238
  65.0 1.3 collective-permute-start.7
  66.3 1.2 collective-permute-done.6.low
  67.5 4.4 %collective-permute-done.7.high = bf16[2,128,256]{2,1,0:T(8,128)(2,1)S(1)} collective-permute-done((bf16[2,128,256]{2,1,0:T(8,128)(2,1)S(1)}, bf16[2,128,256]{2,1,0:T(8,128)(2,1)S(1)}, u32[]{:S(2)}, u32[]{:S(2)}) %collective-permute-start.7) | collective-permute-done | bytes 131104 | tf_op jit(solution)/shard_map/ppermute | solution.py:237
  71.8 4.0 %first_weights.1 = bf16[128,1728]{1,0:T(8,128)(2,1)S(1)} custom-call(bf16[2,4,4,192,256]{4,3,2,1,0:T(8,128)(2,1)S(1)} %copy-done.1, f32[2,2,4,128,256]{4,3,2,1,0:T(8,128)S(1)} %copy-done.3, f32[2,128,256]{2,1,0:T(8,128)S(1)} %get-tuple-element.13.mid, bf16[2,128,256]{2,1,0:T(8,128)(2,1)S(1)} %collective-permute-done.6.low, ...), custom_call_target="tpu_custom_call" | custom-call | flops 1800000000 | bytes 6209536 | tf_op jit(solution)/shard_map/first_weights/pallas_call | solution.py:168
  75.9 0.5 broadcast.4
  76.4 0.9 reduce.1
  77.3 1.2 reshape.47
  78.6 26.9 %all-to-all-start.2 = ((bf16[128,2,864]{2,1,0:T(2,128)(2,1)}), bf16[128,2,864]{2,1,0:T(2,128)(2,1)}, u32[]{:S(2)}, u32[]{:S(2)}) async-start(bf16[128,2,864]{2,1,0:T(2,128)(2,1)} %reshape.47), calls=%async_computation.2 | async-start | bytes 917504 | tf_op jit(solution)/shard_map/all_to_all | solution.py:258
  105.5 1.0 second_weights.1
  106.5 1.7 reshape.42
  108.1 9.9 %all-to-all-done.2 = bf16[128,2,864]{2,1,0:T(2,128)(2,1)} async-done(((bf16[128,2,864]{2,1,0:T(2,128)(2,1)}), bf16[128,2,864]{2,1,0:T(2,128)(2,1)}, u32[]{:S(2)}, u32[]{:S(2)}) %all-to-all-start.2) | async-done | bytes 442400 | tf_op jit(solution)/shard_map/all_to_all | solution.py:258
  118.0 4.8 %all-to-all-start.3 = ((bf16[128,2,3456]{2,1,0:T(2,128)(2,1)}), bf16[128,2,3456]{2,1,0:T(2,128)(2,1)S(1)}, u32[]{:S(2)}, u32[]{:S(2)}) async-start(bf16[128,2,3456]{2,1,0:T(2,128)(2,1)} %reshape.42), calls=%async_computation.3 | async-start | bytes 3538944 | tf_op jit(solution)/shard_map/all_to_all | solution.py:258
  122.9 3.2 %reshape.48 = bf16[128,1,1728]{2,1,0:T(2,128)(2,1)S(1)} reshape(bf16[128,2,864]{2,1,0:T(2,128)(2,1)} %all-to-all-done.2) | data formatting | bytes 884736
  126.0 0.9 convert_reduce_fusion.1
  126.9 22.2 %all-to-all-done.3 = bf16[128,2,3456]{2,1,0:T(2,128)(2,1)S(1)} async-done(((bf16[128,2,3456]{2,1,0:T(2,128)(2,1)}), bf16[128,2,3456]{2,1,0:T(2,128)(2,1)S(1)}, u32[]{:S(2)}, u32[]{:S(2)}) %all-to-all-start.3) | async-done | bytes 1769504 | tf_op jit(solution)/shard_map/all_to_all | solution.py:258
  149.1 1.4 convert_reduce_fusion
  150.6 0.1 pad_maximum_fusion
  150.6 0.3 broadcast_in_dim.15
  150.9 15.0 %all_to_all.29 = f32[16,1,8640]{2,1,0:T(1,128)S(1)} all-to-all(f32[16,1,8640]{2,1,0:T(1,128)S(1)} %broadcast_in_dim.15), channel_id=1, replica_groups=mesh['space'=16,'filt'=8] {'space'}, dimensions={0} | all-to-all | bytes 1105920 | tf_op jit(solution)/shard_map/all_to_all | solution.py:266
  166.0 0.2 slice.17
  166.1 0.1 reshape.45
  166.2 1.0 copy.21
  167.3 0.1 reshape.44
  167.4 0.8 copy.20
  (15 shorter events, 0.2 us)
Async XLA Ops:
  7.2 49.1 %all-gather.3.cloned.1.call-start = ((), (), s32[]{:S(2)}) async-start(), calls=%async_computation.5 | async-start | bytes 1990656 | tf_op jit(solution)/shard_map/all_gather | solution.py:194
  7.9 11.9 %all-to-all-start.1 = ((bf16[8,2,2,32,128]{4,3,2,1,0:T(8,128)(2,1)}), bf16[8,2,2,32,128]{4,3,2,1,0:T(8,128)(2,1)S(1)}, u32[]{:S(2)}, u32[]{:S(2)}) async-start(bf16[8,2,2,32,128]{4,3,2,1,0:T(8,128)(2,1)} %bitcast.32), calls=%async_computation.1 | async-start | bytes 524288 | tf_op jit(solution)/shard_map/all_to_all | solution.py:196
  20.7 18.3 %all-to-all-start = ((bf16[8,3,16,576]{3,2,1,0:T(8,128)(2,1)}), bf16[8,3,16,576]{3,2,1,0:T(8,128)(2,1)S(1)}, u32[]{:S(2)}, u32[]{:S(2)}) async-start(bf16[8,3,16,576]{3,2,1,0:T(8,128)(2,1)} %broadcast_in_dim.14), calls=%async_computation | async-start | bytes 983040 | tf_op jit(solution)/shard_map/all_to_all | solution.py:191
  25.2 9.6 %collective-permute-start = (bf16[2,4,64,256]{3,2,1,0:T(8,128)(2,1)S(1)}, bf16[2,4,64,256]{3,2,1,0:T(8,128)(2,1)S(1)}, u32[]{:S(2)}, u32[]{:S(2)}) collective-permute-start(bf16[2,4,64,256]{3,2,1,0:T(8,128)(2,1)S(1)} %get-tuple-element.23), channel_id=1, source_target_pairs={{0,8},{8,16},{16,24},{24,32},{32,40},{40,48},{48,56},{56,64},{64,7... | collective-permute-start | bytes 786440 | tf_op jit(solution)/shard_map/ppermute | solution.py:187
  28.8 10.2 %collective-permute-start.1 = (bf16[2,4,64,256]{3,2,1,0:T(8,128)(2,1)S(1)}, bf16[2,4,64,256]{3,2,1,0:T(8,128)(2,1)S(1)}, u32[]{:S(2)}, u32[]{:S(2)}) collective-permute-start(bf16[2,4,64,256]{3,2,1,0:T(8,128)(2,1)S(1)} %get-tuple-element.22), channel_id=1, source_target_pairs={{8,0},{16,8},{24,16},{32,24},{40,32},{48,40},{56,48},{64,56},{72,6... | collective-permute-start | bytes 786440 | tf_op jit(solution)/shard_map/ppermute | solution.py:188
  31.2 18.9 %collective-permute-start.4 = (bf16[8,2,32,128]{3,2,1,0:T(8,128)(2,1)S(1)}, bf16[8,2,32,128]{3,2,1,0:T(8,128)(2,1)S(1)}, u32[]{:S(2)}, u32[]{:S(2)}) collective-permute-start(bf16[8,2,32,128]{3,2,1,0:T(8,128)(2,1)S(1)} %get-tuple-element.25), channel_id=1, source_target_pairs={{0,0},{1,16},{2,32},{3,48},{4,64},{5,80},{6,96},{7,112},{8,8},{9,2... | collective-permute-start | bytes 393224 | tf_op jit(solution)/shard_map/ppermute | solution.py:204
  31.9 18.2 %collective-permute-start.5 = (bf16[8,2,32,128]{3,2,1,0:T(8,128)(2,1)S(1)}, bf16[8,2,32,128]{3,2,1,0:T(8,128)(2,1)S(1)}, u32[]{:S(2)}, u32[]{:S(2)}) collective-permute-start(bf16[8,2,32,128]{3,2,1,0:T(8,128)(2,1)S(1)} %get-tuple-element.24), channel_id=1, source_target_pairs={{0,8},{1,24},{2,40},{3,56},{4,72},{5,88},{6,104},{7,120},{8,0},{9,... | collective-permute-start | bytes 393224 | tf_op jit(solution)/shard_map/ppermute | solution.py:207
  43.9 1.4 copy-start.2
  45.3 8.5 %collective-permute-start.2 = (bf16[2,2,128,128]{3,2,1,0:T(8,128)(2,1)S(1)}, bf16[2,2,128,128]{3,2,1,0:T(8,128)(2,1)S(1)}, u32[]{:S(2)}, u32[]{:S(2)}) collective-permute-start(bf16[2,2,128,128]{3,2,1,0:T(8,128)(2,1)S(1)} %get-tuple-element.12.own), channel_id=1, source_target_pairs={{0,8},{8,16},{16,24},{24,32},{32,40},{40,48},{48,56},{56,64},{64,7... | collective-permute-start | bytes 393224 | tf_op jit(solution)/shard_map/ppermute | solution.py:219
  48.8 7.5 %collective-permute-start.3 = (bf16[2,2,128,128]{3,2,1,0:T(8,128)(2,1)S(1)}, bf16[2,2,128,128]{3,2,1,0:T(8,128)(2,1)S(1)}, u32[]{:S(2)}, u32[]{:S(2)}) collective-permute-start(bf16[2,2,128,128]{3,2,1,0:T(8,128)(2,1)S(1)} %get-tuple-element.12.own), channel_id=1, source_target_pairs={{8,0},{16,8},{24,16},{32,24},{40,32},{48,40},{56,48},{64,56},{72,6... | collective-permute-start | bytes 393224 | tf_op jit(solution)/shard_map/ppermute | solution.py:220
  56.2 1.5 copy-start
  57.7 14.1 %copy-start.1 = (bf16[2,4,4,192,256]{4,3,2,1,0:T(8,128)(2,1)S(1)}, bf16[2,4,4,192,256]{4,3,2,1,0:T(8,128)(2,1)}, u32[]{:S(2)}) copy-start(bf16[2,4,4,192,256]{4,3,2,1,0:T(8,128)(2,1)} %get-tuple-element.10.taps) | copy-start | bytes 9437188
  57.7 14.1 %copy-start.3 = (f32[2,2,4,128,256]{4,3,2,1,0:T(8,128)S(1)}, f32[2,2,4,128,256]{4,3,2,1,0:T(8,128)}, u32[]{:S(2)}) copy-start(f32[2,2,4,128,256]{4,3,2,1,0:T(8,128)} %copy-done.2) | copy-start | bytes 6291460
  60.7 6.8 %collective-permute-start.6 = (bf16[2,128,256]{2,1,0:T(8,128)(2,1)S(1)}, bf16[2,128,256]{2,1,0:T(8,128)(2,1)S(1)}, u32[]{:S(2)}, u32[]{:S(2)}) collective-permute-start(bf16[2,128,256]{2,1,0:T(8,128)(2,1)S(1)} %get-tuple-element.14), channel_id=1, source_target_pairs={{0,8},{8,16},{16,24},{24,32},{32,40},{40,48},{48,56},{56,64},{64,7... | collective-permute-start | bytes 393224 | tf_op jit(solution)/shard_map/ppermute | solution.py:238
  65.0 6.9 %collective-permute-start.7 = (bf16[2,128,256]{2,1,0:T(8,128)(2,1)S(1)}, bf16[2,128,256]{2,1,0:T(8,128)(2,1)S(1)}, u32[]{:S(2)}, u32[]{:S(2)}) collective-permute-start(bf16[2,128,256]{2,1,0:T(8,128)(2,1)S(1)} %get-tuple-element.15), channel_id=1, source_target_pairs={{8,0},{16,8},{24,16},{32,24},{40,32},{48,40},{56,48},{64,56},{72,6... | collective-permute-start | bytes 393224 | tf_op jit(solution)/shard_map/ppermute | solution.py:237
  78.6 39.5 %all-to-all-start.2 = ((bf16[128,2,864]{2,1,0:T(2,128)(2,1)}), bf16[128,2,864]{2,1,0:T(2,128)(2,1)}, u32[]{:S(2)}, u32[]{:S(2)}) async-start(bf16[128,2,864]{2,1,0:T(2,128)(2,1)} %reshape.47), calls=%async_computation.2 | async-start | bytes 917504 | tf_op jit(solution)/shard_map/all_to_all | solution.py:258
  118.0 31.1 %all-to-all-start.3 = ((bf16[128,2,3456]{2,1,0:T(2,128)(2,1)}), bf16[128,2,3456]{2,1,0:T(2,128)(2,1)S(1)}, u32[]{:S(2)}, u32[]{:S(2)}) async-start(bf16[128,2,3456]{2,1,0:T(2,128)(2,1)} %reshape.42), calls=%async_computation.3 | async-start | bytes 3538944 | tf_op jit(solution)/shard_map/all_to_all | solution.py:258
Sparse Core Ops, SparseCore 0:
  9.7 29.0 all-gather.2

commit v2 on v1

v2 whole, which is shorter than its diff:
```python
import functools

import jax
import jax.numpy as jnp
from jax import lax
from jax.experimental import pallas as pl
from jax.experimental.pallas import tpu as pltpu
from jax.sharding import PartitionSpec as P

BF = jnp.bfloat16
F32 = jnp.float32
ROOT = 0.7978845608028654
CUBE = 0.044715


def dot(a, b):
    return lax.dot_general(a, b, (((1,), (0,)), ((), ())), preferred_element_type=F32)


def dot_nt(a, b):
    return lax.dot_general(a, b, (((1,), (1,)), ((), ())), preferred_element_type=F32)


def dot_tn(a, b):
    return lax.dot_general(a, b, (((0,), (0,)), ((), ())), preferred_element_type=F32)


def gelu_and_slope(v):
    square = v * v
    t = jnp.tanh(ROOT * v * (1.0 + CUBE * square))
    half = 0.5 * (1.0 + t)
    slope = half + 0.5 * v * (1.0 - t * t) * (ROOT * (1.0 + 3.0 * CUBE * square))
    return v * half, slope


def split_shift(e):
    row = lax.broadcasted_iota(jnp.int32, (256, 256), 0)
    col = lax.broadcasted_iota(jnp.int32, (256, 256), 1)
    source = 2 * (col & 127) + (col >> 7) + (e - 1)
    return jnp.where(row == source, 1.0, 0.0).astype(BF)


def pair_shift(e):
    row = lax.broadcasted_iota(jnp.int32, (256, 256), 0)
    col = lax.broadcasted_iota(jnp.int32, (256, 256), 1)
    same = (row >> 7) == (col >> 7)
    return jnp.where(same & ((row & 127) == (col & 127) + (e - 1)), 1.0, 0.0).astype(BF)


def pack_inputs(weight, cot, out):
    for a in range(3):
        for j in range(0, 8, 2):
            pair = jnp.concatenate([weight[9 * a + j], weight[9 * a + j + 1]], axis=1)
            for f in range(8):
                out[f, a * 64 + j * 8 : a * 64 + j * 8 + 16] = pair
    pair = jnp.concatenate([weight[8], weight[17]], axis=1)
    last = jnp.concatenate([weight[26], jnp.zeros_like(weight[26])], axis=1)
    for f in range(8):
        out[f, 192:208] = pair
        out[f, 208:224] = last
        out[f, 224:352] = cot[0, 2 * f : 2 * f + 2].reshape(128, 128)


def first_rows(packed, a):
    tiles = [packed[:, a * 64 + j * 16 : a * 64 + j * 16 + 16].reshape(128, 128) for j in range(4)]
    row = 208 if a == 2 else 192
    tiles.append(packed[:, row : row + 16].reshape(128, 128)[:, 64 * (a % 2) : 64 * (a % 2) + 64])
    return jnp.concatenate(tiles, axis=1)


def low_and_high(place, one, two):
    even = place[0] == 0
    two = jnp.where(place[2] == 1, jnp.zeros_like(two), two)
    return jnp.where(even, two, one), jnp.where(even, one, two)


def first_forward(place, own, one, two, packed, taps, slope, pooled, weight):
    shifts = [split_shift(e) for e in range(3)]
    for a in range(3):
        weight[a] = first_rows(packed, a)

    @pl.loop(0, 2)
    def _(s):
        low, high = low_and_high(place, one[s], two[s])
        for depth, cells in enumerate((low, own[s, 0], own[s, 1], high)):
            cells = cells.reshape(256, 256)
            for e in range(3):
                taps[s, depth, :, e * 64 : (e + 1) * 64, :] = (
                    dot(cells, shifts[e]).astype(BF).reshape(4, 64, 256)
                )
        for pair in range(2):
            total = None
            for z in range(2):
                for y in (2 * pair, 2 * pair + 1):
                    first, last = max(y - 1, 0), min(y + 2, 4)
                    left = (first - y + 1) * 192
                    size = (last - first) * 192
                    pre = None
                    for a in range(3):
                        w = weight[a, :, left : left + size]
                        part = dot(w, taps[s, z + a, first:last].reshape(size, 256))
                        pre = part if pre is None else pre + part
                    value, rate = gelu_and_slope(pre)
                    slope[s, z, y] = rate
                    total = value if total is None else total + value
            pooled[s, pair] = ((total[:, :128] + total[:, 128:]) * 0.125).astype(BF)


def other_blocks(place):
    filt = place[1]
    return [filt ^ (2 * d + c) for c in range(2) for d in range(4)]


def split_cot(place, packed, same, other):
    for f in range(8):
        same[f] = packed[f, pl.ds(pl.multiple_of(224 + 64 * place[0], 32), 64)]
        other[f] = packed[f, pl.ds(pl.multiple_of(288 - 64 * place[0], 32), 64)]


def join_cot(place, same, other, out):
    even = place[0] == 0
    blocks = other_blocks(place)
    for y in range(2):
        here = pl.ds(32 * y, 32)
        a = jnp.concatenate([same[f, here] for f in blocks], axis=0)
        b = jnp.concatenate([other[f, here] for f in blocks], axis=0)
        out[y, :, 0:128] = jnp.where(even, a, b)
        out[y, :, 128:256] = jnp.where(even, b, a)


def second_layer(place, own, one, two, weight, across, cot, grads, taps, mid, first, second, spread):
    even = place[0] == 0

    def rows(k):
        return jnp.concatenate([weight[:, k].reshape(128, 128), across[:, k].reshape(128, 128)], axis=0)

    left, right = pair_shift(0), pair_shift(2)
    for y in range(2):
        low, high = low_and_high(
            place,
            jnp.concatenate([one[0, y], one[1, y]], axis=1),
            jnp.concatenate([two[0, y], two[1, y]], axis=1),
        )
        mine = jnp.concatenate([own[0, y], own[1, y]], axis=1)
        for a, cells in enumerate((low, mine, high)):
            taps[a, y, 0:128] = dot(cells, left).astype(BF)
            taps[a, y, 128:256] = cells
            taps[a, y, 256:384] = dot(cells, right).astype(BF)
    for y in range(2):
        pre = None
        for a in range(3):
            base = 9 * a + 3 * (1 - y)
            w = jnp.concatenate([rows(base + j) for j in range(6)], axis=1)
            part = dot(w, taps[a].reshape(768, 256))
            pre = part if pre is None else pre + part
        _, rate = gelu_and_slope(pre)
        grad = (cot[y].astype(F32) * rate).astype(BF)
        grads[y] = grad
        spread[y, 0] = dot(grad, right).astype(BF)
        spread[y, 1] = grad
        spread[y, 2] = dot(grad, left).astype(BF)
    for y in range(2):
        parts = []
        for a in range(3):
            total = None
            for source in range(2):
                base = 9 * a + 3 * (y - source + 1)
                w = jnp.concatenate([rows(base + e) for e in range(3)], axis=0)
                part = dot_tn(w, spread[source].reshape(768, 256))
                total = part if total is None else total + part
            parts.append(total)
        down, mid[y], up = parts
        first[y] = jnp.where(even, up, down).astype(BF)
        second[y] = jnp.where(even, down, up).astype(BF)


def second_weights(grads, taps, mine, across):
    for a in range(3):
        for b in range(3):
            total = None
            for y in range(2):
                row = y + b - 1
                if 0 <= row < 2:
                    part = dot_nt(grads[y], taps[a, row])
                    total = part if total is None else total + part
            total = total.astype(BF)
            for e in range(3):
                k = 9 * a + 3 * b + e
                lanes = slice(e * 128, (e + 1) * 128)
                mine[:, k] = total[:128, lanes].reshape(4, 32, 128)
                across[:, k] = total[128:, lanes].reshape(4, 32, 128)


def add_cores(mine, across, own, *others):
    own[...] = mine[0].astype(F32) + across[0].astype(F32)
    for d, out in enumerate(others):
        out[...] = (mine[d + 1].astype(F32) + across[d + 1].astype(F32)).astype(BF)


def first_weights(place, taps, slope, mid, one, two, out, total):
    inside = place[2] == 0
    total[...] = jnp.zeros_like(total)

    @pl.loop(0, 2)
    def _(s):
        for pair in range(2):
            lanes = pl.ds(pl.multiple_of(s * 128, 128), 128)
            back = (
                mid[pair, :, lanes]
                + one[pair, :, lanes].astype(F32)
                + jnp.where(inside, two[pair, :, lanes].astype(F32), 0.0)
            ) * 0.125
            back = jnp.concatenate([back, back], axis=1)
            for z in range(2):
                for y in (2 * pair, 2 * pair + 1):
                    inner = (slope[s, z, y] * back).astype(BF)
                    first, last = max(y - 1, 0), min(y + 2, 4)
                    left = (first - y + 1) * 192
                    size = (last - first) * 192
                    for a in range(3):
                        total[a, :, left : left + size] += dot_nt(
                            inner, taps[s, z + a, first:last].reshape(size, 256)
                        )

    for a in range(3):
        out[:, a] = total[a].astype(BF).reshape(8, 16, 576)


def add_across(own, one, two, three, out):
    out[...] = (
        own[...] + one[...].astype(F32) + two[...].astype(F32) + three[...].astype(F32)
    ).astype(out.dtype)


def pack(first, second, out):
    out[0:864] = second[...].reshape(864, 128)
    for a in range(3):
        total = first[0, a].astype(F32)
        for f in range(1, 8):
            total = total + first[f, a].astype(F32)
        total = total.astype(out.dtype)
        for j in range(4):
            row = 864 + a * 64 + j * 16
            out[row : row + 16] = total[:, j * 128 : (j + 1) * 128]
        row = 1056 + a * 16
        last = total[:, 512:576]
        out[row : row + 16] = jnp.concatenate([last, jnp.zeros_like(last)], axis=1)
    out[1104:1152] = jnp.zeros((48, 128), out.dtype)


def add_up(parts, out):
    total = parts[0].astype(F32)
    for s in range(1, 16):
        total = total + parts[s].astype(F32)
    total = total.astype(out.dtype)
    for s in range(16):
        out[s] = total


def unpack(rows, first, second):
    for k in range(27):
        second[k] = rows[k * 32 : (k + 1) * 32].astype(F32)
    for a in range(3):
        for j in range(9):
            row = 864 + a * 64 + (j // 2) * 16 if j < 8 else 1056 + a * 16
            half = (j % 2) * 64
            first[9 * a + j] = rows[row : row + 16].astype(F32)[:, half : half + 64]


VMEM = pl.BlockSpec(memory_space=pltpu.VMEM)
HBM = pl.BlockSpec(memory_space=pltpu.HBM)
SMEM = pl.BlockSpec(memory_space=pltpu.SMEM)


def call(kernel, ins, outs, scratch, flops, name, far_in=(), far=(), limit=24):
    shapes = [jax.ShapeDtypeStruct(s, d) for s, d in outs]
    size = sum(x.size * x.dtype.itemsize for x in list(ins) + shapes)
    return pl.pallas_call(
        kernel,
        out_shape=shapes,
        in_specs=[
            SMEM if x.dtype == jnp.int32 else HBM if i in far_in else VMEM for i, x in enumerate(ins)
        ],
        out_specs=[HBM if i in far else VMEM for i in range(len(outs))],
        scratch_shapes=scratch,
        compiler_params=pltpu.CompilerParams(vmem_limit_bytes=limit * 1024 * 1024),
        cost_estimate=pl.CostEstimate(flops=flops, bytes_accessed=size, transcendentals=0),
        name=name,
    )(*ins)


SEND = jnp.bfloat16
LONG = 20_000_000_000


def after(value, *others):
    return lax.optimization_barrier((value,) + others)[0]


def per_device(volume, weight_first, weight_second, cotangent):
    space, filt = lax.axis_index("space"), lax.axis_index("filt")
    ns, nf = lax.axis_size("space"), lax.axis_size("filt")
    parity = space % 2
    edge = ((space == 0) | (space == ns - 1)).astype(jnp.int32)
    place = jnp.stack([parity, filt, edge])
    ones = [(i, i ^ 1) for i in range(ns)]
    twos = [(i, (((i + 1) ^ 1) - 1) % ns) for i in range(ns)]

    by_x = [[(i, i ^ (2 * d)) for i in range(nf)] for d in range(4)]
    by_core = [(i, i ^ 1) for i in range(nf)]

    def face(depth):
        zero = jnp.int32(0)
        cells = lax.dynamic_slice(volume, (2 * filt, depth, zero, zero, zero), (2, 1, 4, 64, 256))
        return cells[:, 0]

    one = lax.ppermute(face(1 - parity), "space", ones)
    two = lax.ppermute(face(parity), "space", twos)
    own = lax.dynamic_slice_in_dim(volume, 2 * filt, 2, axis=0)
    (pieces,) = call(
        pack_inputs, (weight_first, cotangent), (((8, 352, 128), BF),), [], 0, "pack_inputs", limit=60
    )
    packed = lax.all_to_all(pieces, "filt", 0, 0, tiled=True)
    weights = [weight_second] + [
        lax.ppermute(after(weight_second, pieces), "filt", by_x[d]) for d in range(1, 4)
    ]

    def turned(shift):
        return [
            (s * nf + f, (2 * f + (s + shift) % 2) * nf + s // 2)
            for s in range(ns)
            for f in range(nf)
        ]

    half = ((8, 64, 128), BF)
    cot_a, cot_b = call(split_cot, (place, packed), (half, half), [], 0, "split_cot")
    cot_a = lax.ppermute(cot_a, ("space", "filt"), turned(0))
    cot_b = lax.ppermute(cot_b, ("space", "filt"), turned(1))

    taps, slope, pooled = call(
        first_forward,
        (place, own, one, two, packed),
        (((2, 4, 4, 192, 256), BF), ((2, 2, 4, 128, 256), F32), ((2, 2, 128, 128), BF)),
        [
            pltpu.VMEM((3, 128, 576), BF),
        ],
        LONG,
        "first_forward",
    )
    pool_one = lax.ppermute(pooled, "space", ones)
    pool_two = lax.ppermute(pooled, "space", twos)
    same_core = jnp.stack([after(w, pooled) for w in weights])
    other_core = lax.ppermute(same_core, "filt", by_core)
    (cot,) = call(
        join_cot, (place, cot_a, cot_b), (((2, 256, 256), BF),), [], LONG, "join_cot"
    )
    grads, taps_second, mid, out_one, out_two = call(
        second_layer,
        (place, pooled, pool_one, pool_two, same_core, other_core, cot),
        (
            ((2, 256, 256), BF),
            ((3, 2, 384, 256), BF),
            ((2, 128, 256), F32),
            ((2, 128, 256), BF),
            ((2, 128, 256), BF),
        ),
        [pltpu.VMEM((2, 3, 256, 256), BF)],
        2_000_000_000,
        "second_layer",
    )
    back_one = lax.ppermute(out_one, "space", ones)
    back_two = lax.ppermute(out_two, "space", twos)
    mine, across = call(
        second_weights,
        (grads, taps_second),
        (((4, 27, 32, 128), BF), ((4, 27, 32, 128), BF)),
        [],
        900_000_000,
        "second_weights",
    )
    across = lax.ppermute(across, "filt", by_core)
    whole = (27, 32, 128)
    own_second, *others = call(
        add_cores, (mine, across), ((whole, F32),) + ((whole, BF),) * 3, [], 0, "add_cores"
    )
    got_second = [lax.ppermute(others[d - 1], "filt", by_x[d]) for d in range(1, 4)]
    (terms_first,) = call(
        first_weights,
        (place, taps, slope, mid, after(back_one, mine), back_two),
        (((8, 3, 16, 576), BF),),
        [pltpu.VMEM((3, 128, 576), F32)],
        LONG,
        "first_weights",
    )
    got_first = lax.all_to_all(terms_first, "filt", 0, 0, tiled=True)

    (mine_second,) = call(
        add_across, (own_second, *got_second), ((whole, SEND),), [], LONG, "add_across"
    )
    (rows,) = call(pack, (got_first, mine_second), (((1152, 128), SEND),), [], 0, "pack")
    parts = lax.all_to_all(rows.reshape(ns, 72, 128), "space", 0, 0, tiled=True)
    (mine,) = call(add_up, (parts,), (((16, 72, 128), SEND),), [], 0, "add_up")
    rows = lax.all_to_all(mine, "space", 0, 0, tiled=True).reshape(1152, 128)
    return call(
        unpack,
        (rows,),
        (((27, 16, 64), F32), ((27, 32, 128), F32)),
        [],
        0,
        "unpack",
    )


def solution(mesh):
    return jax.shard_map(
        per_device,
        mesh=mesh,
        in_specs=(
            P(None, "space", None, None, None),
            P(None, "filt", None),
            P(None, "filt", None),
            P("space", None, None, "filt", None),
        ),
        out_specs=(P(None, "filt", None), P(None, "filt", None)),
        check_vma=False,
    )
```

time: 176 us -> 114 us (0.65)
  waiting for transfers between devices: 55.3 us -> 15.9 us
  local copies, waits for them, and re-layouts: 16.1 us -> 2.15 us
  between operations: 14.2 us -> 0.78 us
  blocking collectives: 15 us -> 26 us
  starting transfers between devices: 58.1 us -> 49.7 us
  Pallas kernels: 13 us -> 18.5 us
  other arithmetic: 3.3 us -> 0.19 us
    all_to_all x4 -> x2, waiting for transfers between devices: 38.5 us -> 7.61 us  [the longest x1 7.6 us: per_device(): got_first = lax.all_to_all(terms_first, 'filt', 0, 0, tiled=True)]
    all_to_all x4 -> x2, starting transfers between devices: 39.6 us -> 8.83 us  [the longest x1 4.45 us: per_device(): got_first = lax.all_to_all(terms_first, 'filt', 0, 0, tiled=True)]
    ppermute x8 -> x16, starting transfers between devices: 18.5 us -> 40.8 us  [the longest x1 10.1 us: per_device(): back_two = lax.ppermute(out_two, 'space', twos)]
    all_to_all x1 -> x2, blocking collectives: 15 us -> 26 us  [the longest x1 14.3 us: per_device(): parts = lax.all_to_all(rows.reshape(ns, 72, 128), 'space', 0, 0, tiled=True)]
    unnamed x13 -> x2, local copies, waits for them, and re-layouts: 9.11 us -> 0.01 us
    ppermute x8 -> x16, waiting for transfers between devices: 16.1 us -> 8.27 us  [the longest x1 2.81 us: per_device(): cot_b = lax.ppermute(cot_b, ('space', 'filt'), turned(1))]
    pallas_call x4 -> x12, Pallas kernels: 13 us -> 18.5 us  [call(): pl.pallas_call(kernel, out_shape=shapes, in_specs=[SMEM if x.dtype == jnp...]
    reshape x6 -> x0, local copies, waits for them, and re-layouts: 3.35 us -> none  [the longest x2 2.2 us: reduce(): terms.reshape(count, rows, -1)]
  transfers between devices with their start and end apart: 13 -> 18, of which waited for: 9 -> 5; matrix products, arithmetic and copies ran while one was open for 6% -> 2% of each run, Pallas kernels for 3% -> 10%
where the time goes in v2:
time: 114 us; the launch traced here: 113 us
  starting transfers between devices  49.7 us (44%)
  blocking collectives  26 us (23%)
  Pallas kernels  18.5 us (16%)
  waiting for transfers between devices  15.9 us (14%)
  local copies, waits for them, and re-layouts  2.15 us (2%)
    pallas_call x12, Pallas kernels, call(): pl.pallas_call(kernel, out_shape=shapes, in_specs=[SMEM if x.dtype == jnp...  18.5 us
    all_to_all x1, blocking collectives, per_device(): parts = lax.all_to_all(rows.reshape(ns, 72, 128), 'space', 0, 0, tiled=True)  14.3 us
    all_to_all x1, blocking collectives, per_device(): rows = lax.all_to_all(mine, 'space', 0, 0, tiled=True).reshape(1152, 128)  11.7 us
    ppermute x1, starting transfers between devices, per_device(): back_two = lax.ppermute(out_two, 'space', twos)  10.1 us
    all_to_all x1, waiting for transfers between devices, per_device(): got_first = lax.all_to_all(terms_first, 'filt', 0, 0, tiled=True)  7.6 us
    ppermute x1, starting transfers between devices, per_device(): two = lax.ppermute(face(parity), 'space', twos)  6.57 us
    ppermute x3, starting transfers between devices, per_device(): lax.ppermute(others[d - 1], 'filt', by_x[d])  4.77 us
    all_to_all x1, starting transfers between devices, per_device(): got_first = lax.all_to_all(terms_first, 'filt', 0, 0, tiled=True)  4.45 us
  transfers between devices with their start and end apart: 18, of which 5 were waited for; matrix products, arithmetic and copies ran while one was open for 2% of the time, Pallas kernels for 10%

profile of v2, /device:TPU:0, one launch (start us, length us, event | category | flops | bytes accessed | tf_op | source)
XLA Modules:
  0.0 113.2 jit_solution(8357987656380649186)
XLA Ops:
  0.6 2.0 %pack_inputs.1 = bf16[8,352,128]{2,1,0:T(8,128)(2,1)} custom-call(bf16[27,16,64]{2,1,0:T(8,128)(2,1)} %weight.1, bf16[1,16,2,32,128]{4,3,2,1,0:T(8,128)(2,1)} %cot.1), custom_call_target="tpu_custom_call" | custom-call | bytes 1038336 | tf_op jit(solution)/shard_map/pack_inputs/pallas_call | solution.py:278
  2.6 4.4 %all-to-all-start = ((bf16[8,352,128]{2,1,0:T(8,128)(2,1)}), bf16[8,352,128]{2,1,0:T(8,128)(2,1)S(1)}, u32[]{:S(2)}, u32[]{:S(2)}) async-start(bf16[8,352,128]{2,1,0:T(8,128)(2,1)} %pack_inputs.1), calls=%async_computation | async-start | bytes 1441792 | tf_op jit(solution)/shard_map/all_to_all | solution.py:323
  7.0 1.1 dynamic-slice_bitcast_fusion
  8.1 6.6 %collective-permute-start.1 = (bf16[2,4,64,256]{3,2,1,0:T(8,128)(2,1)S(1)}, bf16[2,4,64,256]{3,2,1,0:T(8,128)(2,1)S(1)}, u32[]{:S(2)}, u32[]{:S(2)}) collective-permute-start(bf16[2,4,64,256]{3,2,1,0:T(8,128)(2,1)S(1)} %get-tuple-element.46), channel_id=1, source_target_pairs={{0,120},{8,16},{16,8},{24,32},{32,24},{40,48},{48,40},{56,64},{64,... | collective-permute-start | bytes 786440 | tf_op jit(solution)/shard_map/ppermute | solution.py:318
  14.7 0.0 collective-permute-start
  14.7 3.2 %collective-permute-start.6 = (bf16[27,32,128]{2,1,0:T(8,128)(2,1)}, bf16[27,32,128]{2,1,0:T(8,128)(2,1)S(1)}, u32[]{:S(2)}, u32[]{:S(2)}) collective-permute-start(bf16[27,32,128]{2,1,0:T(8,128)(2,1)} %param.6), channel_id=1, source_target_pairs={{0,6},{1,7},{2,4},{3,5},{4,2},{5,3},{6,0},{7,1},{8,14},{9,15},{10,... | collective-permute-start | bytes 663560 | tf_op jit(solution)/shard_map/ppermute | solution.py:325
  17.9 0.9 collective-permute-start.5
  18.7 0.0 collective-permute-start.4
  18.8 0.1 pad_add_fusion.place
  18.8 1.1 constant_dynamic-slice_fusion.own
  19.9 0.0 copy-start
  19.9 1.7 %collective-permute-done.1.two = bf16[2,4,64,256]{3,2,1,0:T(8,128)(2,1)S(1)} collective-permute-done((bf16[2,4,64,256]{3,2,1,0:T(8,128)(2,1)S(1)}, bf16[2,4,64,256]{3,2,1,0:T(8,128)(2,1)S(1)}, u32[]{:S(2)}, u32[]{:S(2)}) %collective-permute-start.1) | collective-permute-done | bytes 262176 | tf_op jit(solution)/shard_map/ppermute | solution.py:318
  21.6 1.5 %collective-permute-done.one = bf16[2,4,64,256]{3,2,1,0:T(8,128)(2,1)S(1)} collective-permute-done((bf16[2,4,64,256]{3,2,1,0:T(8,128)(2,1)S(1)}, bf16[2,4,64,256]{3,2,1,0:T(8,128)(2,1)S(1)}, u32[]{:S(2)}, u32[]{:S(2)}) %collective-permute-start) | collective-permute-done | bytes 262176 | tf_op jit(solution)/shard_map/ppermute | solution.py:317
  23.1 0.0 all-to-all-done.packed
  23.1 4.2 %first_forward.1 = (bf16[2,4,4,192,256]{4,3,2,1,0:T(8,128)(2,1)S(1)}, f32[2,2,4,128,256]{4,3,2,1,0:T(8,128)S(1)}, bf16[2,2,128,128]{3,2,1,0:T(8,128)(2,1)S(1)}) custom-call(s32[3]{0:T(128)S(1)} %pad_add_fusion.place, bf16[2,2,4,64,256]{4,3,2,1,0:T(8,128)(2,1)S(1)} %constant_dynamic-slice_fusion.own, bf16[2,4,64,256]{3,2,1,0:T(8,128)(2,1)S(1)} %collective-permute-done.one, ...), custom_call_target="tpu_custom_call" | custom-call | flops 20000000000 | bytes 7143436 | tf_op jit(solution)/shard_map/first_forward/pallas_call | solution.py:278
  27.3 3.7 %collective-permute-start.3 = (bf16[2,2,128,128]{3,2,1,0:T(8,128)(2,1)S(1)}, bf16[2,2,128,128]{3,2,1,0:T(8,128)(2,1)S(1)}, u32[]{:S(2)}, u32[]{:S(2)}) collective-permute-start(bf16[2,2,128,128]{3,2,1,0:T(8,128)(2,1)S(1)} %get-tuple-element.26.own), channel_id=1, source_target_pairs={{0,120},{8,16},{16,8},{24,32},{32,24},{40,48},{48,40},{56,64},{64,... | collective-permute-start | bytes 393224 | tf_op jit(solution)/shard_map/ppermute | solution.py:351
  31.0 0.0 collective-permute-start.2
  31.0 0.6 split_cot.1
  31.6 0.7 collective-permute-start.8
  32.3 0.0 collective-permute-done.5
  32.3 2.1 %collective-permute-start.9 = (bf16[8,64,128]{2,1,0:T(8,128)(2,1)S(1)}, bf16[8,64,128]{2,1,0:T(8,128)(2,1)S(1)}, u32[]{:S(2)}, u32[]{:S(2)}) collective-permute-start(bf16[8,64,128]{2,1,0:T(8,128)(2,1)S(1)} %get-tuple-element.33), channel_id=1, source_target_pairs={{0,8},{1,24},{2,40},{3,56},{4,72},{5,88},{6,104},{7,120},{8,0},{9,... | collective-permute-start | bytes 393224 | tf_op jit(solution)/shard_map/ppermute | solution.py:338
  34.4 0.0 collective-permute-done.4
  34.4 0.1 pad_maximum_fusion.weight
  34.5 2.9 %collective-permute-start.7 = (bf16[4,27,32,128]{3,2,1,0:T(8,128)(2,1)S(1)}, bf16[4,27,32,128]{3,2,1,0:T(8,128)(2,1)S(1)}, u32[]{:S(2)}, u32[]{:S(2)}) collective-permute-start(bf16[4,27,32,128]{3,2,1,0:T(8,128)(2,1)S(1)} %pad_maximum_fusion.weight), channel_id=1, source_target_pairs={{0,1},{1,0},{2,3},{3,2},{4,5},{5,4},{6,7},{7,6},{8,9},{9,8},{10,11... | collective-permute-start | bytes 2654216 | tf_op jit(solution)/shard_map/ppermute | solution.py:353
  37.4 0.0 collective-permute-done.8.same
  37.4 2.8 %collective-permute-done.9.other = bf16[8,64,128]{2,1,0:T(8,128)(2,1)S(1)} collective-permute-done((bf16[8,64,128]{2,1,0:T(8,128)(2,1)S(1)}, bf16[8,64,128]{2,1,0:T(8,128)(2,1)S(1)}, u32[]{:S(2)}, u32[]{:S(2)}) %collective-permute-start.9) | collective-permute-done | bytes 131104 | tf_op jit(solution)/shard_map/ppermute | solution.py:338
  40.2 0.6 join_cot.1.cot
  40.8 0.0 collective-permute-done.2.one
  40.8 0.0 collective-permute-done.7.across
  40.8 3.5 %second_layer.1 = (bf16[2,256,256]{2,1,0:T(8,128)(2,1)S(1)}, bf16[3,2,384,256]{3,2,1,0:T(8,128)(2,1)S(1)}, f32[2,128,256]{2,1,0:T(8,128)S(1)}, bf16[2,128,256]{2,1,0:T(8,128)(2,1)S(1)}, bf16[2,128,256]{2,1,0:T(8,128)(2,1)S(1)}) custom-call(s32[3]{0:T(128)S(1)} %pad_add_fusion.place, bf16[2,2,128,128]{3,2,1,0:T(8,128)(2,1)S(1)} %get-tuple-element.26.own, ...), custom_call_target="tpu_custom_call" | custom-call | flops 2000000000 | bytes 4390924 | tf_op jit(solution)/shard_map/second_layer/pallas_call | solution.py:278
  44.3 1.0 second_weights.1
  45.3 4.1 %collective-permute-start.12 = (bf16[4,27,32,128]{3,2,1,0:T(8,128)(2,1)S(1)}, bf16[4,27,32,128]{3,2,1,0:T(8,128)(2,1)S(1)}, u32[]{:S(2)}, u32[]{:S(2)}) collective-permute-start(bf16[4,27,32,128]{3,2,1,0:T(8,128)(2,1)S(1)} %get-tuple-element.41), channel_id=1, source_target_pairs={{0,1},{1,0},{2,3},{3,2},{4,5},{5,4},{6,7},{7,6},{8,9},{9,8},{10,11... | collective-permute-start | bytes 2654216 | tf_op jit(solution)/shard_map/ppermute | solution.py:381
  49.4 1.9 %collective-permute-start.10 = (bf16[2,128,256]{2,1,0:T(8,128)(2,1)S(1)}, bf16[2,128,256]{2,1,0:T(8,128)(2,1)S(1)}, u32[]{:S(2)}, u32[]{:S(2)}) collective-permute-start(bf16[2,128,256]{2,1,0:T(8,128)(2,1)S(1)} %get-tuple-element.35), channel_id=1, source_target_pairs={{0,8},{8,0},{16,24},{24,16},{32,40},{40,32},{48,56},{56,48},{64,72... | collective-permute-start | bytes 393224 | tf_op jit(solution)/shard_map/ppermute | solution.py:371
  51.3 10.1 %collective-permute-start.11 = (bf16[2,128,256]{2,1,0:T(8,128)(2,1)S(1)}, bf16[2,128,256]{2,1,0:T(8,128)(2,1)S(1)}, u32[]{:S(2)}, u32[]{:S(2)}) collective-permute-start(bf16[2,128,256]{2,1,0:T(8,128)(2,1)S(1)} %get-tuple-element.40), channel_id=1, source_target_pairs={{0,120},{8,16},{16,8},{24,32},{32,24},{40,48},{48,40},{56,64},{64,... | collective-permute-start | bytes 393224 | tf_op jit(solution)/shard_map/ppermute | solution.py:372
  61.4 0.2 add_cores.1
  61.6 0.1 collective-permute-start.13
  61.7 4.6 %collective-permute-start.14 = (bf16[27,32,128]{2,1,0:T(8,128)(2,1)S(1)}, bf16[27,32,128]{2,1,0:T(8,128)(2,1)S(1)}, u32[]{:S(2)}, u32[]{:S(2)}) collective-permute-start(bf16[27,32,128]{2,1,0:T(8,128)(2,1)S(1)} %get-tuple-element.44), channel_id=1, source_target_pairs={{0,4},{1,5},{2,6},{3,7},{4,0},{5,1},{6,2},{7,3},{8,12},{9,13},{10,... | collective-permute-start | bytes 663560 | tf_op jit(solution)/shard_map/ppermute | solution.py:386
  66.3 0.1 collective-permute-start.15
  66.4 5.3 %first_weights.1 = bf16[8,3,16,576]{3,2,1,0:T(8,128)(2,1)} custom-call(s32[3]{0:T(128)S(1)} %pad_add_fusion.place, bf16[2,4,4,192,256]{4,3,2,1,0:T(8,128)(2,1)S(1)} %get-tuple-element.24.taps, f32[2,2,4,128,256]{4,3,2,1,0:T(8,128)S(1)} %get-tuple-element.25.slope, f32[2,128,256]{2,1,0:T(8,128)S(1)} %get-tuple-element.34.mid, ...), custom_call_target="tpu_custom_call" | custom-call | flops 20000000000 | bytes 6209548 | tf_op jit(solution)/shard_map/first_weights/pallas_call | solution.py:278
  71.7 4.4 %all-to-all-start.1 = ((bf16[8,3,16,576]{3,2,1,0:T(8,128)(2,1)}), bf16[8,3,16,576]{3,2,1,0:T(8,128)(2,1)S(1)}, u32[]{:S(2)}, u32[]{:S(2)}) async-start(bf16[8,3,16,576]{3,2,1,0:T(8,128)(2,1)} %first_weights.1), calls=%async_computation.1 | async-start | bytes 983040 | tf_op jit(solution)/shard_map/all_to_all | solution.py:395
  76.2 2.3 %collective-permute-done.15.three = bf16[27,32,128]{2,1,0:T(8,128)(2,1)S(1)} collective-permute-done((bf16[27,32,128]{2,1,0:T(8,128)(2,1)S(1)}, bf16[27,32,128]{2,1,0:T(8,128)(2,1)S(1)}, u32[]{:S(2)}, u32[]{:S(2)}) %collective-permute-start.15) | collective-permute-done | bytes 221216 | tf_op jit(solution)/shard_map/ppermute | solution.py:386
  78.4 0.1 add_across.1.second
  78.5 7.6 %all-to-all-done.1.first = bf16[8,3,16,576]{3,2,1,0:T(8,128)(2,1)S(1)} async-done(((bf16[8,3,16,576]{3,2,1,0:T(8,128)(2,1)}), bf16[8,3,16,576]{3,2,1,0:T(8,128)(2,1)S(1)}, u32[]{:S(2)}, u32[]{:S(2)}) %all-to-all-start.1) | async-done | bytes 442400 | tf_op jit(solution)/shard_map/all_to_all | solution.py:395
  86.1 0.1 pack.1
  86.2 14.3 %all_to_all.20.parts = bf16[16,72,128]{2,1,0:T(8,128)(2,1)S(1)} all-to-all(bf16[16,72,128]{2,1,0:T(8,128)(2,1)S(1)} %bitcast.14), channel_id=1, replica_groups=mesh['space'=16,'filt'=8] {'space'}, dimensions={0} | all-to-all | bytes 589824 | tf_op jit(solution)/shard_map/all_to_all | solution.py:401
  100.5 0.1 add_up.1
  100.6 11.7 %all_to_all.21 = bf16[16,72,128]{2,1,0:T(8,128)(2,1)S(1)} all-to-all(bf16[16,72,128]{2,1,0:T(8,128)(2,1)S(1)} %add_up.1), channel_id=1, replica_groups=mesh['space'=16,'filt'=8] {'space'}, dimensions={0} | all-to-all | bytes 589824 | tf_op jit(solution)/shard_map/all_to_all | solution.py:403
  112.3 0.9 unpack.1
  (8 shorter events, 0.0 us)
Async XLA Ops:
  2.6 20.5 %all-to-all-start = ((bf16[8,352,128]{2,1,0:T(8,128)(2,1)}), bf16[8,352,128]{2,1,0:T(8,128)(2,1)S(1)}, u32[]{:S(2)}, u32[]{:S(2)}) async-start(bf16[8,352,128]{2,1,0:T(8,128)(2,1)} %pack_inputs.1), calls=%async_computation | async-start | bytes 1441792 | tf_op jit(solution)/shard_map/all_to_all | solution.py:323
  8.1 13.5 %collective-permute-start.1 = (bf16[2,4,64,256]{3,2,1,0:T(8,128)(2,1)S(1)}, bf16[2,4,64,256]{3,2,1,0:T(8,128)(2,1)S(1)}, u32[]{:S(2)}, u32[]{:S(2)}) collective-permute-start(bf16[2,4,64,256]{3,2,1,0:T(8,128)(2,1)S(1)} %get-tuple-element.46), channel_id=1, source_target_pairs={{0,120},{8,16},{16,8},{24,32},{32,24},{40,48},{48,40},{56,64},{64,... | collective-permute-start | bytes 786440 | tf_op jit(solution)/shard_map/ppermute | solution.py:318
  14.7 8.4 %collective-permute-start = (bf16[2,4,64,256]{3,2,1,0:T(8,128)(2,1)S(1)}, bf16[2,4,64,256]{3,2,1,0:T(8,128)(2,1)S(1)}, u32[]{:S(2)}, u32[]{:S(2)}) collective-permute-start(bf16[2,4,64,256]{3,2,1,0:T(8,128)(2,1)S(1)} %get-tuple-element.47), channel_id=1, source_target_pairs={{0,8},{8,0},{16,24},{24,16},{32,40},{40,32},{48,56},{56,48},{64,72... | collective-permute-start | bytes 786440 | tf_op jit(solution)/shard_map/ppermute | solution.py:317
  14.7 16.9 %collective-permute-start.6 = (bf16[27,32,128]{2,1,0:T(8,128)(2,1)}, bf16[27,32,128]{2,1,0:T(8,128)(2,1)S(1)}, u32[]{:S(2)}, u32[]{:S(2)}) collective-permute-start(bf16[27,32,128]{2,1,0:T(8,128)(2,1)} %param.6), channel_id=1, source_target_pairs={{0,6},{1,7},{2,4},{3,5},{4,2},{5,3},{6,0},{7,1},{8,14},{9,15},{10,... | collective-permute-start | bytes 663560 | tf_op jit(solution)/shard_map/ppermute | solution.py:325
  17.9 14.4 %collective-permute-start.5 = (bf16[27,32,128]{2,1,0:T(8,128)(2,1)}, bf16[27,32,128]{2,1,0:T(8,128)(2,1)S(1)}, u32[]{:S(2)}, u32[]{:S(2)}) collective-permute-start(bf16[27,32,128]{2,1,0:T(8,128)(2,1)} %param.6), channel_id=1, source_target_pairs={{0,4},{1,5},{2,6},{3,7},{4,0},{5,1},{6,2},{7,3},{8,12},{9,13},{10,... | collective-permute-start | bytes 663560 | tf_op jit(solution)/shard_map/ppermute | solution.py:325
  18.7 15.6 %collective-permute-start.4 = (bf16[27,32,128]{2,1,0:T(8,128)(2,1)}, bf16[27,32,128]{2,1,0:T(8,128)(2,1)S(1)}, u32[]{:S(2)}, u32[]{:S(2)}) collective-permute-start(bf16[27,32,128]{2,1,0:T(8,128)(2,1)} %param.6), channel_id=1, source_target_pairs={{0,2},{1,3},{2,0},{3,1},{4,6},{5,7},{6,4},{7,5},{8,10},{9,11},{10,... | collective-permute-start | bytes 663560 | tf_op jit(solution)/shard_map/ppermute | solution.py:325
  19.9 14.5 %copy-start = (bf16[27,32,128]{2,1,0:T(8,128)(2,1)S(1)}, bf16[27,32,128]{2,1,0:T(8,128)(2,1)}, u32[]{:S(2)}) copy-start(bf16[27,32,128]{2,1,0:T(8,128)(2,1)} %param.6) | copy-start | bytes 663556
  27.3 13.5 %collective-permute-start.3 = (bf16[2,2,128,128]{3,2,1,0:T(8,128)(2,1)S(1)}, bf16[2,2,128,128]{3,2,1,0:T(8,128)(2,1)S(1)}, u32[]{:S(2)}, u32[]{:S(2)}) collective-permute-start(bf16[2,2,128,128]{3,2,1,0:T(8,128)(2,1)S(1)} %get-tuple-element.26.own), channel_id=1, source_target_pairs={{0,120},{8,16},{16,8},{24,32},{32,24},{40,48},{48,40},{56,64},{64,... | collective-permute-start | bytes 393224 | tf_op jit(solution)/shard_map/ppermute | solution.py:351
  31.0 9.8 %collective-permute-start.2 = (bf16[2,2,128,128]{3,2,1,0:T(8,128)(2,1)S(1)}, bf16[2,2,128,128]{3,2,1,0:T(8,128)(2,1)S(1)}, u32[]{:S(2)}, u32[]{:S(2)}) collective-permute-start(bf16[2,2,128,128]{3,2,1,0:T(8,128)(2,1)S(1)} %get-tuple-element.26.own), channel_id=1, source_target_pairs={{0,8},{8,0},{16,24},{24,16},{32,40},{40,32},{48,56},{56,48},{64,72... | collective-permute-start | bytes 393224 | tf_op jit(solution)/shard_map/ppermute | solution.py:350
  31.6 5.8 %collective-permute-start.8 = (bf16[8,64,128]{2,1,0:T(8,128)(2,1)S(1)}, bf16[8,64,128]{2,1,0:T(8,128)(2,1)S(1)}, u32[]{:S(2)}, u32[]{:S(2)}) collective-permute-start(bf16[8,64,128]{2,1,0:T(8,128)(2,1)S(1)} %get-tuple-element.32), channel_id=1, source_target_pairs={{0,0},{1,16},{2,32},{3,48},{4,64},{5,80},{6,96},{7,112},{8,8},{9,2... | collective-permute-start | bytes 393224 | tf_op jit(solution)/shard_map/ppermute | solution.py:337
  32.3 7.9 %collective-permute-start.9 = (bf16[8,64,128]{2,1,0:T(8,128)(2,1)S(1)}, bf16[8,64,128]{2,1,0:T(8,128)(2,1)S(1)}, u32[]{:S(2)}, u32[]{:S(2)}) collective-permute-start(bf16[8,64,128]{2,1,0:T(8,128)(2,1)S(1)} %get-tuple-element.33), channel_id=1, source_target_pairs={{0,8},{1,24},{2,40},{3,56},{4,72},{5,88},{6,104},{7,120},{8,0},{9,... | collective-permute-start | bytes 393224 | tf_op jit(solution)/shard_map/ppermute | solution.py:338
  34.5 6.3 %collective-permute-start.7 = (bf16[4,27,32,128]{3,2,1,0:T(8,128)(2,1)S(1)}, bf16[4,27,32,128]{3,2,1,0:T(8,128)(2,1)S(1)}, u32[]{:S(2)}, u32[]{:S(2)}) collective-permute-start(bf16[4,27,32,128]{3,2,1,0:T(8,128)(2,1)S(1)} %pad_maximum_fusion.weight), channel_id=1, source_target_pairs={{0,1},{1,0},{2,3},{3,2},{4,5},{5,4},{6,7},{7,6},{8,9},{9,8},{10,11... | collective-permute-start | bytes 2654216 | tf_op jit(solution)/shard_map/ppermute | solution.py:353
  45.3 16.1 %collective-permute-start.12 = (bf16[4,27,32,128]{3,2,1,0:T(8,128)(2,1)S(1)}, bf16[4,27,32,128]{3,2,1,0:T(8,128)(2,1)S(1)}, u32[]{:S(2)}, u32[]{:S(2)}) collective-permute-start(bf16[4,27,32,128]{3,2,1,0:T(8,128)(2,1)S(1)} %get-tuple-element.41), channel_id=1, source_target_pairs={{0,1},{1,0},{2,3},{3,2},{4,5},{5,4},{6,7},{7,6},{8,9},{9,8},{10,11... | collective-permute-start | bytes 2654216 | tf_op jit(solution)/shard_map/ppermute | solution.py:381
  49.4 12.0 %collective-permute-start.10 = (bf16[2,128,256]{2,1,0:T(8,128)(2,1)S(1)}, bf16[2,128,256]{2,1,0:T(8,128)(2,1)S(1)}, u32[]{:S(2)}, u32[]{:S(2)}) collective-permute-start(bf16[2,128,256]{2,1,0:T(8,128)(2,1)S(1)} %get-tuple-element.35), channel_id=1, source_target_pairs={{0,8},{8,0},{16,24},{24,16},{32,40},{40,32},{48,56},{56,48},{64,72... | collective-permute-start | bytes 393224 | tf_op jit(solution)/shard_map/ppermute | solution.py:371
  51.3 15.1 %collective-permute-start.11 = (bf16[2,128,256]{2,1,0:T(8,128)(2,1)S(1)}, bf16[2,128,256]{2,1,0:T(8,128)(2,1)S(1)}, u32[]{:S(2)}, u32[]{:S(2)}) collective-permute-start(bf16[2,128,256]{2,1,0:T(8,128)(2,1)S(1)} %get-tuple-element.40), channel_id=1, source_target_pairs={{0,120},{8,16},{16,8},{24,32},{32,24},{40,48},{48,40},{56,64},{64,... | collective-permute-start | bytes 393224 | tf_op jit(solution)/shard_map/ppermute | solution.py:372
  61.6 14.6 %collective-permute-start.13 = (bf16[27,32,128]{2,1,0:T(8,128)(2,1)S(1)}, bf16[27,32,128]{2,1,0:T(8,128)(2,1)S(1)}, u32[]{:S(2)}, u32[]{:S(2)}) collective-permute-start(bf16[27,32,128]{2,1,0:T(8,128)(2,1)S(1)} %get-tuple-element.43), channel_id=1, source_target_pairs={{0,2},{1,3},{2,0},{3,1},{4,6},{5,7},{6,4},{7,5},{8,10},{9,11},{10,... | collective-permute-start | bytes 663560 | tf_op jit(solution)/shard_map/ppermute | solution.py:386
  61.7 14.5 %collective-permute-start.14 = (bf16[27,32,128]{2,1,0:T(8,128)(2,1)S(1)}, bf16[27,32,128]{2,1,0:T(8,128)(2,1)S(1)}, u32[]{:S(2)}, u32[]{:S(2)}) collective-permute-start(bf16[27,32,128]{2,1,0:T(8,128)(2,1)S(1)} %get-tuple-element.44), channel_id=1, source_target_pairs={{0,4},{1,5},{2,6},{3,7},{4,0},{5,1},{6,2},{7,3},{8,12},{9,13},{10,... | collective-permute-start | bytes 663560 | tf_op jit(solution)/shard_map/ppermute | solution.py:386
  66.3 12.1 %collective-permute-start.15 = (bf16[27,32,128]{2,1,0:T(8,128)(2,1)S(1)}, bf16[27,32,128]{2,1,0:T(8,128)(2,1)S(1)}, u32[]{:S(2)}, u32[]{:S(2)}) collective-permute-start(bf16[27,32,128]{2,1,0:T(8,128)(2,1)S(1)} %get-tuple-element.45), channel_id=1, source_target_pairs={{0,6},{1,7},{2,4},{3,5},{4,2},{5,3},{6,0},{7,1},{8,14},{9,15},{10,... | collective-permute-start | bytes 663560 | tf_op jit(solution)/shard_map/ppermute | solution.py:386
  71.7 14.4 %all-to-all-start.1 = ((bf16[8,3,16,576]{3,2,1,0:T(8,128)(2,1)}), bf16[8,3,16,576]{3,2,1,0:T(8,128)(2,1)S(1)}, u32[]{:S(2)}, u32[]{:S(2)}) async-start(bf16[8,3,16,576]{3,2,1,0:T(8,128)(2,1)} %first_weights.1), calls=%async_computation.1 | async-start | bytes 983040 | tf_op jit(solution)/shard_map/all_to_all | solution.py:395

commit v3 on v2

--- a/solution.py
+++ b/solution.py
@@ -47,24 +47,22 @@
     return jnp.where(same & ((row & 127) == (col & 127) + (e - 1)), 1.0, 0.0).astype(BF)
 
 
-def pack_inputs(weight, cot, out):
+def pack_weights(weight, second, out):
     for a in range(3):
         for j in range(0, 8, 2):
             pair = jnp.concatenate([weight[9 * a + j], weight[9 * a + j + 1]], axis=1)
-            for f in range(8):
-                out[f, a * 64 + j * 8 : a * 64 + j * 8 + 16] = pair
-    pair = jnp.concatenate([weight[8], weight[17]], axis=1)
-    last = jnp.concatenate([weight[26], jnp.zeros_like(weight[26])], axis=1)
-    for f in range(8):
-        out[f, 192:208] = pair
-        out[f, 208:224] = last
-        out[f, 224:352] = cot[0, 2 * f : 2 * f + 2].reshape(128, 128)
-
-
-def first_rows(packed, a):
-    tiles = [packed[:, a * 64 + j * 16 : a * 64 + j * 16 + 16].reshape(128, 128) for j in range(4)]
-    row = 208 if a == 2 else 192
-    tiles.append(packed[:, row : row + 16].reshape(128, 128)[:, 64 * (a % 2) : 64 * (a % 2) + 64])
+            out[a * 64 + j * 8 : a * 64 + j * 8 + 16] = pair
+    out[192:208] = jnp.concatenate([weight[8], weight[17]], axis=1)
+    out[208:224] = jnp.concatenate([weight[26], jnp.zeros_like(weight[26])], axis=1)
+    out[224:1088] = second[...].reshape(864, 128)
+
+
+def first_rows(pieces, a):
+    def stacked(row):
+        return jnp.concatenate([piece[row : row + 16] for piece in pieces], axis=0)
+
+    tiles = [stacked(a * 64 + j * 16) for j in range(4)]
+    tiles.append(stacked(208 if a == 2 else 192)[:, 64 * (a % 2) : 64 * (a % 2) + 64])
     return jnp.concatenate(tiles, axis=1)
 
 
@@ -74,10 +72,16 @@
     return jnp.where(even, two, one), jnp.where(even, one, two)
 
 
-def first_forward(place, own, one, two, packed, taps, slope, pooled, weight):
+def first_forward(place, own, one, two, packed, across, taps, slope, pooled, weight, edges):
     shifts = [split_shift(e) for e in range(3)]
-    for a in range(3):
-        weight[a] = first_rows(packed, a)
+    pieces = []
+    for f in range(8):
+        where = place[1] ^ f
+        pieces.append(jnp.where((where & 1) == 0, packed[where >> 1], across[where >> 1]))
+    parts = [first_rows(pieces, a) for a in range(3)]
+    weight[...] = jnp.concatenate(parts, axis=1)
+    edges[0] = jnp.concatenate([w[:, 192:] for w in parts], axis=1)
+    edges[1] = jnp.concatenate([w[:, :384] for w in parts], axis=1)
 
     @pl.loop(0, 2)
     def _(s):
@@ -93,13 +97,10 @@
             for z in range(2):
                 for y in (2 * pair, 2 * pair + 1):
                     first, last = max(y - 1, 0), min(y + 2, 4)
-                    left = (first - y + 1) * 192
                     size = (last - first) * 192
-                    pre = None
-                    for a in range(3):
-                        w = weight[a, :, left : left + size]
-                        part = dot(w, taps[s, z + a, first:last].reshape(size, 256))
-                        pre = part if pre is None else pre + part
+                    w = weight[...] if size == 576 else edges[y // 3]
+                    cells = [taps[s, z + a, first:last].reshape(size, 256) for a in range(3)]
+                    pre = dot(w, jnp.concatenate(cells, axis=0))
                     value, rate = gelu_and_slope(pre)
                     slope[s, z, y] = rate
                     total = value if total is None else total + value
@@ -111,28 +112,15 @@
     return [filt ^ (2 * d + c) for c in range(2) for d in range(4)]
 
 
-def split_cot(place, packed, same, other):
-    for f in range(8):
-        same[f] = packed[f, pl.ds(pl.multiple_of(224 + 64 * place[0], 32), 64)]
-        other[f] = packed[f, pl.ds(pl.multiple_of(288 - 64 * place[0], 32), 64)]
-
-
-def join_cot(place, same, other, out):
+def second_layer(place, own, one, two, weight, across, cot, grads, taps, mid, first, second, spread):
     even = place[0] == 0
     blocks = other_blocks(place)
-    for y in range(2):
-        here = pl.ds(32 * y, 32)
-        a = jnp.concatenate([same[f, here] for f in blocks], axis=0)
-        b = jnp.concatenate([other[f, here] for f in blocks], axis=0)
-        out[y, :, 0:128] = jnp.where(even, a, b)
-        out[y, :, 128:256] = jnp.where(even, b, a)
-
-
-def second_layer(place, own, one, two, weight, across, cot, grads, taps, mid, first, second, spread):
-    even = place[0] == 0
 
     def rows(k):
-        return jnp.concatenate([weight[:, k].reshape(128, 128), across[:, k].reshape(128, 128)], axis=0)
+        here = slice(224 + 32 * k, 256 + 32 * k)
+        return jnp.concatenate(
+            [weight[:, here].reshape(128, 128), across[:, here].reshape(128, 128)], axis=0
+        )
 
     left, right = pair_shift(0), pair_shift(2)
     for y in range(2):
@@ -154,7 +142,8 @@
             part = dot(w, taps[a].reshape(768, 256))
             pre = part if pre is None else pre + part
         _, rate = gelu_and_slope(pre)
-        grad = (cot[y].astype(F32) * rate).astype(BF)
+        pair = [jnp.concatenate([cot[f, j, y] for f in blocks], axis=0) for j in range(2)]
+        grad = (jnp.concatenate(pair, axis=1).astype(F32) * rate).astype(BF)
         grads[y] = grad
         spread[y, 0] = dot(grad, right).astype(BF)
         spread[y, 1] = grad
@@ -211,19 +200,27 @@
                 + jnp.where(inside, two[pair, :, lanes].astype(F32), 0.0)
             ) * 0.125
             back = jnp.concatenate([back, back], axis=1)
-            for z in range(2):
-                for y in (2 * pair, 2 * pair + 1):
-                    inner = (slope[s, z, y] * back).astype(BF)
-                    first, last = max(y - 1, 0), min(y + 2, 4)
-                    left = (first - y + 1) * 192
-                    size = (last - first) * 192
-                    for a in range(3):
-                        total[a, :, left : left + size] += dot_nt(
-                            inner, taps[s, z + a, first:last].reshape(size, 256)
-                        )
+            inner = [
+                jnp.concatenate(
+                    [(slope[s, z, 2 * pair + i] * back).astype(BF) for i in range(2)], axis=0
+                )
+                for z in range(2)
+            ]
+            inner = jnp.concatenate(inner, axis=1)
+            for a in range(3):
+                cells = [
+                    taps[s, z + a, pair : pair + 3].reshape(576, 256) for z in range(2)
+                ]
+                part = dot_nt(jnp.concatenate(cells, axis=1), inner)
+                if pair == 0:
+                    total[a] += part[:, 128:]
+                    total[a, 192:576] += part[0:384, :128]
+                else:
+                    total[a] += part[:, :128]
+                    total[a, 0:384] += part[192:576, 128:]
 
     for a in range(3):
-        out[:, a] = total[a].astype(BF).reshape(8, 16, 576)
+        out[:, a] = total[a].T.astype(BF).reshape(8, 16, 576)
 
 
 def add_across(own, one, two, three, out):
@@ -268,7 +265,7 @@
 
 
 VMEM = pl.BlockSpec(memory_space=pltpu.VMEM)
-HBM = pl.BlockSpec(memory_space=pltpu.HBM)
+HBM = pl.BlockSpec(memory_space=pl.ANY)
 SMEM = pl.BlockSpec(memory_space=pltpu.SMEM)
 
 
@@ -317,46 +314,31 @@
     one = lax.ppermute(face(1 - parity), "space", ones)
     two = lax.ppermute(face(parity), "space", twos)
     own = lax.dynamic_slice_in_dim(volume, 2 * filt, 2, axis=0)
-    (pieces,) = call(
-        pack_inputs, (weight_first, cotangent), (((8, 352, 128), BF),), [], 0, "pack_inputs", limit=60
-    )
-    packed = lax.all_to_all(pieces, "filt", 0, 0, tiled=True)
-    weights = [weight_second] + [
-        lax.ppermute(after(weight_second, pieces), "filt", by_x[d]) for d in range(1, 4)
-    ]
-
-    def turned(shift):
-        return [
-            (s * nf + f, (2 * f + (s + shift) % 2) * nf + s // 2)
-            for s in range(ns)
-            for f in range(nf)
-        ]
-
-    half = ((8, 64, 128), BF)
-    cot_a, cot_b = call(split_cot, (place, packed), (half, half), [], 0, "split_cot")
-    cot_a = lax.ppermute(cot_a, ("space", "filt"), turned(0))
-    cot_b = lax.ppermute(cot_b, ("space", "filt"), turned(1))
+    by_sample = lax.all_to_all(cotangent[0], "space", 0, 0, tiled=True)
+    (piece,) = call(
+        pack_weights, (after(weight_first, one), weight_second), (((1088, 128), BF),), [], 0, "pack_weights"
+    )
+    others = [lax.ppermute(piece, "filt", by_x[d]) for d in range(1, 4)]
+    cot = lax.all_to_all(by_sample.reshape(nf, 2, 2, 32, 128), "filt", 0, 0, tiled=True)
+    weights = jnp.stack([after(w, own, two, cot) for w in [piece] + others])
+    across = lax.ppermute(weights, "filt", by_core)
 
     taps, slope, pooled = call(
         first_forward,
-        (place, own, one, two, packed),
+        (place, after(own, cot), one, two, weights, across),
         (((2, 4, 4, 192, 256), BF), ((2, 2, 4, 128, 256), F32), ((2, 2, 128, 128), BF)),
         [
-            pltpu.VMEM((3, 128, 576), BF),
+            pltpu.VMEM((128, 1728), BF),
+            pltpu.VMEM((2, 128, 1152), BF),
         ],
         LONG,
         "first_forward",
     )
     pool_one = lax.ppermute(pooled, "space", ones)
     pool_two = lax.ppermute(pooled, "space", twos)
-    same_core = jnp.stack([after(w, pooled) for w in weights])
-    other_core = lax.ppermute(same_core, "filt", by_core)
-    (cot,) = call(
-        join_cot, (place, cot_a, cot_b), (((2, 256, 256), BF),), [], LONG, "join_cot"
-    )
     grads, taps_second, mid, out_one, out_two = call(
         second_layer,
-        (place, pooled, pool_one, pool_two, same_core, other_core, cot),
+        (place, pooled, pool_one, pool_two, weights, across, cot),
         (
             ((2, 256, 256), BF),
             ((3, 2, 384, 256), BF),
@@ -388,7 +370,7 @@
         first_weights,
         (place, taps, slope, mid, after(back_one, mine), back_two),
         (((8, 3, 16, 576), BF),),
-        [pltpu.VMEM((3, 128, 576), F32)],
+        [pltpu.VMEM((3, 576, 128), F32)],
         LONG,
         "first_weights",
     )

time: 114 us -> 110 us (0.965)
  starting transfers between devices: 49.7 us -> 39.9 us
  waiting for transfers between devices: 15.9 us -> 25.6 us
  Pallas kernels: 18.5 us -> 13.8 us
  local copies, waits for them, and re-layouts: 2.15 us -> 3.89 us
    all_to_all x1 -> x2, starting transfers between devices: 4.38 us -> 12.1 us  [the longest x1 7.81 us: per_device(): by_sample = lax.all_to_all(cotangent[0], 'space', 0, 0, tiled=True)]
    ppermute x1, starting transfers between devices: 10.1 us -> 3.41 us  [per_device(): back_two = lax.ppermute(out_two, 'space', twos)]
    all_to_all x1 -> x2, waiting for transfers between devices: 0.01 us -> 5.75 us  [the longest x1 5.74 us: per_device(): lax.all_to_all(by_sample.reshape(nf, 2, 2, 32, 128), 'filt', 0, 0, tiled=...]
    ppermute x6 -> x4, starting transfers between devices: 9.73 us -> 4.26 us  [the longest x3 4.17 us: per_device(): others = [lax.ppermute(piece, 'filt', by_x[d]) for d in range(1, 4)]]
    pallas_call x12 -> x10, Pallas kernels: 18.5 us -> 13.8 us  [call(): pl.pallas_call(kernel, out_shape=shapes, in_specs=[SMEM if x.dtype == jnp...]
    ppermute x1, waiting for transfers between devices: 0.01 us -> 4.43 us  [per_device(): pool_two = lax.ppermute(pooled, 'space', twos)]
    ppermute x1, starting transfers between devices: 4.11 us -> 0.09 us  [per_device(): across = lax.ppermute(across, 'filt', by_core)]
    ppermute x1, waiting for transfers between devices: 0.01 us -> 2.14 us  [per_device(): back_one = lax.ppermute(out_one, 'space', ones)]
  transfers between devices with their start and end apart: 18 -> 17, of which waited for: 5 -> 7; matrix products, arithmetic and copies ran while one was open for 2% -> 1% of each run, Pallas kernels for 10% -> 4%
where the time goes in v3:
time: 110 us
  starting transfers between devices  39.9 us (36%)
  waiting for transfers between devices  25.6 us (23%)
  blocking collectives  25.4 us (23%)
  Pallas kernels  13.8 us (13%)
  local copies, waits for them, and re-layouts  3.89 us (4%)
    pallas_call x10, Pallas kernels, call(): pl.pallas_call(kernel, out_shape=shapes, in_specs=[SMEM if x.dtype == jnp...  13.8 us
    all_to_all x1, blocking collectives, per_device(): parts = lax.all_to_all(rows.reshape(ns, 72, 128), 'space', 0, 0, tiled=True)  13.6 us
    all_to_all x1, blocking collectives, per_device(): rows = lax.all_to_all(mine, 'space', 0, 0, tiled=True).reshape(1152, 128)  11.7 us
    all_to_all x1, starting transfers between devices, per_device(): by_sample = lax.all_to_all(cotangent[0], 'space', 0, 0, tiled=True)  7.81 us
    all_to_all x1, waiting for transfers between devices, per_device(): got_first = lax.all_to_all(terms_first, 'filt', 0, 0, tiled=True)  7.6 us
    all_to_all x1, waiting for transfers between devices, per_device(): lax.all_to_all(by_sample.reshape(nf, 2, 2, 32, 128), 'filt', 0, 0, tiled=...  5.74 us
    ppermute x1, starting transfers between devices, per_device(): two = lax.ppermute(face(parity), 'space', twos)  5.2 us
    ppermute x3, starting transfers between devices, per_device(): lax.ppermute(others[d - 1], 'filt', by_x[d])  4.78 us
  transfers between devices with their start and end apart: 17, of which 7 were waited for; matrix products, arithmetic and copies ran while one was open for 1% of the time, Pallas kernels for 4%

profile of v3, /device:TPU:0, one launch (start us, length us, event | category | flops | bytes accessed | tf_op | source)
XLA Modules:
  0.0 109.7 jit_solution(13063898039444918301)
XLA Ops:
  0.7 1.2 %dynamic-slice_bitcast_fusion = (bf16[2,4,64,256]{3,2,1,0:T(8,128)(2,1)S(1)}, bf16[2,4,64,256]{3,2,1,0:T(8,128)(2,1)S(1)}) fusion(bf16[16,2,4,64,256]{4,3,2,1,0:T(8,128)(2,1)} %param.4, s32[]{:T(128)S(6)} %select_n.19, s32[]{:T(128)S(6)} %select_n.21, s32[]{:T(128)S(6)} %select_n.20), kind=kLoop, calls=%fused_computation.1 | loop fusion | bytes 1048588 | tf_op jit(solution)/shard_map/squeeze | solution.py:312
  1.8 1.7 %collective-permute-start = (bf16[2,4,64,256]{3,2,1,0:T(8,128)(2,1)S(1)}, bf16[2,4,64,256]{3,2,1,0:T(8,128)(2,1)S(1)}, u32[]{:S(2)}, u32[]{:S(2)}) collective-permute-start(bf16[2,4,64,256]{3,2,1,0:T(8,128)(2,1)S(1)} %get-tuple-element.45), channel_id=1, source_target_pairs={{0,8},{8,0},{16,24},{24,16},{32,40},{40,32},{48,56},{56,48},{64,72... | collective-permute-start | bytes 786440 | tf_op jit(solution)/shard_map/ppermute | solution.py:314
  3.6 7.8 %all-to-all-start = ((bf16[16,2,32,128]{3,2,1,0:T(8,128)(2,1)}), bf16[16,2,32,128]{3,2,1,0:T(8,128)(2,1)}, u32[]{:S(2)}, u32[]{:S(2)}) async-start(bf16[16,2,32,128]{3,2,1,0:T(8,128)(2,1)} %bitcast.21), calls=%async_computation | async-start | bytes 524288 | tf_op jit(solution)/shard_map/all_to_all | solution.py:317
  11.4 0.0 collective-permute-done.one
  11.4 0.1 pack_weights.1
  11.5 2.8 %collective-permute-start.4 = (bf16[1088,128]{1,0:T(8,128)(2,1)S(1)}, bf16[1088,128]{1,0:T(8,128)(2,1)S(1)}, u32[]{:S(2)}, u32[]{:S(2)}) collective-permute-start(bf16[1088,128]{1,0:T(8,128)(2,1)S(1)} %pack_weights.1), channel_id=1, source_target_pairs={{0,6},{1,7},{2,4},{3,5},{4,2},{5,3},{6,0},{7,1},{8,14},{9,15},{10,... | collective-permute-start | bytes 835592 | tf_op jit(solution)/shard_map/ppermute | solution.py:321
  14.3 0.8 collective-permute-start.3
  15.1 0.5 collective-permute-start.2
  15.7 5.2 %collective-permute-start.1 = (bf16[2,4,64,256]{3,2,1,0:T(8,128)(2,1)S(1)}, bf16[2,4,64,256]{3,2,1,0:T(8,128)(2,1)S(1)}, u32[]{:S(2)}, u32[]{:S(2)}) collective-permute-start(bf16[2,4,64,256]{3,2,1,0:T(8,128)(2,1)S(1)} %get-tuple-element.44), channel_id=1, source_target_pairs={{0,120},{8,16},{16,8},{24,32},{32,24},{40,48},{48,40},{56,64},{64,... | collective-permute-start | bytes 786440 | tf_op jit(solution)/shard_map/ppermute | solution.py:315
  20.9 0.0 all-to-all-done
  20.9 4.3 %all-to-all-start.1 = ((bf16[8,2,2,32,128]{4,3,2,1,0:T(8,128)(2,1)}), bf16[8,2,2,32,128]{4,3,2,1,0:T(8,128)(2,1)S(1)}, u32[]{:S(2)}, u32[]{:S(2)}) async-start(bf16[8,2,2,32,128]{4,3,2,1,0:T(8,128)(2,1)} %bitcast.4), calls=%async_computation.1 | async-start | bytes 524288 | tf_op jit(solution)/shard_map/all_to_all | solution.py:322
  25.2 1.1 constant_dynamic-slice_fusion.own
  26.3 0.0 collective-permute-done.1.two
  26.3 0.0 copy-start.2
  26.3 0.7 copy-done.2
  27.0 5.7 %all-to-all-done.1.cot = bf16[8,2,2,32,128]{4,3,2,1,0:T(8,128)(2,1)S(1)} async-done(((bf16[8,2,2,32,128]{4,3,2,1,0:T(8,128)(2,1)}), bf16[8,2,2,32,128]{4,3,2,1,0:T(8,128)(2,1)S(1)}, u32[]{:S(2)}, u32[]{:S(2)}) %all-to-all-start.1) | async-done | bytes 262176 | tf_op jit(solution)/shard_map/all_to_all | solution.py:322
  32.7 0.0 collective-permute-done.4
  32.7 0.1 pad_maximum_fusion.packed.weight
  32.9 0.1 collective-permute-start.5
  33.0 0.1 pad_add_fusion.place
  33.1 2.7 %collective-permute-done.5.across = bf16[4,1088,128]{2,1,0:T(8,128)(2,1)S(1)} collective-permute-done((bf16[4,1088,128]{2,1,0:T(8,128)(2,1)S(1)}, bf16[4,1088,128]{2,1,0:T(8,128)(2,1)S(1)}, u32[]{:S(2)}, u32[]{:S(2)}) %collective-permute-start.5) | collective-permute-done | bytes 1114144 | tf_op jit(solution)/shard_map/ppermute | solution.py:324
  35.7 0.9 copy-done.3
  36.7 4.0 %first_forward.1 = (bf16[2,4,4,192,256]{4,3,2,1,0:T(8,128)(2,1)S(1)}, f32[2,2,4,128,256]{4,3,2,1,0:T(8,128)S(1)}, bf16[2,2,128,128]{3,2,1,0:T(8,128)(2,1)S(1)}) custom-call(s32[3]{0:T(128)S(1)} %pad_add_fusion.place, bf16[2,2,4,64,256]{4,3,2,1,0:T(8,128)(2,1)S(1)} %constant_dynamic-slice_fusion.own, bf16[2,4,64,256]{3,2,1,0:T(8,128)(2,1)S(1)} %collective-permute-done.one, ...), custom_call_target="tpu_custom_call" | custom-call | flops 20000000000 | bytes 8650764 | tf_op jit(solution)/shard_map/first_forward/pallas_call | solution.py:275
  40.7 4.5 %collective-permute-start.7 = (bf16[2,2,128,128]{3,2,1,0:T(8,128)(2,1)S(1)}, bf16[2,2,128,128]{3,2,1,0:T(8,128)(2,1)S(1)}, u32[]{:S(2)}, u32[]{:S(2)}) collective-permute-start(bf16[2,2,128,128]{3,2,1,0:T(8,128)(2,1)S(1)} %get-tuple-element.31.own), channel_id=1, source_target_pairs={{0,120},{8,16},{16,8},{24,32},{32,24},{40,48},{48,40},{56,64},{64,... | collective-permute-start | bytes 393224 | tf_op jit(solution)/shard_map/ppermute | solution.py:338
  45.2 4.4 %collective-permute-done.7.two = bf16[2,2,128,128]{3,2,1,0:T(8,128)(2,1)S(1)} collective-permute-done((bf16[2,2,128,128]{3,2,1,0:T(8,128)(2,1)S(1)}, bf16[2,2,128,128]{3,2,1,0:T(8,128)(2,1)S(1)}, u32[]{:S(2)}, u32[]{:S(2)}) %collective-permute-start.7) | collective-permute-done | bytes 131104 | tf_op jit(solution)/shard_map/ppermute | solution.py:338
  49.7 0.8 collective-permute-done.6.one
  50.5 3.5 %second_layer.1 = (bf16[2,256,256]{2,1,0:T(8,128)(2,1)S(1)}, bf16[3,2,384,256]{3,2,1,0:T(8,128)(2,1)S(1)}, f32[2,128,256]{2,1,0:T(8,128)S(1)}, bf16[2,128,256]{2,1,0:T(8,128)(2,1)S(1)}, bf16[2,128,256]{2,1,0:T(8,128)(2,1)S(1)}) custom-call(s32[3]{0:T(128)S(1)} %pad_add_fusion.place, bf16[2,2,128,128]{3,2,1,0:T(8,128)(2,1)S(1)} %get-tuple-element.31.own, ...), custom_call_target="tpu_custom_call" | custom-call | flops 2000000000 | bytes 4849676 | tf_op jit(solution)/shard_map/second_layer/pallas_call | solution.py:275
  54.0 1.0 second_weights.1
  55.0 0.1 collective-permute-start.10
  55.1 0.4 collective-permute-start.8
  55.4 3.4 %collective-permute-start.9 = (bf16[2,128,256]{2,1,0:T(8,128)(2,1)S(1)}, bf16[2,128,256]{2,1,0:T(8,128)(2,1)S(1)}, u32[]{:S(2)}, u32[]{:S(2)}) collective-permute-start(bf16[2,128,256]{2,1,0:T(8,128)(2,1)S(1)} %get-tuple-element.38), channel_id=1, source_target_pairs={{0,120},{8,16},{16,8},{24,32},{32,24},{40,48},{48,40},{56,64},{64,... | collective-permute-start | bytes 393224 | tf_op jit(solution)/shard_map/ppermute | solution.py:354
  58.9 2.1 %collective-permute-done.8.one = bf16[2,128,256]{2,1,0:T(8,128)(2,1)S(1)} collective-permute-done((bf16[2,128,256]{2,1,0:T(8,128)(2,1)S(1)}, bf16[2,128,256]{2,1,0:T(8,128)(2,1)S(1)}, u32[]{:S(2)}, u32[]{:S(2)}) %collective-permute-start.8) | collective-permute-done | bytes 131104 | tf_op jit(solution)/shard_map/ppermute | solution.py:353
  61.0 0.2 add_cores.1
  61.2 0.3 collective-permute-start.11
  61.5 1.7 %collective-permute-start.12 = (bf16[27,32,128]{2,1,0:T(8,128)(2,1)S(1)}, bf16[27,32,128]{2,1,0:T(8,128)(2,1)S(1)}, u32[]{:S(2)}, u32[]{:S(2)}) collective-permute-start(bf16[27,32,128]{2,1,0:T(8,128)(2,1)S(1)} %get-tuple-element.42), channel_id=1, source_target_pairs={{0,4},{1,5},{2,6},{3,7},{4,0},{5,1},{6,2},{7,3},{8,12},{9,13},{10,... | collective-permute-start | bytes 663560 | tf_op jit(solution)/shard_map/ppermute | solution.py:368
  63.2 2.8 %collective-permute-start.13 = (bf16[27,32,128]{2,1,0:T(8,128)(2,1)S(1)}, bf16[27,32,128]{2,1,0:T(8,128)(2,1)S(1)}, u32[]{:S(2)}, u32[]{:S(2)}) collective-permute-start(bf16[27,32,128]{2,1,0:T(8,128)(2,1)S(1)} %get-tuple-element.43), channel_id=1, source_target_pairs={{0,6},{1,7},{2,4},{3,5},{4,2},{5,3},{6,0},{7,1},{8,14},{9,15},{10,... | collective-permute-start | bytes 663560 | tf_op jit(solution)/shard_map/ppermute | solution.py:368
  66.0 0.0 collective-permute-done.9.two
  66.0 3.9 %first_weights.1 = bf16[8,3,16,576]{3,2,1,0:T(8,128)(2,1)} custom-call(s32[3]{0:T(128)S(1)} %pad_add_fusion.place, bf16[2,4,4,192,256]{4,3,2,1,0:T(8,128)(2,1)S(1)} %get-tuple-element.29.taps, f32[2,2,4,128,256]{4,3,2,1,0:T(8,128)S(1)} %get-tuple-element.30.slope, f32[2,128,256]{2,1,0:T(8,128)S(1)} %get-tuple-element.32.mid, ...), custom_call_target="tpu_custom_call" | custom-call | flops 20000000000 | bytes 6209548 | tf_op jit(solution)/shard_map/first_weights/pallas_call | solution.py:275
  69.9 3.5 %all-to-all-start.2 = ((bf16[8,3,16,576]{3,2,1,0:T(8,128)(2,1)}), bf16[8,3,16,576]{3,2,1,0:T(8,128)(2,1)S(1)}, u32[]{:S(2)}, u32[]{:S(2)}) async-start(bf16[8,3,16,576]{3,2,1,0:T(8,128)(2,1)} %first_weights.1), calls=%async_computation.2 | async-start | bytes 983040 | tf_op jit(solution)/shard_map/all_to_all | solution.py:377
  73.4 0.0 collective-permute-done.11.one
  73.4 2.2 %collective-permute-done.13.three = bf16[27,32,128]{2,1,0:T(8,128)(2,1)S(1)} collective-permute-done((bf16[27,32,128]{2,1,0:T(8,128)(2,1)S(1)}, bf16[27,32,128]{2,1,0:T(8,128)(2,1)S(1)}, u32[]{:S(2)}, u32[]{:S(2)}) %collective-permute-start.13) | collective-permute-done | bytes 221216 | tf_op jit(solution)/shard_map/ppermute | solution.py:368
  75.6 0.1 add_across.1.second
  75.7 7.6 %all-to-all-done.2.first = bf16[8,3,16,576]{3,2,1,0:T(8,128)(2,1)S(1)} async-done(((bf16[8,3,16,576]{3,2,1,0:T(8,128)(2,1)}), bf16[8,3,16,576]{3,2,1,0:T(8,128)(2,1)S(1)}, u32[]{:S(2)}, u32[]{:S(2)}) %all-to-all-start.2) | async-done | bytes 442400 | tf_op jit(solution)/shard_map/all_to_all | solution.py:377
  83.3 0.1 pack.1
  83.4 13.6 %all_to_all.25.parts = bf16[16,72,128]{2,1,0:T(8,128)(2,1)S(1)} all-to-all(bf16[16,72,128]{2,1,0:T(8,128)(2,1)S(1)} %bitcast.16), channel_id=1, replica_groups=mesh['space'=16,'filt'=8] {'space'}, dimensions={0} | all-to-all | bytes 589824 | tf_op jit(solution)/shard_map/all_to_all | solution.py:383
  97.0 0.1 add_up.1
  97.1 11.7 %all_to_all.26 = bf16[16,72,128]{2,1,0:T(8,128)(2,1)S(1)} all-to-all(bf16[16,72,128]{2,1,0:T(8,128)(2,1)S(1)} %add_up.1), channel_id=1, replica_groups=mesh['space'=16,'filt'=8] {'space'}, dimensions={0} | all-to-all | bytes 589824 | tf_op jit(solution)/shard_map/all_to_all | solution.py:385
  108.8 0.9 unpack.1
  (10 shorter events, 0.0 us)
Async XLA Ops:
  0.6 10.8 %copy-start.1 = (bf16[27,16,64]{2,1,0:T(8,128)(2,1)S(1)}, bf16[27,16,64]{2,1,0:T(8,128)(2,1)}, u32[]{:S(2)}) copy-start(bf16[27,16,64]{2,1,0:T(8,128)(2,1)} %weight) | copy-start | bytes 165892
  0.6 10.8 %copy-start = (bf16[27,32,128]{2,1,0:T(8,128)(2,1)S(1)}, bf16[27,32,128]{2,1,0:T(8,128)(2,1)}, u32[]{:S(2)}) copy-start(bf16[27,32,128]{2,1,0:T(8,128)(2,1)} %second.1) | copy-start | bytes 663556
  1.8 9.6 %collective-permute-start = (bf16[2,4,64,256]{3,2,1,0:T(8,128)(2,1)S(1)}, bf16[2,4,64,256]{3,2,1,0:T(8,128)(2,1)S(1)}, u32[]{:S(2)}, u32[]{:S(2)}) collective-permute-start(bf16[2,4,64,256]{3,2,1,0:T(8,128)(2,1)S(1)} %get-tuple-element.45), channel_id=1, source_target_pairs={{0,8},{8,0},{16,24},{24,16},{32,40},{40,32},{48,56},{56,48},{64,72... | collective-permute-start | bytes 786440 | tf_op jit(solution)/shard_map/ppermute | solution.py:314
  3.6 17.3 %all-to-all-start = ((bf16[16,2,32,128]{3,2,1,0:T(8,128)(2,1)}), bf16[16,2,32,128]{3,2,1,0:T(8,128)(2,1)}, u32[]{:S(2)}, u32[]{:S(2)}) async-start(bf16[16,2,32,128]{3,2,1,0:T(8,128)(2,1)} %bitcast.21), calls=%async_computation | async-start | bytes 524288 | tf_op jit(solution)/shard_map/all_to_all | solution.py:317
  11.5 21.2 %collective-permute-start.4 = (bf16[1088,128]{1,0:T(8,128)(2,1)S(1)}, bf16[1088,128]{1,0:T(8,128)(2,1)S(1)}, u32[]{:S(2)}, u32[]{:S(2)}) collective-permute-start(bf16[1088,128]{1,0:T(8,128)(2,1)S(1)} %pack_weights.1), channel_id=1, source_target_pairs={{0,6},{1,7},{2,4},{3,5},{4,2},{5,3},{6,0},{7,1},{8,14},{9,15},{10,... | collective-permute-start | bytes 835592 | tf_op jit(solution)/shard_map/ppermute | solution.py:321
  14.3 18.4 %collective-permute-start.3 = (bf16[1088,128]{1,0:T(8,128)(2,1)S(1)}, bf16[1088,128]{1,0:T(8,128)(2,1)S(1)}, u32[]{:S(2)}, u32[]{:S(2)}) collective-permute-start(bf16[1088,128]{1,0:T(8,128)(2,1)S(1)} %pack_weights.1), channel_id=1, source_target_pairs={{0,4},{1,5},{2,6},{3,7},{4,0},{5,1},{6,2},{7,3},{8,12},{9,13},{10,... | collective-permute-start | bytes 835592 | tf_op jit(solution)/shard_map/ppermute | solution.py:321
  15.1 17.6 %collective-permute-start.2 = (bf16[1088,128]{1,0:T(8,128)(2,1)S(1)}, bf16[1088,128]{1,0:T(8,128)(2,1)S(1)}, u32[]{:S(2)}, u32[]{:S(2)}) collective-permute-start(bf16[1088,128]{1,0:T(8,128)(2,1)S(1)} %pack_weights.1), channel_id=1, source_target_pairs={{0,2},{1,3},{2,0},{3,1},{4,6},{5,7},{6,4},{7,5},{8,10},{9,11},{10,... | collective-permute-start | bytes 835592 | tf_op jit(solution)/shard_map/ppermute | solution.py:321
  15.7 10.6 %collective-permute-start.1 = (bf16[2,4,64,256]{3,2,1,0:T(8,128)(2,1)S(1)}, bf16[2,4,64,256]{3,2,1,0:T(8,128)(2,1)S(1)}, u32[]{:S(2)}, u32[]{:S(2)}) collective-permute-start(bf16[2,4,64,256]{3,2,1,0:T(8,128)(2,1)S(1)} %get-tuple-element.44), channel_id=1, source_target_pairs={{0,120},{8,16},{16,8},{24,32},{32,24},{40,48},{48,40},{56,64},{64,... | collective-permute-start | bytes 786440 | tf_op jit(solution)/shard_map/ppermute | solution.py:315
  20.9 11.8 %all-to-all-start.1 = ((bf16[8,2,2,32,128]{4,3,2,1,0:T(8,128)(2,1)}), bf16[8,2,2,32,128]{4,3,2,1,0:T(8,128)(2,1)S(1)}, u32[]{:S(2)}, u32[]{:S(2)}) async-start(bf16[8,2,2,32,128]{4,3,2,1,0:T(8,128)(2,1)} %bitcast.4), calls=%async_computation.1 | async-start | bytes 524288 | tf_op jit(solution)/shard_map/all_to_all | solution.py:322
  26.3 0.7 copy-start.2
  32.9 2.8 %collective-permute-start.5 = (bf16[4,1088,128]{2,1,0:T(8,128)(2,1)S(1)}, bf16[4,1088,128]{2,1,0:T(8,128)(2,1)S(1)}, u32[]{:S(2)}, u32[]{:S(2)}) collective-permute-start(bf16[4,1088,128]{2,1,0:T(8,128)(2,1)S(1)} %pad_maximum_fusion.packed.weight), channel_id=1, source_target_pairs={{0,1},{1,0},{2,3},{3,2},{4,5},{5,4},{6,7},{7,6},{8,9},{9,8},{10,11... | collective-permute-start | bytes 3342344 | tf_op jit(solution)/shard_map/ppermute | solution.py:324
  35.7 1.0 copy-start.3
  40.7 8.9 %collective-permute-start.7 = (bf16[2,2,128,128]{3,2,1,0:T(8,128)(2,1)S(1)}, bf16[2,2,128,128]{3,2,1,0:T(8,128)(2,1)S(1)}, u32[]{:S(2)}, u32[]{:S(2)}) collective-permute-start(bf16[2,2,128,128]{3,2,1,0:T(8,128)(2,1)S(1)} %get-tuple-element.31.own), channel_id=1, source_target_pairs={{0,120},{8,16},{16,8},{24,32},{32,24},{40,48},{48,40},{56,64},{64,... | collective-permute-start | bytes 393224 | tf_op jit(solution)/shard_map/ppermute | solution.py:338
  45.2 5.3 %collective-permute-start.6 = (bf16[2,2,128,128]{3,2,1,0:T(8,128)(2,1)S(1)}, bf16[2,2,128,128]{3,2,1,0:T(8,128)(2,1)S(1)}, u32[]{:S(2)}, u32[]{:S(2)}) collective-permute-start(bf16[2,2,128,128]{3,2,1,0:T(8,128)(2,1)S(1)} %get-tuple-element.31.own), channel_id=1, source_target_pairs={{0,8},{8,0},{16,24},{24,16},{32,40},{40,32},{48,56},{56,48},{64,72... | collective-permute-start | bytes 393224 | tf_op jit(solution)/shard_map/ppermute | solution.py:337
  55.0 6.0 %collective-permute-start.10 = (bf16[4,27,32,128]{3,2,1,0:T(8,128)(2,1)S(1)}, bf16[4,27,32,128]{3,2,1,0:T(8,128)(2,1)S(1)}, u32[]{:S(2)}, u32[]{:S(2)}) collective-permute-start(bf16[4,27,32,128]{3,2,1,0:T(8,128)(2,1)S(1)} %get-tuple-element.39), channel_id=1, source_target_pairs={{0,1},{1,0},{2,3},{3,2},{4,5},{5,4},{6,7},{7,6},{8,9},{9,8},{10,11... | collective-permute-start | bytes 2654216 | tf_op jit(solution)/shard_map/ppermute | solution.py:363
  55.1 5.9 %collective-permute-start.8 = (bf16[2,128,256]{2,1,0:T(8,128)(2,1)S(1)}, bf16[2,128,256]{2,1,0:T(8,128)(2,1)S(1)}, u32[]{:S(2)}, u32[]{:S(2)}) collective-permute-start(bf16[2,128,256]{2,1,0:T(8,128)(2,1)S(1)} %get-tuple-element.33), channel_id=1, source_target_pairs={{0,8},{8,0},{16,24},{24,16},{32,40},{40,32},{48,56},{56,48},{64,72... | collective-permute-start | bytes 393224 | tf_op jit(solution)/shard_map/ppermute | solution.py:353
  55.4 10.5 %collective-permute-start.9 = (bf16[2,128,256]{2,1,0:T(8,128)(2,1)S(1)}, bf16[2,128,256]{2,1,0:T(8,128)(2,1)S(1)}, u32[]{:S(2)}, u32[]{:S(2)}) collective-permute-start(bf16[2,128,256]{2,1,0:T(8,128)(2,1)S(1)} %get-tuple-element.38), channel_id=1, source_target_pairs={{0,120},{8,16},{16,8},{24,32},{32,24},{40,48},{48,40},{56,64},{64,... | collective-permute-start | bytes 393224 | tf_op jit(solution)/shard_map/ppermute | solution.py:354
  61.2 12.2 %collective-permute-start.11 = (bf16[27,32,128]{2,1,0:T(8,128)(2,1)S(1)}, bf16[27,32,128]{2,1,0:T(8,128)(2,1)S(1)}, u32[]{:S(2)}, u32[]{:S(2)}) collective-permute-start(bf16[27,32,128]{2,1,0:T(8,128)(2,1)S(1)} %get-tuple-element.41), channel_id=1, source_target_pairs={{0,2},{1,3},{2,0},{3,1},{4,6},{5,7},{6,4},{7,5},{8,10},{9,11},{10,... | collective-permute-start | bytes 663560 | tf_op jit(solution)/shard_map/ppermute | solution.py:368
  61.5 11.9 %collective-permute-start.12 = (bf16[27,32,128]{2,1,0:T(8,128)(2,1)S(1)}, bf16[27,32,128]{2,1,0:T(8,128)(2,1)S(1)}, u32[]{:S(2)}, u32[]{:S(2)}) collective-permute-start(bf16[27,32,128]{2,1,0:T(8,128)(2,1)S(1)} %get-tuple-element.42), channel_id=1, source_target_pairs={{0,4},{1,5},{2,6},{3,7},{4,0},{5,1},{6,2},{7,3},{8,12},{9,13},{10,... | collective-permute-start | bytes 663560 | tf_op jit(solution)/shard_map/ppermute | solution.py:368
  63.2 12.4 %collective-permute-start.13 = (bf16[27,32,128]{2,1,0:T(8,128)(2,1)S(1)}, bf16[27,32,128]{2,1,0:T(8,128)(2,1)S(1)}, u32[]{:S(2)}, u32[]{:S(2)}) collective-permute-start(bf16[27,32,128]{2,1,0:T(8,128)(2,1)S(1)} %get-tuple-element.43), channel_id=1, source_target_pairs={{0,6},{1,7},{2,4},{3,5},{4,2},{5,3},{6,0},{7,1},{8,14},{9,15},{10,... | collective-permute-start | bytes 663560 | tf_op jit(solution)/shard_map/ppermute | solution.py:368
  69.9 13.4 %all-to-all-start.2 = ((bf16[8,3,16,576]{3,2,1,0:T(8,128)(2,1)}), bf16[8,3,16,576]{3,2,1,0:T(8,128)(2,1)S(1)}, u32[]{:S(2)}, u32[]{:S(2)}) async-start(bf16[8,3,16,576]{3,2,1,0:T(8,128)(2,1)} %first_weights.1), calls=%async_computation.2 | async-start | bytes 983040 | tf_op jit(solution)/shard_map/all_to_all | solution.py:377

commit v4 on v3

--- a/solution.py
+++ b/solution.py
@@ -64,6 +64,21 @@
     tiles = [stacked(a * 64 + j * 16) for j in range(4)]
     tiles.append(stacked(208 if a == 2 else 192)[:, 64 * (a % 2) : 64 * (a % 2) + 64])
     return jnp.concatenate(tiles, axis=1)
+
+
+def deal_cot(place, cot, *outs):
+    for d, out in enumerate(outs):
+        here = (place[1] >> 1) ^ d
+        for j in range(4):
+            out[j] = cot[4 * here + j]
+
+
+def sort_cot(place, p0, p1, p2, p3, mine, across):
+    core = place[1] & 1
+    for d, piece in enumerate((p0, p1, p2, p3)):
+        for j in range(2):
+            mine[d, j] = piece[2 * core + j]
+            across[d, j] = piece[2 - 2 * core + j]
 
 
 def low_and_high(place, one, two):
@@ -107,14 +122,10 @@
             pooled[s, pair] = ((total[:, :128] + total[:, 128:]) * 0.125).astype(BF)
 
 
-def other_blocks(place):
-    filt = place[1]
-    return [filt ^ (2 * d + c) for c in range(2) for d in range(4)]
-
-
-def second_layer(place, own, one, two, weight, across, cot, grads, taps, mid, first, second, spread):
+def second_layer(
+    place, own, one, two, weight, across, cot, cot_across, grads, taps, mid, first, second, spread
+):
     even = place[0] == 0
-    blocks = other_blocks(place)
 
     def rows(k):
         here = slice(224 + 32 * k, 256 + 32 * k)
@@ -142,7 +153,10 @@
             part = dot(w, taps[a].reshape(768, 256))
             pre = part if pre is None else pre + part
         _, rate = gelu_and_slope(pre)
-        pair = [jnp.concatenate([cot[f, j, y] for f in blocks], axis=0) for j in range(2)]
+        pair = [
+            jnp.concatenate([c[d, j, y] for c in (cot, cot_across) for d in range(4)], axis=0)
+            for j in range(2)
+        ]
         grad = (jnp.concatenate(pair, axis=1).astype(F32) * rate).astype(BF)
         grads[y] = grad
         spread[y, 0] = dot(grad, right).astype(BF)
@@ -311,21 +325,25 @@
         cells = lax.dynamic_slice(volume, (2 * filt, depth, zero, zero, zero), (2, 1, 4, 64, 256))
         return cells[:, 0]
 
-    one = lax.ppermute(face(1 - parity), "space", ones)
-    two = lax.ppermute(face(parity), "space", twos)
-    own = lax.dynamic_slice_in_dim(volume, 2 * filt, 2, axis=0)
+    outer, inner = face(1 - parity), face(parity)
+    one = lax.ppermute(outer, "space", ones)
+    two = lax.ppermute(inner, "space", twos)
     by_sample = lax.all_to_all(cotangent[0], "space", 0, 0, tiled=True)
     (piece,) = call(
-        pack_weights, (after(weight_first, one), weight_second), (((1088, 128), BF),), [], 0, "pack_weights"
+        pack_weights, (after(weight_first, outer, inner), weight_second), (((1088, 128), BF),), [], 0, "pack_weights"
     )
     others = [lax.ppermute(piece, "filt", by_x[d]) for d in range(1, 4)]
-    cot = lax.all_to_all(by_sample.reshape(nf, 2, 2, 32, 128), "filt", 0, 0, tiled=True)
-    weights = jnp.stack([after(w, own, two, cot) for w in [piece] + others])
+    own = lax.dynamic_slice_in_dim(after(volume, by_sample), 2 * filt, 2, axis=0)
+    weights = jnp.stack([after(w, by_sample, one, two) for w in [piece] + others])
     across = lax.ppermute(weights, "filt", by_core)
+
+    part = ((4, 2, 32, 128), BF)
+    pieces = call(deal_cot, (place, by_sample), (part,) * 4, [], 0, "deal_cot")
+    pieces = [pieces[0]] + [lax.ppermute(pieces[d], "filt", by_x[d]) for d in range(1, 4)]
 
     taps, slope, pooled = call(
         first_forward,
-        (place, after(own, cot), one, two, weights, across),
+        (place, own, one, two, weights, across),
         (((2, 4, 4, 192, 256), BF), ((2, 2, 4, 128, 256), F32), ((2, 2, 128, 128), BF)),
         [
             pltpu.VMEM((128, 1728), BF),
@@ -336,9 +354,12 @@
     )
     pool_one = lax.ppermute(pooled, "space", ones)
     pool_two = lax.ppermute(pooled, "space", twos)
+    half = ((4, 2, 2, 32, 128), BF)
+    cot, cot_across = call(sort_cot, (place, after(pieces[0], pooled), *pieces[1:]), (half, half), [], 0, "sort_cot")
+    cot_across = lax.ppermute(cot_across, "filt", by_core)
     grads, taps_second, mid, out_one, out_two = call(
         second_layer,
-        (place, pooled, pool_one, pool_two, weights, across, cot),
+        (place, pooled, pool_one, pool_two, weights, across, cot, cot_across),
         (
             ((2, 256, 256), BF),
             ((3, 2, 384, 256), BF),

time: 110 us -> 104 us (0.945)
  starting transfers between devices: 39.9 us -> 28.1 us
  blocking collectives: 25.4 us -> 36 us
  waiting for transfers between devices: 25.6 us -> 21.5 us
  local copies, waits for them, and re-layouts: 3.89 us -> 2.26 us
  Pallas kernels: 13.8 us -> 15 us
    all_to_all x0 -> x1, blocking collectives: none -> 12.4 us  [per_device(): by_sample = lax.all_to_all(cotangent[0], 'space', 0, 0, tiled=True)]
    all_to_all x2 -> x0, starting transfers between devices: 12.1 us -> none  [the longest x1 7.81 us: per_device(): by_sample = lax.all_to_all(cotangent[0], 'space', 0, 0, tiled=True)]
    all_to_all x2 -> x0, waiting for transfers between devices: 5.75 us -> none  [the longest x1 5.74 us: per_device(): lax.all_to_all(by_sample.reshape(nf, 2, 2, 32, 128), 'filt', 0, 0, tiled=...]
    ppermute x2 -> x6, starting transfers between devices: 6.94 us -> 11.4 us  [the longest x1 6.57 us: per_device(): two = lax.ppermute(inner, 'space', twos)]
    ppermute x1, waiting for transfers between devices: 4.43 us -> 7.79 us  [per_device(): pool_two = lax.ppermute(pooled, 'space', twos)]
    ppermute x1, starting transfers between devices: 4.5 us -> 1.44 us  [per_device(): pool_two = lax.ppermute(pooled, 'space', twos)]
    ppermute x1, waiting for transfers between devices: 2.65 us -> 0.01 us  [per_device(): across = lax.ppermute(weights, 'filt', by_core)]
    all_to_all x1, blocking collectives: 13.6 us -> 11.8 us  [per_device(): parts = lax.all_to_all(rows.reshape(ns, 72, 128), 'space', 0, 0, tiled=True)]
  transfers between devices with their start and end apart: 17 -> 19, of which waited for: 7 -> 5; matrix products, arithmetic and copies ran while one was open for 1% -> 1% of each run, Pallas kernels for 4% -> 8%
where the time goes in v4:
time: 104 us
  blocking collectives  36 us (35%)
  starting transfers between devices  28.1 us (27%)
  waiting for transfers between devices  21.5 us (21%)
  Pallas kernels  15 us (14%)
  local copies, waits for them, and re-layouts  2.26 us (2%)
    pallas_call x12, Pallas kernels, call(): pl.pallas_call(kernel, out_shape=shapes, in_specs=[SMEM if x.dtype == jnp...  15 us
    all_to_all x1, blocking collectives, per_device(): by_sample = lax.all_to_all(cotangent[0], 'space', 0, 0, tiled=True)  12.4 us
    all_to_all x1, blocking collectives, per_device(): parts = lax.all_to_all(rows.reshape(ns, 72, 128), 'space', 0, 0, tiled=True)  11.8 us
    all_to_all x1, blocking collectives, per_device(): rows = lax.all_to_all(mine, 'space', 0, 0, tiled=True).reshape(1152, 128)  11.7 us
    ppermute x1, waiting for transfers between devices, per_device(): pool_two = lax.ppermute(pooled, 'space', twos)  7.79 us
    ppermute x1, starting transfers between devices, per_device(): two = lax.ppermute(inner, 'space', twos)  6.57 us
    all_to_all x1, waiting for transfers between devices, per_device(): got_first = lax.all_to_all(terms_first, 'filt', 0, 0, tiled=True)  5.94 us
    ppermute x3, starting transfers between devices, per_device(): lax.ppermute(others[d - 1], 'filt', by_x[d])  4.78 us
  transfers between devices with their start and end apart: 19, of which 5 were waited for; matrix products, arithmetic and copies ran while one was open for 1% of the time, Pallas kernels for 8%

profile of v4, /device:TPU:0, one launch (start us, length us, event | category | flops | bytes accessed | tf_op | source)
XLA Modules:
  0.0 103.9 jit_solution(9195212556494554199)
XLA Ops:
  0.7 1.2 %dynamic-slice_bitcast_fusion = (bf16[2,4,64,256]{3,2,1,0:T(8,128)(2,1)S(1)}, bf16[2,4,64,256]{3,2,1,0:T(8,128)(2,1)S(1)}) fusion(bf16[16,2,4,64,256]{4,3,2,1,0:T(8,128)(2,1)} %param.4, s32[]{:T(128)S(6)} %select_n.19, s32[]{:T(128)S(6)} %select_n.21, s32[]{:T(128)S(6)} %select_n.20), kind=kLoop, calls=%fused_computation.1 | loop fusion | bytes 1048588 | tf_op jit(solution)/shard_map/squeeze | solution.py:326
  1.9 0.1 pack_weights.1
  2.0 2.9 %collective-permute-start.4 = (bf16[1088,128]{1,0:T(8,128)(2,1)S(1)}, bf16[1088,128]{1,0:T(8,128)(2,1)S(1)}, u32[]{:S(2)}, u32[]{:S(2)}) collective-permute-start(bf16[1088,128]{1,0:T(8,128)(2,1)S(1)} %pack_weights.1), channel_id=1, source_target_pairs={{0,6},{1,7},{2,4},{3,5},{4,2},{5,3},{6,0},{7,1},{8,14},{9,15},{10,... | collective-permute-start | bytes 835592 | tf_op jit(solution)/shard_map/ppermute | solution.py:335
  4.9 0.8 collective-permute-start.3
  5.7 0.5 collective-permute-start.2
  6.1 6.6 %collective-permute-start.1 = (bf16[2,4,64,256]{3,2,1,0:T(8,128)(2,1)S(1)}, bf16[2,4,64,256]{3,2,1,0:T(8,128)(2,1)S(1)}, u32[]{:S(2)}, u32[]{:S(2)}) collective-permute-start(bf16[2,4,64,256]{3,2,1,0:T(8,128)(2,1)S(1)} %get-tuple-element.58), channel_id=1, source_target_pairs={{0,120},{8,16},{16,8},{24,32},{32,24},{40,48},{48,40},{56,64},{64,... | collective-permute-start | bytes 786440 | tf_op jit(solution)/shard_map/ppermute | solution.py:330
  12.7 12.4 %all_to_all.20.cot = bf16[16,2,32,128]{3,2,1,0:T(8,128)(2,1)S(1)} all-to-all(bf16[16,2,32,128]{3,2,1,0:T(8,128)(2,1)S(1)} %bitcast.20), channel_id=1, replica_groups=mesh['space'=16,'filt'=8] {'space'}, dimensions={0} | all-to-all | bytes 524288 | tf_op jit(solution)/shard_map/all_to_all | solution.py:331
  25.2 0.0 collective-permute-done.3
  25.2 0.1 pad_maximum_fusion.packed.weight
  25.3 0.1 collective-permute-start.5
  25.4 0.1 pad_add_fusion.place
  25.5 0.6 deal_cot.1
  26.1 1.6 %collective-permute-start.8 = (bf16[4,2,32,128]{3,2,1,0:T(8,128)(2,1)S(1)}, bf16[4,2,32,128]{3,2,1,0:T(8,128)(2,1)S(1)}, u32[]{:S(2)}, u32[]{:S(2)}) collective-permute-start(bf16[4,2,32,128]{3,2,1,0:T(8,128)(2,1)S(1)} %get-tuple-element.41), channel_id=1, source_target_pairs={{0,2},{1,3},{2,0},{3,1},{4,6},{5,7},{6,4},{7,5},{8,10},{9,11},{10,... | collective-permute-start | bytes 196616 | tf_op jit(solution)/shard_map/ppermute | solution.py:342
  27.7 2.7 %collective-permute-start.9 = (bf16[4,2,32,128]{3,2,1,0:T(8,128)(2,1)S(1)}, bf16[4,2,32,128]{3,2,1,0:T(8,128)(2,1)S(1)}, u32[]{:S(2)}, u32[]{:S(2)}) collective-permute-start(bf16[4,2,32,128]{3,2,1,0:T(8,128)(2,1)S(1)} %get-tuple-element.42), channel_id=1, source_target_pairs={{0,4},{1,5},{2,6},{3,7},{4,0},{5,1},{6,2},{7,3},{8,12},{9,13},{10,... | collective-permute-start | bytes 196616 | tf_op jit(solution)/shard_map/ppermute | solution.py:342
  30.4 0.5 collective-permute-start.10
  30.9 1.1 %constant_dynamic-slice_fusion.own = bf16[2,2,4,64,256]{4,3,2,1,0:T(8,128)(2,1)S(1)} fusion(bf16[16,2,4,64,256]{4,3,2,1,0:T(8,128)(2,1)} %param.4, s32[]{:T(128)S(6)} %select_n.19), kind=kLoop, calls=%fused_computation.3 | loop fusion | bytes 1048580 | tf_op jit(solution)/shard_map/dynamic_slice | solution.py:336
  32.0 0.0 collective-permute-done.5.across
  32.0 4.1 %first_forward.1 = (bf16[2,4,4,192,256]{4,3,2,1,0:T(8,128)(2,1)S(1)}, f32[2,2,4,128,256]{4,3,2,1,0:T(8,128)S(1)}, bf16[2,2,128,128]{3,2,1,0:T(8,128)(2,1)S(1)}) custom-call(s32[3]{0:T(128)S(1)} %pad_add_fusion.place, bf16[2,2,4,64,256]{4,3,2,1,0:T(8,128)(2,1)S(1)} %constant_dynamic-slice_fusion.own, bf16[2,4,64,256]{3,2,1,0:T(8,128)(2,1)S(1)} %collective-permute-done.one, ...), custom_call_target="tpu_custom_call" | custom-call | flops 20000000000 | bytes 8650764 | tf_op jit(solution)/shard_map/first_forward/pallas_call | solution.py:289
  36.0 0.0 collective-permute-done.8.p1
  36.0 0.0 collective-permute-done.9.p2
  36.1 0.6 sort_cot.1
  36.6 0.1 collective-permute-start.11
  36.7 1.4 %collective-permute-start.7 = (bf16[2,2,128,128]{3,2,1,0:T(8,128)(2,1)S(1)}, bf16[2,2,128,128]{3,2,1,0:T(8,128)(2,1)S(1)}, u32[]{:S(2)}, u32[]{:S(2)}) collective-permute-start(bf16[2,2,128,128]{3,2,1,0:T(8,128)(2,1)S(1)} %get-tuple-element.38.own), channel_id=1, source_target_pairs={{0,120},{8,16},{16,8},{24,32},{32,24},{40,48},{48,40},{56,64},{64,... | collective-permute-start | bytes 393224 | tf_op jit(solution)/shard_map/ppermute | solution.py:356
  38.2 0.0 collective-permute-start.6
  38.2 0.0 collective-permute-done.11.cot_across
  38.2 7.8 %collective-permute-done.7.two = bf16[2,2,128,128]{3,2,1,0:T(8,128)(2,1)S(1)} collective-permute-done((bf16[2,2,128,128]{3,2,1,0:T(8,128)(2,1)S(1)}, bf16[2,2,128,128]{3,2,1,0:T(8,128)(2,1)S(1)}, u32[]{:S(2)}, u32[]{:S(2)}) %collective-permute-start.7) | collective-permute-done | bytes 131104 | tf_op jit(solution)/shard_map/ppermute | solution.py:356
  46.0 3.5 %second_layer.1 = (bf16[2,256,256]{2,1,0:T(8,128)(2,1)S(1)}, bf16[3,2,384,256]{3,2,1,0:T(8,128)(2,1)S(1)}, f32[2,128,256]{2,1,0:T(8,128)S(1)}, bf16[2,128,256]{2,1,0:T(8,128)(2,1)S(1)}, bf16[2,128,256]{2,1,0:T(8,128)(2,1)S(1)}) custom-call(s32[3]{0:T(128)S(1)} %pad_add_fusion.place, bf16[2,2,128,128]{3,2,1,0:T(8,128)(2,1)S(1)} %get-tuple-element.38.own, ...), custom_call_target="tpu_custom_call" | custom-call | flops 2000000000 | bytes 4849676 | tf_op jit(solution)/shard_map/second_layer/pallas_call | solution.py:289
  49.5 1.0 second_weights.1
  50.5 0.1 collective-permute-start.14
  50.6 0.1 collective-permute-start.12
  50.7 2.0 %collective-permute-start.13 = (bf16[2,128,256]{2,1,0:T(8,128)(2,1)S(1)}, bf16[2,128,256]{2,1,0:T(8,128)(2,1)S(1)}, u32[]{:S(2)}, u32[]{:S(2)}) collective-permute-start(bf16[2,128,256]{2,1,0:T(8,128)(2,1)S(1)} %get-tuple-element.52), channel_id=1, source_target_pairs={{0,120},{8,16},{16,8},{24,32},{32,24},{40,48},{48,40},{56,64},{64,... | collective-permute-start | bytes 393224 | tf_op jit(solution)/shard_map/ppermute | solution.py:375
  52.7 3.8 %collective-permute-done.12.one = bf16[2,128,256]{2,1,0:T(8,128)(2,1)S(1)} collective-permute-done((bf16[2,128,256]{2,1,0:T(8,128)(2,1)S(1)}, bf16[2,128,256]{2,1,0:T(8,128)(2,1)S(1)}, u32[]{:S(2)}, u32[]{:S(2)}) %collective-permute-start.12) | collective-permute-done | bytes 131104 | tf_op jit(solution)/shard_map/ppermute | solution.py:374
  56.5 0.0 collective-permute-done.14.across
  56.5 0.2 add_cores.1
  56.7 0.4 collective-permute-start.15
  57.1 3.9 %collective-permute-start.16 = (bf16[27,32,128]{2,1,0:T(8,128)(2,1)S(1)}, bf16[27,32,128]{2,1,0:T(8,128)(2,1)S(1)}, u32[]{:S(2)}, u32[]{:S(2)}) collective-permute-start(bf16[27,32,128]{2,1,0:T(8,128)(2,1)S(1)} %get-tuple-element.56), channel_id=1, source_target_pairs={{0,4},{1,5},{2,6},{3,7},{4,0},{5,1},{6,2},{7,3},{8,12},{9,13},{10,... | collective-permute-start | bytes 663560 | tf_op jit(solution)/shard_map/ppermute | solution.py:389
  61.0 0.5 collective-permute-start.17
  61.5 3.9 %first_weights.1 = bf16[8,3,16,576]{3,2,1,0:T(8,128)(2,1)} custom-call(s32[3]{0:T(128)S(1)} %pad_add_fusion.place, bf16[2,4,4,192,256]{4,3,2,1,0:T(8,128)(2,1)S(1)} %get-tuple-element.36.taps, f32[2,2,4,128,256]{4,3,2,1,0:T(8,128)S(1)} %get-tuple-element.37.slope, f32[2,128,256]{2,1,0:T(8,128)S(1)} %get-tuple-element.46.mid, ...), custom_call_target="tpu_custom_call" | custom-call | flops 20000000000 | bytes 6209548 | tf_op jit(solution)/shard_map/first_weights/pallas_call | solution.py:289
  65.4 4.0 %all-to-all-start.1 = ((bf16[8,3,16,576]{3,2,1,0:T(8,128)(2,1)}), bf16[8,3,16,576]{3,2,1,0:T(8,128)(2,1)S(1)}, u32[]{:S(2)}, u32[]{:S(2)}) async-start(bf16[8,3,16,576]{3,2,1,0:T(8,128)(2,1)} %first_weights.1), calls=%async_computation.1 | async-start | bytes 983040 | tf_op jit(solution)/shard_map/all_to_all | solution.py:398
  69.4 1.4 %collective-permute-done.16.two = bf16[27,32,128]{2,1,0:T(8,128)(2,1)S(1)} collective-permute-done((bf16[27,32,128]{2,1,0:T(8,128)(2,1)S(1)}, bf16[27,32,128]{2,1,0:T(8,128)(2,1)S(1)}, u32[]{:S(2)}, u32[]{:S(2)}) %collective-permute-start.16) | collective-permute-done | bytes 221216 | tf_op jit(solution)/shard_map/ppermute | solution.py:389
  70.8 2.6 %collective-permute-done.17.three = bf16[27,32,128]{2,1,0:T(8,128)(2,1)S(1)} collective-permute-done((bf16[27,32,128]{2,1,0:T(8,128)(2,1)S(1)}, bf16[27,32,128]{2,1,0:T(8,128)(2,1)S(1)}, u32[]{:S(2)}, u32[]{:S(2)}) %collective-permute-start.17) | collective-permute-done | bytes 221216 | tf_op jit(solution)/shard_map/ppermute | solution.py:389
  73.4 0.1 add_across.1.second
  73.5 5.9 %all-to-all-done.1.first = bf16[8,3,16,576]{3,2,1,0:T(8,128)(2,1)S(1)} async-done(((bf16[8,3,16,576]{3,2,1,0:T(8,128)(2,1)}), bf16[8,3,16,576]{3,2,1,0:T(8,128)(2,1)S(1)}, u32[]{:S(2)}, u32[]{:S(2)}) %all-to-all-start.1) | async-done | bytes 442400 | tf_op jit(solution)/shard_map/all_to_all | solution.py:398
  79.4 0.1 pack.1
  79.5 11.8 %all_to_all.21.parts = bf16[16,72,128]{2,1,0:T(8,128)(2,1)S(1)} all-to-all(bf16[16,72,128]{2,1,0:T(8,128)(2,1)S(1)} %bitcast.15), channel_id=1, replica_groups=mesh['space'=16,'filt'=8] {'space'}, dimensions={0} | all-to-all | bytes 589824 | tf_op jit(solution)/shard_map/all_to_all | solution.py:404
  91.3 0.1 add_up.1
  91.3 11.7 %all_to_all.22 = bf16[16,72,128]{2,1,0:T(8,128)(2,1)S(1)} all-to-all(bf16[16,72,128]{2,1,0:T(8,128)(2,1)S(1)} %add_up.1), channel_id=1, replica_groups=mesh['space'=16,'filt'=8] {'space'}, dimensions={0} | all-to-all | bytes 589824 | tf_op jit(solution)/shard_map/all_to_all | solution.py:406
  103.1 0.9 unpack.1
  (15 shorter events, 0.0 us)
Async XLA Ops:
  0.6 1.2 %copy-start.1 = (bf16[27,16,64]{2,1,0:T(8,128)(2,1)S(1)}, bf16[27,16,64]{2,1,0:T(8,128)(2,1)}, u32[]{:S(2)}) copy-start(bf16[27,16,64]{2,1,0:T(8,128)(2,1)} %weight) | copy-start | bytes 165892
  0.6 1.2 %copy-start = (bf16[27,32,128]{2,1,0:T(8,128)(2,1)S(1)}, bf16[27,32,128]{2,1,0:T(8,128)(2,1)}, u32[]{:S(2)}) copy-start(bf16[27,32,128]{2,1,0:T(8,128)(2,1)} %second.1) | copy-start | bytes 663556
  0.7 12.1 %copy-start.2 = (bf16[1,16,2,32,128]{4,3,2,1,0:T(8,128)(2,1)S(1)}, bf16[1,16,2,32,128]{4,3,2,1,0:T(8,128)(2,1)}, u32[]{:S(2)}) copy-start(bf16[1,16,2,32,128]{4,3,2,1,0:T(8,128)(2,1)} %param.7) | copy-start | bytes 786436
  2.0 23.2 %collective-permute-start.4 = (bf16[1088,128]{1,0:T(8,128)(2,1)S(1)}, bf16[1088,128]{1,0:T(8,128)(2,1)S(1)}, u32[]{:S(2)}, u32[]{:S(2)}) collective-permute-start(bf16[1088,128]{1,0:T(8,128)(2,1)S(1)} %pack_weights.1), channel_id=1, source_target_pairs={{0,6},{1,7},{2,4},{3,5},{4,2},{5,3},{6,0},{7,1},{8,14},{9,15},{10,... | collective-permute-start | bytes 835592 | tf_op jit(solution)/shard_map/ppermute | solution.py:335
  4.9 20.3 %collective-permute-start.3 = (bf16[1088,128]{1,0:T(8,128)(2,1)S(1)}, bf16[1088,128]{1,0:T(8,128)(2,1)S(1)}, u32[]{:S(2)}, u32[]{:S(2)}) collective-permute-start(bf16[1088,128]{1,0:T(8,128)(2,1)S(1)} %pack_weights.1), channel_id=1, source_target_pairs={{0,4},{1,5},{2,6},{3,7},{4,0},{5,1},{6,2},{7,3},{8,12},{9,13},{10,... | collective-permute-start | bytes 835592 | tf_op jit(solution)/shard_map/ppermute | solution.py:335
  5.7 19.5 %collective-permute-start.2 = (bf16[1088,128]{1,0:T(8,128)(2,1)S(1)}, bf16[1088,128]{1,0:T(8,128)(2,1)S(1)}, u32[]{:S(2)}, u32[]{:S(2)}) collective-permute-start(bf16[1088,128]{1,0:T(8,128)(2,1)S(1)} %pack_weights.1), channel_id=1, source_target_pairs={{0,2},{1,3},{2,0},{3,1},{4,6},{5,7},{6,4},{7,5},{8,10},{9,11},{10,... | collective-permute-start | bytes 835592 | tf_op jit(solution)/shard_map/ppermute | solution.py:335
  6.1 19.0 %collective-permute-start.1 = (bf16[2,4,64,256]{3,2,1,0:T(8,128)(2,1)S(1)}, bf16[2,4,64,256]{3,2,1,0:T(8,128)(2,1)S(1)}, u32[]{:S(2)}, u32[]{:S(2)}) collective-permute-start(bf16[2,4,64,256]{3,2,1,0:T(8,128)(2,1)S(1)} %get-tuple-element.58), channel_id=1, source_target_pairs={{0,120},{8,16},{16,8},{24,32},{32,24},{40,48},{48,40},{56,64},{64,... | collective-permute-start | bytes 786440 | tf_op jit(solution)/shard_map/ppermute | solution.py:330
  12.7 12.5 %collective-permute-start = (bf16[2,4,64,256]{3,2,1,0:T(8,128)(2,1)S(1)}, bf16[2,4,64,256]{3,2,1,0:T(8,128)(2,1)S(1)}, u32[]{:S(2)}, u32[]{:S(2)}) collective-permute-start(bf16[2,4,64,256]{3,2,1,0:T(8,128)(2,1)S(1)} %get-tuple-element.59), channel_id=1, source_target_pairs={{0,8},{8,0},{16,24},{24,16},{32,40},{40,32},{48,56},{56,48},{64,72... | collective-permute-start | bytes 786440 | tf_op jit(solution)/shard_map/ppermute | solution.py:329
  25.3 6.6 %collective-permute-start.5 = (bf16[4,1088,128]{2,1,0:T(8,128)(2,1)S(1)}, bf16[4,1088,128]{2,1,0:T(8,128)(2,1)S(1)}, u32[]{:S(2)}, u32[]{:S(2)}) collective-permute-start(bf16[4,1088,128]{2,1,0:T(8,128)(2,1)S(1)} %pad_maximum_fusion.packed.weight), channel_id=1, source_target_pairs={{0,1},{1,0},{2,3},{3,2},{4,5},{5,4},{6,7},{7,6},{8,9},{9,8},{10,11... | collective-permute-start | bytes 3342344 | tf_op jit(solution)/shard_map/ppermute | solution.py:338
  26.1 9.9 %collective-permute-start.8 = (bf16[4,2,32,128]{3,2,1,0:T(8,128)(2,1)S(1)}, bf16[4,2,32,128]{3,2,1,0:T(8,128)(2,1)S(1)}, u32[]{:S(2)}, u32[]{:S(2)}) collective-permute-start(bf16[4,2,32,128]{3,2,1,0:T(8,128)(2,1)S(1)} %get-tuple-element.41), channel_id=1, source_target_pairs={{0,2},{1,3},{2,0},{3,1},{4,6},{5,7},{6,4},{7,5},{8,10},{9,11},{10,... | collective-permute-start | bytes 196616 | tf_op jit(solution)/shard_map/ppermute | solution.py:342
  27.7 8.4 %collective-permute-start.9 = (bf16[4,2,32,128]{3,2,1,0:T(8,128)(2,1)S(1)}, bf16[4,2,32,128]{3,2,1,0:T(8,128)(2,1)S(1)}, u32[]{:S(2)}, u32[]{:S(2)}) collective-permute-start(bf16[4,2,32,128]{3,2,1,0:T(8,128)(2,1)S(1)} %get-tuple-element.42), channel_id=1, source_target_pairs={{0,4},{1,5},{2,6},{3,7},{4,0},{5,1},{6,2},{7,3},{8,12},{9,13},{10,... | collective-permute-start | bytes 196616 | tf_op jit(solution)/shard_map/ppermute | solution.py:342
  30.4 5.7 %collective-permute-start.10 = (bf16[4,2,32,128]{3,2,1,0:T(8,128)(2,1)S(1)}, bf16[4,2,32,128]{3,2,1,0:T(8,128)(2,1)S(1)}, u32[]{:S(2)}, u32[]{:S(2)}) collective-permute-start(bf16[4,2,32,128]{3,2,1,0:T(8,128)(2,1)S(1)} %get-tuple-element.43), channel_id=1, source_target_pairs={{0,6},{1,7},{2,4},{3,5},{4,2},{5,3},{6,0},{7,1},{8,14},{9,15},{10,... | collective-permute-start | bytes 196616 | tf_op jit(solution)/shard_map/ppermute | solution.py:342
  36.6 1.5 %collective-permute-start.11 = (bf16[4,2,2,32,128]{4,3,2,1,0:T(8,128)(2,1)S(1)}, bf16[4,2,2,32,128]{4,3,2,1,0:T(8,128)(2,1)S(1)}, u32[]{:S(2)}, u32[]{:S(2)}) collective-permute-start(bf16[4,2,2,32,128]{4,3,2,1,0:T(8,128)(2,1)S(1)} %get-tuple-element.45), channel_id=1, source_target_pairs={{0,1},{1,0},{2,3},{3,2},{4,5},{5,4},{6,7},{7,6},{8,9},{9,8},{10,11... | collective-permute-start | bytes 393224 | tf_op jit(solution)/shard_map/ppermute | solution.py:359
  36.7 9.2 %collective-permute-start.7 = (bf16[2,2,128,128]{3,2,1,0:T(8,128)(2,1)S(1)}, bf16[2,2,128,128]{3,2,1,0:T(8,128)(2,1)S(1)}, u32[]{:S(2)}, u32[]{:S(2)}) collective-permute-start(bf16[2,2,128,128]{3,2,1,0:T(8,128)(2,1)S(1)} %get-tuple-element.38.own), channel_id=1, source_target_pairs={{0,120},{8,16},{16,8},{24,32},{32,24},{40,48},{48,40},{56,64},{64,... | collective-permute-start | bytes 393224 | tf_op jit(solution)/shard_map/ppermute | solution.py:356
  38.2 7.8 %collective-permute-start.6 = (bf16[2,2,128,128]{3,2,1,0:T(8,128)(2,1)S(1)}, bf16[2,2,128,128]{3,2,1,0:T(8,128)(2,1)S(1)}, u32[]{:S(2)}, u32[]{:S(2)}) collective-permute-start(bf16[2,2,128,128]{3,2,1,0:T(8,128)(2,1)S(1)} %get-tuple-element.38.own), channel_id=1, source_target_pairs={{0,8},{8,0},{16,24},{24,16},{32,40},{40,32},{48,56},{56,48},{64,72... | collective-permute-start | bytes 393224 | tf_op jit(solution)/shard_map/ppermute | solution.py:355
  50.5 6.0 %collective-permute-start.14 = (bf16[4,27,32,128]{3,2,1,0:T(8,128)(2,1)S(1)}, bf16[4,27,32,128]{3,2,1,0:T(8,128)(2,1)S(1)}, u32[]{:S(2)}, u32[]{:S(2)}) collective-permute-start(bf16[4,27,32,128]{3,2,1,0:T(8,128)(2,1)S(1)} %get-tuple-element.53), channel_id=1, source_target_pairs={{0,1},{1,0},{2,3},{3,2},{4,5},{5,4},{6,7},{7,6},{8,9},{9,8},{10,11... | collective-permute-start | bytes 2654216 | tf_op jit(solution)/shard_map/ppermute | solution.py:384
  50.6 5.9 %collective-permute-start.12 = (bf16[2,128,256]{2,1,0:T(8,128)(2,1)S(1)}, bf16[2,128,256]{2,1,0:T(8,128)(2,1)S(1)}, u32[]{:S(2)}, u32[]{:S(2)}) collective-permute-start(bf16[2,128,256]{2,1,0:T(8,128)(2,1)S(1)} %get-tuple-element.47), channel_id=1, source_target_pairs={{0,8},{8,0},{16,24},{24,16},{32,40},{40,32},{48,56},{56,48},{64,72... | collective-permute-start | bytes 393224 | tf_op jit(solution)/shard_map/ppermute | solution.py:374
  50.7 10.8 %collective-permute-start.13 = (bf16[2,128,256]{2,1,0:T(8,128)(2,1)S(1)}, bf16[2,128,256]{2,1,0:T(8,128)(2,1)S(1)}, u32[]{:S(2)}, u32[]{:S(2)}) collective-permute-start(bf16[2,128,256]{2,1,0:T(8,128)(2,1)S(1)} %get-tuple-element.52), channel_id=1, source_target_pairs={{0,120},{8,16},{16,8},{24,32},{32,24},{40,48},{48,40},{56,64},{64,... | collective-permute-start | bytes 393224 | tf_op jit(solution)/shard_map/ppermute | solution.py:375
  56.7 12.7 %collective-permute-start.15 = (bf16[27,32,128]{2,1,0:T(8,128)(2,1)S(1)}, bf16[27,32,128]{2,1,0:T(8,128)(2,1)S(1)}, u32[]{:S(2)}, u32[]{:S(2)}) collective-permute-start(bf16[27,32,128]{2,1,0:T(8,128)(2,1)S(1)} %get-tuple-element.55), channel_id=1, source_target_pairs={{0,2},{1,3},{2,0},{3,1},{4,6},{5,7},{6,4},{7,5},{8,10},{9,11},{10,... | collective-permute-start | bytes 663560 | tf_op jit(solution)/shard_map/ppermute | solution.py:389
  57.1 13.7 %collective-permute-start.16 = (bf16[27,32,128]{2,1,0:T(8,128)(2,1)S(1)}, bf16[27,32,128]{2,1,0:T(8,128)(2,1)S(1)}, u32[]{:S(2)}, u32[]{:S(2)}) collective-permute-start(bf16[27,32,128]{2,1,0:T(8,128)(2,1)S(1)} %get-tuple-element.56), channel_id=1, source_target_pairs={{0,4},{1,5},{2,6},{3,7},{4,0},{5,1},{6,2},{7,3},{8,12},{9,13},{10,... | collective-permute-start | bytes 663560 | tf_op jit(solution)/shard_map/ppermute | solution.py:389
  61.0 12.4 %collective-permute-start.17 = (bf16[27,32,128]{2,1,0:T(8,128)(2,1)S(1)}, bf16[27,32,128]{2,1,0:T(8,128)(2,1)S(1)}, u32[]{:S(2)}, u32[]{:S(2)}) collective-permute-start(bf16[27,32,128]{2,1,0:T(8,128)(2,1)S(1)} %get-tuple-element.57), channel_id=1, source_target_pairs={{0,6},{1,7},{2,4},{3,5},{4,2},{5,3},{6,0},{7,1},{8,14},{9,15},{10,... | collective-permute-start | bytes 663560 | tf_op jit(solution)/shard_map/ppermute | solution.py:389
  65.4 14.0 %all-to-all-start.1 = ((bf16[8,3,16,576]{3,2,1,0:T(8,128)(2,1)}), bf16[8,3,16,576]{3,2,1,0:T(8,128)(2,1)S(1)}, u32[]{:S(2)}, u32[]{:S(2)}) async-start(bf16[8,3,16,576]{3,2,1,0:T(8,128)(2,1)} %first_weights.1), calls=%async_computation.1 | async-start | bytes 983040 | tf_op jit(solution)/shard_map/all_to_all | solution.py:398

commit v5 on v4

--- a/solution.py
+++ b/solution.py
@@ -122,17 +122,37 @@
             pooled[s, pair] = ((total[:, :128] + total[:, 128:]) * 0.125).astype(BF)
 
 
+def second_rows(weight, across, k):
+    here = slice(224 + 32 * k, 256 + 32 * k)
+    return jnp.concatenate(
+        [weight[:, here].reshape(128, 128), across[:, here].reshape(128, 128)], axis=0
+    )
+
+
+def forward_rows(weight, across, a, y):
+    base = 9 * a + 3 * (1 - y)
+    return jnp.concatenate([second_rows(weight, across, base + j) for j in range(6)], axis=1)
+
+
+def second_start(own, weight, across, taps, begun, turned):
+    left, right = pair_shift(0), pair_shift(2)
+    for y in range(2):
+        cells = jnp.concatenate([own[0, y], own[1, y]], axis=1)
+        taps[y, 0:128] = dot(cells, left).astype(BF)
+        taps[y, 128:256] = cells
+        taps[y, 256:384] = dot(cells, right).astype(BF)
+    for y in range(2):
+        begun[y] = dot(forward_rows(weight, across, 1, y), taps[...].reshape(768, 256))
+    for k in range(27):
+        e = k % 3
+        turned[k // 3, :, e * 256 : (e + 1) * 256] = second_rows(weight, across, k).T
+
+
 def second_layer(
-    place, own, one, two, weight, across, cot, cot_across, grads, taps, mid, first, second, spread
+    place, one, two, weight, across, cot, cot_across, middle, begun, turned,
+    grads, taps, mid, first, second, spread,
 ):
     even = place[0] == 0
-
-    def rows(k):
-        here = slice(224 + 32 * k, 256 + 32 * k)
-        return jnp.concatenate(
-            [weight[:, here].reshape(128, 128), across[:, here].reshape(128, 128)], axis=0
-        )
-
     left, right = pair_shift(0), pair_shift(2)
     for y in range(2):
         low, high = low_and_high(
@@ -140,18 +160,15 @@
             jnp.concatenate([one[0, y], one[1, y]], axis=1),
             jnp.concatenate([two[0, y], two[1, y]], axis=1),
         )
-        mine = jnp.concatenate([own[0, y], own[1, y]], axis=1)
-        for a, cells in enumerate((low, mine, high)):
+        taps[1, y] = middle[y]
+        for a, cells in ((0, low), (2, high)):
             taps[a, y, 0:128] = dot(cells, left).astype(BF)
             taps[a, y, 128:256] = cells
             taps[a, y, 256:384] = dot(cells, right).astype(BF)
     for y in range(2):
-        pre = None
-        for a in range(3):
-            base = 9 * a + 3 * (1 - y)
-            w = jnp.concatenate([rows(base + j) for j in range(6)], axis=1)
-            part = dot(w, taps[a].reshape(768, 256))
-            pre = part if pre is None else pre + part
+        pre = begun[y]
+        for a in (0, 2):
+            pre = pre + dot(forward_rows(weight, across, a, y), taps[a].reshape(768, 256))
         _, rate = gelu_and_slope(pre)
         pair = [
             jnp.concatenate([c[d, j, y] for c in (cot, cot_across) for d in range(4)], axis=0)
@@ -167,9 +184,8 @@
         for a in range(3):
             total = None
             for source in range(2):
-                base = 9 * a + 3 * (y - source + 1)
-                w = jnp.concatenate([rows(base + e) for e in range(3)], axis=0)
-                part = dot_tn(w, spread[source].reshape(768, 256))
+                w = turned[3 * a + y - source + 1]
+                part = dot(w, spread[source].reshape(768, 256))
                 total = part if total is None else total + part
             parts.append(total)
         down, mid[y], up = parts
@@ -357,9 +373,17 @@
     half = ((4, 2, 2, 32, 128), BF)
     cot, cot_across = call(sort_cot, (place, after(pieces[0], pooled), *pieces[1:]), (half, half), [], 0, "sort_cot")
     cot_across = lax.ppermute(cot_across, "filt", by_core)
+    middle, begun, turned = call(
+        second_start,
+        (pooled, weights, across),
+        (((2, 384, 256), BF), ((2, 256, 256), F32), ((9, 128, 768), BF)),
+        [],
+        LONG,
+        "second_start",
+    )
     grads, taps_second, mid, out_one, out_two = call(
         second_layer,
-        (place, pooled, pool_one, pool_two, weights, across, cot, cot_across),
+        (place, pool_one, pool_two, weights, across, cot, cot_across, middle, begun, turned),
         (
             ((2, 256, 256), BF),
             ((3, 2, 384, 256), BF),

time: 104 us -> 103 us (level)
  waiting for transfers between devices: 21.5 us -> 19.4 us
    ppermute x1, waiting for transfers between devices: 7.79 us -> 4.98 us  [per_device(): pool_two = lax.ppermute(pooled, 'space', twos)]
    pallas_call x12 -> x13, Pallas kernels: 15 us -> 15.1 us  [call(): pl.pallas_call(kernel, out_shape=shapes, in_specs=[SMEM if x.dtype == jnp...]
  transfers between devices with their start and end apart: 19 -> 19, of which waited for: 5 -> 6; matrix products, arithmetic and copies ran while one was open for 1% -> 1% of each run, Pallas kernels for 8% -> 10%
where the time goes in v5:
time: 103 us; the launch traced here: 102 us
  blocking collectives  36.2 us (35%)
  starting transfers between devices  28.2 us (27%)
  waiting for transfers between devices  19.4 us (19%)
  Pallas kernels  15.1 us (15%)
  local copies, waits for them, and re-layouts  2.26 us (2%)
    pallas_call x13, Pallas kernels, call(): pl.pallas_call(kernel, out_shape=shapes, in_specs=[SMEM if x.dtype == jnp...  15.1 us
    all_to_all x1, blocking collectives, per_device(): by_sample = lax.all_to_all(cotangent[0], 'space', 0, 0, tiled=True)  12.4 us
    all_to_all x1, blocking collectives, per_device(): parts = lax.all_to_all(rows.reshape(ns, 72, 128), 'space', 0, 0, tiled=True)  12 us
    all_to_all x1, blocking collectives, per_device(): rows = lax.all_to_all(mine, 'space', 0, 0, tiled=True).reshape(1152, 128)  11.7 us
    ppermute x1, starting transfers between devices, per_device(): two = lax.ppermute(inner, 'space', twos)  6.57 us
    all_to_all x1, waiting for transfers between devices, per_device(): got_first = lax.all_to_all(terms_first, 'filt', 0, 0, tiled=True)  5.94 us
    ppermute x1, waiting for transfers between devices, per_device(): pool_two = lax.ppermute(pooled, 'space', twos)  4.98 us
    ppermute x3, starting transfers between devices, per_device(): lax.ppermute(pieces[d], 'filt', by_x[d])  4.78 us
  transfers between devices with their start and end apart: 19, of which 6 were waited for; matrix products, arithmetic and copies ran while one was open for 1% of the time, Pallas kernels for 10%

profile of v5, /device:TPU:0, one launch (start us, length us, event | category | flops | bytes accessed | tf_op | source)
XLA Modules:
  0.0 102.2 jit_solution(2293839256050254353)
XLA Ops:
  0.7 1.2 %dynamic-slice_bitcast_fusion = (bf16[2,4,64,256]{3,2,1,0:T(8,128)(2,1)S(1)}, bf16[2,4,64,256]{3,2,1,0:T(8,128)(2,1)S(1)}) fusion(bf16[16,2,4,64,256]{4,3,2,1,0:T(8,128)(2,1)} %param.4, s32[]{:T(128)S(6)} %select_n.19, s32[]{:T(128)S(6)} %select_n.21, s32[]{:T(128)S(6)} %select_n.20), kind=kLoop, calls=%fused_computation.1 | loop fusion | bytes 1048588 | tf_op jit(solution)/shard_map/squeeze | solution.py:342
  1.9 0.1 pack_weights.1
  2.0 2.9 %collective-permute-start.4 = (bf16[1088,128]{1,0:T(8,128)(2,1)S(1)}, bf16[1088,128]{1,0:T(8,128)(2,1)S(1)}, u32[]{:S(2)}, u32[]{:S(2)}) collective-permute-start(bf16[1088,128]{1,0:T(8,128)(2,1)S(1)} %pack_weights.1), channel_id=1, source_target_pairs={{0,6},{1,7},{2,4},{3,5},{4,2},{5,3},{6,0},{7,1},{8,14},{9,15},{10,... | collective-permute-start | bytes 835592 | tf_op jit(solution)/shard_map/ppermute | solution.py:351
  4.9 0.8 collective-permute-start.3
  5.7 0.5 collective-permute-start.2
  6.1 6.6 %collective-permute-start.1 = (bf16[2,4,64,256]{3,2,1,0:T(8,128)(2,1)S(1)}, bf16[2,4,64,256]{3,2,1,0:T(8,128)(2,1)S(1)}, u32[]{:S(2)}, u32[]{:S(2)}) collective-permute-start(bf16[2,4,64,256]{3,2,1,0:T(8,128)(2,1)S(1)} %get-tuple-element.64), channel_id=1, source_target_pairs={{0,120},{8,16},{16,8},{24,32},{32,24},{40,48},{48,40},{56,64},{64,... | collective-permute-start | bytes 786440 | tf_op jit(solution)/shard_map/ppermute | solution.py:346
  12.7 12.4 %all_to_all.20.cot = bf16[16,2,32,128]{3,2,1,0:T(8,128)(2,1)S(1)} all-to-all(bf16[16,2,32,128]{3,2,1,0:T(8,128)(2,1)S(1)} %bitcast.20), channel_id=1, replica_groups=mesh['space'=16,'filt'=8] {'space'}, dimensions={0} | all-to-all | bytes 524288 | tf_op jit(solution)/shard_map/all_to_all | solution.py:347
  25.2 0.0 collective-permute-done.3
  25.2 0.1 pad_maximum_fusion.packed.weight
  25.3 0.1 collective-permute-start.5
  25.4 0.1 pad_add_fusion.place
  25.5 0.6 deal_cot.1
  26.1 1.6 %collective-permute-start.8 = (bf16[4,2,32,128]{3,2,1,0:T(8,128)(2,1)S(1)}, bf16[4,2,32,128]{3,2,1,0:T(8,128)(2,1)S(1)}, u32[]{:S(2)}, u32[]{:S(2)}) collective-permute-start(bf16[4,2,32,128]{3,2,1,0:T(8,128)(2,1)S(1)} %get-tuple-element.44), channel_id=1, source_target_pairs={{0,2},{1,3},{2,0},{3,1},{4,6},{5,7},{6,4},{7,5},{8,10},{9,11},{10,... | collective-permute-start | bytes 196616 | tf_op jit(solution)/shard_map/ppermute | solution.py:358
  27.7 2.7 %collective-permute-start.9 = (bf16[4,2,32,128]{3,2,1,0:T(8,128)(2,1)S(1)}, bf16[4,2,32,128]{3,2,1,0:T(8,128)(2,1)S(1)}, u32[]{:S(2)}, u32[]{:S(2)}) collective-permute-start(bf16[4,2,32,128]{3,2,1,0:T(8,128)(2,1)S(1)} %get-tuple-element.45), channel_id=1, source_target_pairs={{0,4},{1,5},{2,6},{3,7},{4,0},{5,1},{6,2},{7,3},{8,12},{9,13},{10,... | collective-permute-start | bytes 196616 | tf_op jit(solution)/shard_map/ppermute | solution.py:358
  30.4 0.5 collective-permute-start.10
  30.9 1.1 %constant_dynamic-slice_fusion.own = bf16[2,2,4,64,256]{4,3,2,1,0:T(8,128)(2,1)S(1)} fusion(bf16[16,2,4,64,256]{4,3,2,1,0:T(8,128)(2,1)} %param.4, s32[]{:T(128)S(6)} %select_n.19), kind=kLoop, calls=%fused_computation.3 | loop fusion | bytes 1048580 | tf_op jit(solution)/shard_map/dynamic_slice | solution.py:352
  32.0 0.0 collective-permute-done.5.across
  32.0 4.1 %first_forward.1 = (bf16[2,4,4,192,256]{4,3,2,1,0:T(8,128)(2,1)S(1)}, f32[2,2,4,128,256]{4,3,2,1,0:T(8,128)S(1)}, bf16[2,2,128,128]{3,2,1,0:T(8,128)(2,1)S(1)}) custom-call(s32[3]{0:T(128)S(1)} %pad_add_fusion.place, bf16[2,2,4,64,256]{4,3,2,1,0:T(8,128)(2,1)S(1)} %constant_dynamic-slice_fusion.own, bf16[2,4,64,256]{3,2,1,0:T(8,128)(2,1)S(1)} %collective-permute-done.one, ...), custom_call_target="tpu_custom_call" | custom-call | flops 20000000000 | bytes 8650764 | tf_op jit(solution)/shard_map/first_forward/pallas_call | solution.py:305
  36.0 1.4 %collective-permute-start.7 = (bf16[2,2,128,128]{3,2,1,0:T(8,128)(2,1)S(1)}, bf16[2,2,128,128]{3,2,1,0:T(8,128)(2,1)S(1)}, u32[]{:S(2)}, u32[]{:S(2)}) collective-permute-start(bf16[2,2,128,128]{3,2,1,0:T(8,128)(2,1)S(1)} %get-tuple-element.41.own), channel_id=1, source_target_pairs={{0,120},{8,16},{16,8},{24,32},{32,24},{40,48},{48,40},{56,64},{64,... | collective-permute-start | bytes 393224 | tf_op jit(solution)/shard_map/ppermute | solution.py:372
  37.5 0.0 collective-permute-start.6
  37.5 0.0 collective-permute-done.10.p3
  37.5 0.6 sort_cot.1
  38.1 0.1 collective-permute-start.11
  38.2 0.6 second_start.1
  38.8 0.7 collective-permute-done.11.cot_across
  39.5 5.0 %collective-permute-done.7.two = bf16[2,2,128,128]{3,2,1,0:T(8,128)(2,1)S(1)} collective-permute-done((bf16[2,2,128,128]{3,2,1,0:T(8,128)(2,1)S(1)}, bf16[2,2,128,128]{3,2,1,0:T(8,128)(2,1)S(1)}, u32[]{:S(2)}, u32[]{:S(2)}) %collective-permute-start.7) | collective-permute-done | bytes 131104 | tf_op jit(solution)/shard_map/ppermute | solution.py:372
  44.5 0.0 collective-permute-done.6.one
  44.5 3.1 %second_layer.1 = (bf16[2,256,256]{2,1,0:T(8,128)(2,1)S(1)}, bf16[3,2,384,256]{3,2,1,0:T(8,128)(2,1)S(1)}, f32[2,128,256]{2,1,0:T(8,128)S(1)}, bf16[2,128,256]{2,1,0:T(8,128)(2,1)S(1)}, bf16[2,128,256]{2,1,0:T(8,128)(2,1)S(1)}) custom-call(s32[3]{0:T(128)S(1)} %pad_add_fusion.place, bf16[2,2,128,128]{3,2,1,0:T(8,128)(2,1)S(1)} %collective-permute-done.6.one, ...), custom_call_target="tpu_custom_call" | custom-call | flops 2000000000 | bytes 7405580 | tf_op jit(solution)/shard_map/second_layer/pallas_call | solution.py:305
  47.6 1.0 second_weights.1
  48.6 0.1 collective-permute-start.14
  48.6 0.1 collective-permute-start.12
  48.7 2.0 %collective-permute-start.13 = (bf16[2,128,256]{2,1,0:T(8,128)(2,1)S(1)}, bf16[2,128,256]{2,1,0:T(8,128)(2,1)S(1)}, u32[]{:S(2)}, u32[]{:S(2)}) collective-permute-start(bf16[2,128,256]{2,1,0:T(8,128)(2,1)S(1)} %get-tuple-element.58), channel_id=1, source_target_pairs={{0,120},{8,16},{16,8},{24,32},{32,24},{40,48},{48,40},{56,64},{64,... | collective-permute-start | bytes 393224 | tf_op jit(solution)/shard_map/ppermute | solution.py:399
  50.8 3.8 %collective-permute-done.12.one = bf16[2,128,256]{2,1,0:T(8,128)(2,1)S(1)} collective-permute-done((bf16[2,128,256]{2,1,0:T(8,128)(2,1)S(1)}, bf16[2,128,256]{2,1,0:T(8,128)(2,1)S(1)}, u32[]{:S(2)}, u32[]{:S(2)}) %collective-permute-start.12) | collective-permute-done | bytes 131104 | tf_op jit(solution)/shard_map/ppermute | solution.py:398
  54.6 0.2 add_cores.1
  54.8 0.4 collective-permute-start.15
  55.1 3.9 %collective-permute-start.16 = (bf16[27,32,128]{2,1,0:T(8,128)(2,1)S(1)}, bf16[27,32,128]{2,1,0:T(8,128)(2,1)S(1)}, u32[]{:S(2)}, u32[]{:S(2)}) collective-permute-start(bf16[27,32,128]{2,1,0:T(8,128)(2,1)S(1)} %get-tuple-element.62), channel_id=1, source_target_pairs={{0,4},{1,5},{2,6},{3,7},{4,0},{5,1},{6,2},{7,3},{8,12},{9,13},{10,... | collective-permute-start | bytes 663560 | tf_op jit(solution)/shard_map/ppermute | solution.py:413
  59.1 0.5 collective-permute-start.17
  59.5 3.9 %first_weights.1 = bf16[8,3,16,576]{3,2,1,0:T(8,128)(2,1)} custom-call(s32[3]{0:T(128)S(1)} %pad_add_fusion.place, bf16[2,4,4,192,256]{4,3,2,1,0:T(8,128)(2,1)S(1)} %get-tuple-element.39.taps, f32[2,2,4,128,256]{4,3,2,1,0:T(8,128)S(1)} %get-tuple-element.40.slope, f32[2,128,256]{2,1,0:T(8,128)S(1)} %get-tuple-element.52.mid, ...), custom_call_target="tpu_custom_call" | custom-call | flops 20000000000 | bytes 6209548 | tf_op jit(solution)/shard_map/first_weights/pallas_call | solution.py:305
  63.4 4.0 %all-to-all-start.1 = ((bf16[8,3,16,576]{3,2,1,0:T(8,128)(2,1)}), bf16[8,3,16,576]{3,2,1,0:T(8,128)(2,1)S(1)}, u32[]{:S(2)}, u32[]{:S(2)}) async-start(bf16[8,3,16,576]{3,2,1,0:T(8,128)(2,1)} %first_weights.1), calls=%async_computation.1 | async-start | bytes 983040 | tf_op jit(solution)/shard_map/all_to_all | solution.py:422
  67.5 1.4 %collective-permute-done.16.two = bf16[27,32,128]{2,1,0:T(8,128)(2,1)S(1)} collective-permute-done((bf16[27,32,128]{2,1,0:T(8,128)(2,1)S(1)}, bf16[27,32,128]{2,1,0:T(8,128)(2,1)S(1)}, u32[]{:S(2)}, u32[]{:S(2)}) %collective-permute-start.16) | collective-permute-done | bytes 221216 | tf_op jit(solution)/shard_map/ppermute | solution.py:413
  68.9 2.6 %collective-permute-done.17.three = bf16[27,32,128]{2,1,0:T(8,128)(2,1)S(1)} collective-permute-done((bf16[27,32,128]{2,1,0:T(8,128)(2,1)S(1)}, bf16[27,32,128]{2,1,0:T(8,128)(2,1)S(1)}, u32[]{:S(2)}, u32[]{:S(2)}) %collective-permute-start.17) | collective-permute-done | bytes 221216 | tf_op jit(solution)/shard_map/ppermute | solution.py:413
  71.4 0.1 add_across.1.second
  71.5 5.9 %all-to-all-done.1.first = bf16[8,3,16,576]{3,2,1,0:T(8,128)(2,1)S(1)} async-done(((bf16[8,3,16,576]{3,2,1,0:T(8,128)(2,1)}), bf16[8,3,16,576]{3,2,1,0:T(8,128)(2,1)S(1)}, u32[]{:S(2)}, u32[]{:S(2)}) %all-to-all-start.1) | async-done | bytes 442400 | tf_op jit(solution)/shard_map/all_to_all | solution.py:422
  77.5 0.1 pack.1
  77.6 12.0 %all_to_all.21.parts = bf16[16,72,128]{2,1,0:T(8,128)(2,1)S(1)} all-to-all(bf16[16,72,128]{2,1,0:T(8,128)(2,1)S(1)} %bitcast.15), channel_id=1, replica_groups=mesh['space'=16,'filt'=8] {'space'}, dimensions={0} | all-to-all | bytes 589824 | tf_op jit(solution)/shard_map/all_to_all | solution.py:428
  89.6 0.1 add_up.1
  89.6 11.7 %all_to_all.22 = bf16[16,72,128]{2,1,0:T(8,128)(2,1)S(1)} all-to-all(bf16[16,72,128]{2,1,0:T(8,128)(2,1)S(1)} %add_up.1), channel_id=1, replica_groups=mesh['space'=16,'filt'=8] {'space'}, dimensions={0} | all-to-all | bytes 589824 | tf_op jit(solution)/shard_map/all_to_all | solution.py:430
  101.3 0.9 unpack.1
  (16 shorter events, 0.0 us)
Async XLA Ops:
  0.6 1.2 %copy-start.1 = (bf16[27,16,64]{2,1,0:T(8,128)(2,1)S(1)}, bf16[27,16,64]{2,1,0:T(8,128)(2,1)}, u32[]{:S(2)}) copy-start(bf16[27,16,64]{2,1,0:T(8,128)(2,1)} %weight) | copy-start | bytes 165892
  0.6 1.2 %copy-start = (bf16[27,32,128]{2,1,0:T(8,128)(2,1)S(1)}, bf16[27,32,128]{2,1,0:T(8,128)(2,1)}, u32[]{:S(2)}) copy-start(bf16[27,32,128]{2,1,0:T(8,128)(2,1)} %second.1) | copy-start | bytes 663556
  0.7 12.1 %copy-start.2 = (bf16[1,16,2,32,128]{4,3,2,1,0:T(8,128)(2,1)S(1)}, bf16[1,16,2,32,128]{4,3,2,1,0:T(8,128)(2,1)}, u32[]{:S(2)}) copy-start(bf16[1,16,2,32,128]{4,3,2,1,0:T(8,128)(2,1)} %param.7) | copy-start | bytes 786436
  2.0 23.2 %collective-permute-start.4 = (bf16[1088,128]{1,0:T(8,128)(2,1)S(1)}, bf16[1088,128]{1,0:T(8,128)(2,1)S(1)}, u32[]{:S(2)}, u32[]{:S(2)}) collective-permute-start(bf16[1088,128]{1,0:T(8,128)(2,1)S(1)} %pack_weights.1), channel_id=1, source_target_pairs={{0,6},{1,7},{2,4},{3,5},{4,2},{5,3},{6,0},{7,1},{8,14},{9,15},{10,... | collective-permute-start | bytes 835592 | tf_op jit(solution)/shard_map/ppermute | solution.py:351
  4.9 20.3 %collective-permute-start.3 = (bf16[1088,128]{1,0:T(8,128)(2,1)S(1)}, bf16[1088,128]{1,0:T(8,128)(2,1)S(1)}, u32[]{:S(2)}, u32[]{:S(2)}) collective-permute-start(bf16[1088,128]{1,0:T(8,128)(2,1)S(1)} %pack_weights.1), channel_id=1, source_target_pairs={{0,4},{1,5},{2,6},{3,7},{4,0},{5,1},{6,2},{7,3},{8,12},{9,13},{10,... | collective-permute-start | bytes 835592 | tf_op jit(solution)/shard_map/ppermute | solution.py:351
  5.7 19.5 %collective-permute-start.2 = (bf16[1088,128]{1,0:T(8,128)(2,1)S(1)}, bf16[1088,128]{1,0:T(8,128)(2,1)S(1)}, u32[]{:S(2)}, u32[]{:S(2)}) collective-permute-start(bf16[1088,128]{1,0:T(8,128)(2,1)S(1)} %pack_weights.1), channel_id=1, source_target_pairs={{0,2},{1,3},{2,0},{3,1},{4,6},{5,7},{6,4},{7,5},{8,10},{9,11},{10,... | collective-permute-start | bytes 835592 | tf_op jit(solution)/shard_map/ppermute | solution.py:351
  6.1 19.0 %collective-permute-start.1 = (bf16[2,4,64,256]{3,2,1,0:T(8,128)(2,1)S(1)}, bf16[2,4,64,256]{3,2,1,0:T(8,128)(2,1)S(1)}, u32[]{:S(2)}, u32[]{:S(2)}) collective-permute-start(bf16[2,4,64,256]{3,2,1,0:T(8,128)(2,1)S(1)} %get-tuple-element.64), channel_id=1, source_target_pairs={{0,120},{8,16},{16,8},{24,32},{32,24},{40,48},{48,40},{56,64},{64,... | collective-permute-start | bytes 786440 | tf_op jit(solution)/shard_map/ppermute | solution.py:346
  12.7 12.5 %collective-permute-start = (bf16[2,4,64,256]{3,2,1,0:T(8,128)(2,1)S(1)}, bf16[2,4,64,256]{3,2,1,0:T(8,128)(2,1)S(1)}, u32[]{:S(2)}, u32[]{:S(2)}) collective-permute-start(bf16[2,4,64,256]{3,2,1,0:T(8,128)(2,1)S(1)} %get-tuple-element.65), channel_id=1, source_target_pairs={{0,8},{8,0},{16,24},{24,16},{32,40},{40,32},{48,56},{56,48},{64,72... | collective-permute-start | bytes 786440 | tf_op jit(solution)/shard_map/ppermute | solution.py:345
  25.3 6.6 %collective-permute-start.5 = (bf16[4,1088,128]{2,1,0:T(8,128)(2,1)S(1)}, bf16[4,1088,128]{2,1,0:T(8,128)(2,1)S(1)}, u32[]{:S(2)}, u32[]{:S(2)}) collective-permute-start(bf16[4,1088,128]{2,1,0:T(8,128)(2,1)S(1)} %pad_maximum_fusion.packed.weight), channel_id=1, source_target_pairs={{0,1},{1,0},{2,3},{3,2},{4,5},{5,4},{6,7},{7,6},{8,9},{9,8},{10,11... | collective-permute-start | bytes 3342344 | tf_op jit(solution)/shard_map/ppermute | solution.py:354
  26.1 11.4 %collective-permute-start.8 = (bf16[4,2,32,128]{3,2,1,0:T(8,128)(2,1)S(1)}, bf16[4,2,32,128]{3,2,1,0:T(8,128)(2,1)S(1)}, u32[]{:S(2)}, u32[]{:S(2)}) collective-permute-start(bf16[4,2,32,128]{3,2,1,0:T(8,128)(2,1)S(1)} %get-tuple-element.44), channel_id=1, source_target_pairs={{0,2},{1,3},{2,0},{3,1},{4,6},{5,7},{6,4},{7,5},{8,10},{9,11},{10,... | collective-permute-start | bytes 196616 | tf_op jit(solution)/shard_map/ppermute | solution.py:358
  27.7 9.8 %collective-permute-start.9 = (bf16[4,2,32,128]{3,2,1,0:T(8,128)(2,1)S(1)}, bf16[4,2,32,128]{3,2,1,0:T(8,128)(2,1)S(1)}, u32[]{:S(2)}, u32[]{:S(2)}) collective-permute-start(bf16[4,2,32,128]{3,2,1,0:T(8,128)(2,1)S(1)} %get-tuple-element.45), channel_id=1, source_target_pairs={{0,4},{1,5},{2,6},{3,7},{4,0},{5,1},{6,2},{7,3},{8,12},{9,13},{10,... | collective-permute-start | bytes 196616 | tf_op jit(solution)/shard_map/ppermute | solution.py:358
  30.4 7.1 %collective-permute-start.10 = (bf16[4,2,32,128]{3,2,1,0:T(8,128)(2,1)S(1)}, bf16[4,2,32,128]{3,2,1,0:T(8,128)(2,1)S(1)}, u32[]{:S(2)}, u32[]{:S(2)}) collective-permute-start(bf16[4,2,32,128]{3,2,1,0:T(8,128)(2,1)S(1)} %get-tuple-element.46), channel_id=1, source_target_pairs={{0,6},{1,7},{2,4},{3,5},{4,2},{5,3},{6,0},{7,1},{8,14},{9,15},{10,... | collective-permute-start | bytes 196616 | tf_op jit(solution)/shard_map/ppermute | solution.py:358
  36.0 8.4 %collective-permute-start.7 = (bf16[2,2,128,128]{3,2,1,0:T(8,128)(2,1)S(1)}, bf16[2,2,128,128]{3,2,1,0:T(8,128)(2,1)S(1)}, u32[]{:S(2)}, u32[]{:S(2)}) collective-permute-start(bf16[2,2,128,128]{3,2,1,0:T(8,128)(2,1)S(1)} %get-tuple-element.41.own), channel_id=1, source_target_pairs={{0,120},{8,16},{16,8},{24,32},{32,24},{40,48},{48,40},{56,64},{64,... | collective-permute-start | bytes 393224 | tf_op jit(solution)/shard_map/ppermute | solution.py:372
  37.5 7.0 %collective-permute-start.6 = (bf16[2,2,128,128]{3,2,1,0:T(8,128)(2,1)S(1)}, bf16[2,2,128,128]{3,2,1,0:T(8,128)(2,1)S(1)}, u32[]{:S(2)}, u32[]{:S(2)}) collective-permute-start(bf16[2,2,128,128]{3,2,1,0:T(8,128)(2,1)S(1)} %get-tuple-element.41.own), channel_id=1, source_target_pairs={{0,8},{8,0},{16,24},{24,16},{32,40},{40,32},{48,56},{56,48},{64,72... | collective-permute-start | bytes 393224 | tf_op jit(solution)/shard_map/ppermute | solution.py:371
  38.1 1.4 %collective-permute-start.11 = (bf16[4,2,2,32,128]{4,3,2,1,0:T(8,128)(2,1)S(1)}, bf16[4,2,2,32,128]{4,3,2,1,0:T(8,128)(2,1)S(1)}, u32[]{:S(2)}, u32[]{:S(2)}) collective-permute-start(bf16[4,2,2,32,128]{4,3,2,1,0:T(8,128)(2,1)S(1)} %get-tuple-element.48), channel_id=1, source_target_pairs={{0,1},{1,0},{2,3},{3,2},{4,5},{5,4},{6,7},{7,6},{8,9},{9,8},{10,11... | collective-permute-start | bytes 393224 | tf_op jit(solution)/shard_map/ppermute | solution.py:375
  48.6 6.0 %collective-permute-start.14 = (bf16[4,27,32,128]{3,2,1,0:T(8,128)(2,1)S(1)}, bf16[4,27,32,128]{3,2,1,0:T(8,128)(2,1)S(1)}, u32[]{:S(2)}, u32[]{:S(2)}) collective-permute-start(bf16[4,27,32,128]{3,2,1,0:T(8,128)(2,1)S(1)} %get-tuple-element.59), channel_id=1, source_target_pairs={{0,1},{1,0},{2,3},{3,2},{4,5},{5,4},{6,7},{7,6},{8,9},{9,8},{10,11... | collective-permute-start | bytes 2654216 | tf_op jit(solution)/shard_map/ppermute | solution.py:408
  48.6 5.9 %collective-permute-start.12 = (bf16[2,128,256]{2,1,0:T(8,128)(2,1)S(1)}, bf16[2,128,256]{2,1,0:T(8,128)(2,1)S(1)}, u32[]{:S(2)}, u32[]{:S(2)}) collective-permute-start(bf16[2,128,256]{2,1,0:T(8,128)(2,1)S(1)} %get-tuple-element.53), channel_id=1, source_target_pairs={{0,8},{8,0},{16,24},{24,16},{32,40},{40,32},{48,56},{56,48},{64,72... | collective-permute-start | bytes 393224 | tf_op jit(solution)/shard_map/ppermute | solution.py:398
  48.7 10.8 %collective-permute-start.13 = (bf16[2,128,256]{2,1,0:T(8,128)(2,1)S(1)}, bf16[2,128,256]{2,1,0:T(8,128)(2,1)S(1)}, u32[]{:S(2)}, u32[]{:S(2)}) collective-permute-start(bf16[2,128,256]{2,1,0:T(8,128)(2,1)S(1)} %get-tuple-element.58), channel_id=1, source_target_pairs={{0,120},{8,16},{16,8},{24,32},{32,24},{40,48},{48,40},{56,64},{64,... | collective-permute-start | bytes 393224 | tf_op jit(solution)/shard_map/ppermute | solution.py:399
  54.8 12.7 %collective-permute-start.15 = (bf16[27,32,128]{2,1,0:T(8,128)(2,1)S(1)}, bf16[27,32,128]{2,1,0:T(8,128)(2,1)S(1)}, u32[]{:S(2)}, u32[]{:S(2)}) collective-permute-start(bf16[27,32,128]{2,1,0:T(8,128)(2,1)S(1)} %get-tuple-element.61), channel_id=1, source_target_pairs={{0,2},{1,3},{2,0},{3,1},{4,6},{5,7},{6,4},{7,5},{8,10},{9,11},{10,... | collective-permute-start | bytes 663560 | tf_op jit(solution)/shard_map/ppermute | solution.py:413
  55.1 13.7 %collective-permute-start.16 = (bf16[27,32,128]{2,1,0:T(8,128)(2,1)S(1)}, bf16[27,32,128]{2,1,0:T(8,128)(2,1)S(1)}, u32[]{:S(2)}, u32[]{:S(2)}) collective-permute-start(bf16[27,32,128]{2,1,0:T(8,128)(2,1)S(1)} %get-tuple-element.62), channel_id=1, source_target_pairs={{0,4},{1,5},{2,6},{3,7},{4,0},{5,1},{6,2},{7,3},{8,12},{9,13},{10,... | collective-permute-start | bytes 663560 | tf_op jit(solution)/shard_map/ppermute | solution.py:413
  59.1 12.4 %collective-permute-start.17 = (bf16[27,32,128]{2,1,0:T(8,128)(2,1)S(1)}, bf16[27,32,128]{2,1,0:T(8,128)(2,1)S(1)}, u32[]{:S(2)}, u32[]{:S(2)}) collective-permute-start(bf16[27,32,128]{2,1,0:T(8,128)(2,1)S(1)} %get-tuple-element.63), channel_id=1, source_target_pairs={{0,6},{1,7},{2,4},{3,5},{4,2},{5,3},{6,0},{7,1},{8,14},{9,15},{10,... | collective-permute-start | bytes 663560 | tf_op jit(solution)/shard_map/ppermute | solution.py:413
  63.4 14.0 %all-to-all-start.1 = ((bf16[8,3,16,576]{3,2,1,0:T(8,128)(2,1)}), bf16[8,3,16,576]{3,2,1,0:T(8,128)(2,1)S(1)}, u32[]{:S(2)}, u32[]{:S(2)}) async-start(bf16[8,3,16,576]{3,2,1,0:T(8,128)(2,1)} %first_weights.1), calls=%async_computation.1 | async-start | bytes 983040 | tf_op jit(solution)/shard_map/all_to_all | solution.py:422

commit v6 on v5

--- a/solution.py
+++ b/solution.py
@@ -27,9 +27,8 @@
 
 def gelu_and_slope(v):
     square = v * v
-    t = jnp.tanh(ROOT * v * (1.0 + CUBE * square))
-    half = 0.5 * (1.0 + t)
-    slope = half + 0.5 * v * (1.0 - t * t) * (ROOT * (1.0 + 3.0 * CUBE * square))
+    half = 0.5 + 0.5 * jnp.tanh(v * (ROOT + ROOT * CUBE * square))
+    slope = half + (half - half * half) * (v * (2.0 * ROOT + 6.0 * ROOT * CUBE * square))
     return v * half, slope
 
 
@@ -250,7 +249,7 @@
                     total[a, 0:384] += part[192:576, 128:]
 
     for a in range(3):
-        out[:, a] = total[a].T.astype(BF).reshape(8, 16, 576)
+        out[:, a] = total[a].astype(BF).T.reshape(8, 16, 576)
 
 
 def add_across(own, one, two, three, out):

time: 103 us -> 102 us (level)
  no operation moved by 1% of the time
where the time goes in v6:
time: 102 us
  blocking collectives  36.2 us (35%)
  starting transfers between devices  28.1 us (28%)
  waiting for transfers between devices  19.4 us (19%)
  Pallas kernels  15 us (15%)
  local copies, waits for them, and re-layouts  2.26 us (2%)
    pallas_call x13, Pallas kernels, call(): pl.pallas_call(kernel, out_shape=shapes, in_specs=[SMEM if x.dtype == jnp...  15 us
    all_to_all x1, blocking collectives, per_device(): by_sample = lax.all_to_all(cotangent[0], 'space', 0, 0, tiled=True)  12.4 us
    all_to_all x1, blocking collectives, per_device(): parts = lax.all_to_all(rows.reshape(ns, 72, 128), 'space', 0, 0, tiled=True)  12 us
    all_to_all x1, blocking collectives, per_device(): rows = lax.all_to_all(mine, 'space', 0, 0, tiled=True).reshape(1152, 128)  11.7 us
    ppermute x1, starting transfers between devices, per_device(): two = lax.ppermute(inner, 'space', twos)  6.57 us
    all_to_all x1, waiting for transfers between devices, per_device(): got_first = lax.all_to_all(terms_first, 'filt', 0, 0, tiled=True)  5.93 us
    ppermute x1, waiting for transfers between devices, per_device(): pool_two = lax.ppermute(pooled, 'space', twos)  4.99 us
    ppermute x3, starting transfers between devices, per_device(): lax.ppermute(others[d - 1], 'filt', by_x[d])  4.78 us
  transfers between devices with their start and end apart: 19, of which 6 were waited for; matrix products, arithmetic and copies ran while one was open for 1% of the time, Pallas kernels for 10%

profile of v6, /device:TPU:0, one launch (start us, length us, event | category | flops | bytes accessed | tf_op | source)
XLA Modules:
  0.0 102.1 jit_solution(14264125828366306493)
XLA Ops:
  0.7 1.2 %dynamic-slice_bitcast_fusion = (bf16[2,4,64,256]{3,2,1,0:T(8,128)(2,1)S(1)}, bf16[2,4,64,256]{3,2,1,0:T(8,128)(2,1)S(1)}) fusion(bf16[16,2,4,64,256]{4,3,2,1,0:T(8,128)(2,1)} %param.4, s32[]{:T(128)S(6)} %select_n.19, s32[]{:T(128)S(6)} %select_n.21, s32[]{:T(128)S(6)} %select_n.20), kind=kLoop, calls=%fused_computation.1 | loop fusion | bytes 1048588 | tf_op jit(solution)/shard_map/squeeze | solution.py:341
  1.9 0.1 pack_weights.1
  2.0 2.9 %collective-permute-start.4 = (bf16[1088,128]{1,0:T(8,128)(2,1)S(1)}, bf16[1088,128]{1,0:T(8,128)(2,1)S(1)}, u32[]{:S(2)}, u32[]{:S(2)}) collective-permute-start(bf16[1088,128]{1,0:T(8,128)(2,1)S(1)} %pack_weights.1), channel_id=1, source_target_pairs={{0,6},{1,7},{2,4},{3,5},{4,2},{5,3},{6,0},{7,1},{8,14},{9,15},{10,... | collective-permute-start | bytes 835592 | tf_op jit(solution)/shard_map/ppermute | solution.py:350
  4.9 0.8 collective-permute-start.3
  5.7 0.5 collective-permute-start.2
  6.1 6.6 %collective-permute-start.1 = (bf16[2,4,64,256]{3,2,1,0:T(8,128)(2,1)S(1)}, bf16[2,4,64,256]{3,2,1,0:T(8,128)(2,1)S(1)}, u32[]{:S(2)}, u32[]{:S(2)}) collective-permute-start(bf16[2,4,64,256]{3,2,1,0:T(8,128)(2,1)S(1)} %get-tuple-element.64), channel_id=1, source_target_pairs={{0,120},{8,16},{16,8},{24,32},{32,24},{40,48},{48,40},{56,64},{64,... | collective-permute-start | bytes 786440 | tf_op jit(solution)/shard_map/ppermute | solution.py:345
  12.7 12.4 %all_to_all.20.cot = bf16[16,2,32,128]{3,2,1,0:T(8,128)(2,1)S(1)} all-to-all(bf16[16,2,32,128]{3,2,1,0:T(8,128)(2,1)S(1)} %bitcast.20), channel_id=1, replica_groups=mesh['space'=16,'filt'=8] {'space'}, dimensions={0} | all-to-all | bytes 524288 | tf_op jit(solution)/shard_map/all_to_all | solution.py:346
  25.2 0.0 collective-permute-done.3
  25.2 0.1 pad_maximum_fusion.packed.weight
  25.3 0.1 collective-permute-start.5
  25.4 0.1 pad_add_fusion.place
  25.5 0.6 deal_cot.1
  26.1 1.6 %collective-permute-start.8 = (bf16[4,2,32,128]{3,2,1,0:T(8,128)(2,1)S(1)}, bf16[4,2,32,128]{3,2,1,0:T(8,128)(2,1)S(1)}, u32[]{:S(2)}, u32[]{:S(2)}) collective-permute-start(bf16[4,2,32,128]{3,2,1,0:T(8,128)(2,1)S(1)} %get-tuple-element.44), channel_id=1, source_target_pairs={{0,2},{1,3},{2,0},{3,1},{4,6},{5,7},{6,4},{7,5},{8,10},{9,11},{10,... | collective-permute-start | bytes 196616 | tf_op jit(solution)/shard_map/ppermute | solution.py:357
  27.7 2.7 %collective-permute-start.9 = (bf16[4,2,32,128]{3,2,1,0:T(8,128)(2,1)S(1)}, bf16[4,2,32,128]{3,2,1,0:T(8,128)(2,1)S(1)}, u32[]{:S(2)}, u32[]{:S(2)}) collective-permute-start(bf16[4,2,32,128]{3,2,1,0:T(8,128)(2,1)S(1)} %get-tuple-element.45), channel_id=1, source_target_pairs={{0,4},{1,5},{2,6},{3,7},{4,0},{5,1},{6,2},{7,3},{8,12},{9,13},{10,... | collective-permute-start | bytes 196616 | tf_op jit(solution)/shard_map/ppermute | solution.py:357
  30.4 0.5 collective-permute-start.10
  30.9 1.1 %constant_dynamic-slice_fusion.own = bf16[2,2,4,64,256]{4,3,2,1,0:T(8,128)(2,1)S(1)} fusion(bf16[16,2,4,64,256]{4,3,2,1,0:T(8,128)(2,1)} %param.4, s32[]{:T(128)S(6)} %select_n.19), kind=kLoop, calls=%fused_computation.3 | loop fusion | bytes 1048580 | tf_op jit(solution)/shard_map/dynamic_slice | solution.py:351
  32.0 0.0 collective-permute-done.5.across
  32.0 4.0 %first_forward.1 = (bf16[2,4,4,192,256]{4,3,2,1,0:T(8,128)(2,1)S(1)}, f32[2,2,4,128,256]{4,3,2,1,0:T(8,128)S(1)}, bf16[2,2,128,128]{3,2,1,0:T(8,128)(2,1)S(1)}) custom-call(s32[3]{0:T(128)S(1)} %pad_add_fusion.place, bf16[2,2,4,64,256]{4,3,2,1,0:T(8,128)(2,1)S(1)} %constant_dynamic-slice_fusion.own, bf16[2,4,64,256]{3,2,1,0:T(8,128)(2,1)S(1)} %collective-permute-done.one, ...), custom_call_target="tpu_custom_call" | custom-call | flops 20000000000 | bytes 8650764 | tf_op jit(solution)/shard_map/first_forward/pallas_call | solution.py:304
  36.0 1.4 %collective-permute-start.7 = (bf16[2,2,128,128]{3,2,1,0:T(8,128)(2,1)S(1)}, bf16[2,2,128,128]{3,2,1,0:T(8,128)(2,1)S(1)}, u32[]{:S(2)}, u32[]{:S(2)}) collective-permute-start(bf16[2,2,128,128]{3,2,1,0:T(8,128)(2,1)S(1)} %get-tuple-element.41.own), channel_id=1, source_target_pairs={{0,120},{8,16},{16,8},{24,32},{32,24},{40,48},{48,40},{56,64},{64,... | collective-permute-start | bytes 393224 | tf_op jit(solution)/shard_map/ppermute | solution.py:371
  37.4 0.0 collective-permute-done.10.p3
  37.5 0.6 sort_cot.1
  38.0 0.1 collective-permute-start.11
  38.1 0.6 second_start.1
  38.7 0.7 collective-permute-done.11.cot_across
  39.5 5.0 %collective-permute-done.7.two = bf16[2,2,128,128]{3,2,1,0:T(8,128)(2,1)S(1)} collective-permute-done((bf16[2,2,128,128]{3,2,1,0:T(8,128)(2,1)S(1)}, bf16[2,2,128,128]{3,2,1,0:T(8,128)(2,1)S(1)}, u32[]{:S(2)}, u32[]{:S(2)}) %collective-permute-start.7) | collective-permute-done | bytes 131104 | tf_op jit(solution)/shard_map/ppermute | solution.py:371
  44.4 0.0 collective-permute-done.6.one
  44.4 3.0 %second_layer.1 = (bf16[2,256,256]{2,1,0:T(8,128)(2,1)S(1)}, bf16[3,2,384,256]{3,2,1,0:T(8,128)(2,1)S(1)}, f32[2,128,256]{2,1,0:T(8,128)S(1)}, bf16[2,128,256]{2,1,0:T(8,128)(2,1)S(1)}, bf16[2,128,256]{2,1,0:T(8,128)(2,1)S(1)}) custom-call(s32[3]{0:T(128)S(1)} %pad_add_fusion.place, bf16[2,2,128,128]{3,2,1,0:T(8,128)(2,1)S(1)} %collective-permute-done.6.one, ...), custom_call_target="tpu_custom_call" | custom-call | flops 2000000000 | bytes 7405580 | tf_op jit(solution)/shard_map/second_layer/pallas_call | solution.py:304
  47.5 1.0 second_weights.1
  48.5 0.1 collective-permute-start.14
  48.6 0.1 collective-permute-start.12
  48.6 2.0 %collective-permute-start.13 = (bf16[2,128,256]{2,1,0:T(8,128)(2,1)S(1)}, bf16[2,128,256]{2,1,0:T(8,128)(2,1)S(1)}, u32[]{:S(2)}, u32[]{:S(2)}) collective-permute-start(bf16[2,128,256]{2,1,0:T(8,128)(2,1)S(1)} %get-tuple-element.58), channel_id=1, source_target_pairs={{0,120},{8,16},{16,8},{24,32},{32,24},{40,48},{48,40},{56,64},{64,... | collective-permute-start | bytes 393224 | tf_op jit(solution)/shard_map/ppermute | solution.py:398
  50.7 3.8 %collective-permute-done.12.one = bf16[2,128,256]{2,1,0:T(8,128)(2,1)S(1)} collective-permute-done((bf16[2,128,256]{2,1,0:T(8,128)(2,1)S(1)}, bf16[2,128,256]{2,1,0:T(8,128)(2,1)S(1)}, u32[]{:S(2)}, u32[]{:S(2)}) %collective-permute-start.12) | collective-permute-done | bytes 131104 | tf_op jit(solution)/shard_map/ppermute | solution.py:397
  54.5 0.2 add_cores.1
  54.7 0.4 collective-permute-start.15
  55.0 3.9 %collective-permute-start.16 = (bf16[27,32,128]{2,1,0:T(8,128)(2,1)S(1)}, bf16[27,32,128]{2,1,0:T(8,128)(2,1)S(1)}, u32[]{:S(2)}, u32[]{:S(2)}) collective-permute-start(bf16[27,32,128]{2,1,0:T(8,128)(2,1)S(1)} %get-tuple-element.62), channel_id=1, source_target_pairs={{0,4},{1,5},{2,6},{3,7},{4,0},{5,1},{6,2},{7,3},{8,12},{9,13},{10,... | collective-permute-start | bytes 663560 | tf_op jit(solution)/shard_map/ppermute | solution.py:412
  59.0 0.5 collective-permute-start.17
  59.5 0.0 collective-permute-done.13.two
  59.5 3.9 %first_weights.1 = bf16[8,3,16,576]{3,2,1,0:T(8,128)(2,1)} custom-call(s32[3]{0:T(128)S(1)} %pad_add_fusion.place, bf16[2,4,4,192,256]{4,3,2,1,0:T(8,128)(2,1)S(1)} %get-tuple-element.39.taps, f32[2,2,4,128,256]{4,3,2,1,0:T(8,128)S(1)} %get-tuple-element.40.slope, f32[2,128,256]{2,1,0:T(8,128)S(1)} %get-tuple-element.52.mid, ...), custom_call_target="tpu_custom_call" | custom-call | flops 20000000000 | bytes 6209548 | tf_op jit(solution)/shard_map/first_weights/pallas_call | solution.py:304
  63.4 4.0 %all-to-all-start.1 = ((bf16[8,3,16,576]{3,2,1,0:T(8,128)(2,1)}), bf16[8,3,16,576]{3,2,1,0:T(8,128)(2,1)S(1)}, u32[]{:S(2)}, u32[]{:S(2)}) async-start(bf16[8,3,16,576]{3,2,1,0:T(8,128)(2,1)} %first_weights.1), calls=%async_computation.1 | async-start | bytes 983040 | tf_op jit(solution)/shard_map/all_to_all | solution.py:421
  67.4 1.4 %collective-permute-done.16.two = bf16[27,32,128]{2,1,0:T(8,128)(2,1)S(1)} collective-permute-done((bf16[27,32,128]{2,1,0:T(8,128)(2,1)S(1)}, bf16[27,32,128]{2,1,0:T(8,128)(2,1)S(1)}, u32[]{:S(2)}, u32[]{:S(2)}) %collective-permute-start.16) | collective-permute-done | bytes 221216 | tf_op jit(solution)/shard_map/ppermute | solution.py:412
  68.8 2.6 %collective-permute-done.17.three = bf16[27,32,128]{2,1,0:T(8,128)(2,1)S(1)} collective-permute-done((bf16[27,32,128]{2,1,0:T(8,128)(2,1)S(1)}, bf16[27,32,128]{2,1,0:T(8,128)(2,1)S(1)}, u32[]{:S(2)}, u32[]{:S(2)}) %collective-permute-start.17) | collective-permute-done | bytes 221216 | tf_op jit(solution)/shard_map/ppermute | solution.py:412
  71.3 0.1 add_across.1.second
  71.4 5.9 %all-to-all-done.1.first = bf16[8,3,16,576]{3,2,1,0:T(8,128)(2,1)S(1)} async-done(((bf16[8,3,16,576]{3,2,1,0:T(8,128)(2,1)}), bf16[8,3,16,576]{3,2,1,0:T(8,128)(2,1)S(1)}, u32[]{:S(2)}, u32[]{:S(2)}) %all-to-all-start.1) | async-done | bytes 442400 | tf_op jit(solution)/shard_map/all_to_all | solution.py:421
  77.4 0.1 pack.1
  77.5 12.0 %all_to_all.21.parts = bf16[16,72,128]{2,1,0:T(8,128)(2,1)S(1)} all-to-all(bf16[16,72,128]{2,1,0:T(8,128)(2,1)S(1)} %bitcast.15), channel_id=1, replica_groups=mesh['space'=16,'filt'=8] {'space'}, dimensions={0} | all-to-all | bytes 589824 | tf_op jit(solution)/shard_map/all_to_all | solution.py:427
  89.5 0.1 add_up.1
  89.5 11.7 %all_to_all.22 = bf16[16,72,128]{2,1,0:T(8,128)(2,1)S(1)} all-to-all(bf16[16,72,128]{2,1,0:T(8,128)(2,1)S(1)} %add_up.1), channel_id=1, replica_groups=mesh['space'=16,'filt'=8] {'space'}, dimensions={0} | all-to-all | bytes 589824 | tf_op jit(solution)/shard_map/all_to_all | solution.py:429
  101.2 0.9 unpack.1
  (16 shorter events, 0.0 us)
Async XLA Ops:
  0.6 1.2 %copy-start.1 = (bf16[27,16,64]{2,1,0:T(8,128)(2,1)S(1)}, bf16[27,16,64]{2,1,0:T(8,128)(2,1)}, u32[]{:S(2)}) copy-start(bf16[27,16,64]{2,1,0:T(8,128)(2,1)} %weight) | copy-start | bytes 165892
  0.6 1.2 %copy-start = (bf16[27,32,128]{2,1,0:T(8,128)(2,1)S(1)}, bf16[27,32,128]{2,1,0:T(8,128)(2,1)}, u32[]{:S(2)}) copy-start(bf16[27,32,128]{2,1,0:T(8,128)(2,1)} %second.1) | copy-start | bytes 663556
  0.7 12.1 %copy-start.2 = (bf16[1,16,2,32,128]{4,3,2,1,0:T(8,128)(2,1)S(1)}, bf16[1,16,2,32,128]{4,3,2,1,0:T(8,128)(2,1)}, u32[]{:S(2)}) copy-start(bf16[1,16,2,32,128]{4,3,2,1,0:T(8,128)(2,1)} %param.7) | copy-start | bytes 786436
  2.0 23.2 %collective-permute-start.4 = (bf16[1088,128]{1,0:T(8,128)(2,1)S(1)}, bf16[1088,128]{1,0:T(8,128)(2,1)S(1)}, u32[]{:S(2)}, u32[]{:S(2)}) collective-permute-start(bf16[1088,128]{1,0:T(8,128)(2,1)S(1)} %pack_weights.1), channel_id=1, source_target_pairs={{0,6},{1,7},{2,4},{3,5},{4,2},{5,3},{6,0},{7,1},{8,14},{9,15},{10,... | collective-permute-start | bytes 835592 | tf_op jit(solution)/shard_map/ppermute | solution.py:350
  4.9 20.3 %collective-permute-start.3 = (bf16[1088,128]{1,0:T(8,128)(2,1)S(1)}, bf16[1088,128]{1,0:T(8,128)(2,1)S(1)}, u32[]{:S(2)}, u32[]{:S(2)}) collective-permute-start(bf16[1088,128]{1,0:T(8,128)(2,1)S(1)} %pack_weights.1), channel_id=1, source_target_pairs={{0,4},{1,5},{2,6},{3,7},{4,0},{5,1},{6,2},{7,3},{8,12},{9,13},{10,... | collective-permute-start | bytes 835592 | tf_op jit(solution)/shard_map/ppermute | solution.py:350
  5.7 19.5 %collective-permute-start.2 = (bf16[1088,128]{1,0:T(8,128)(2,1)S(1)}, bf16[1088,128]{1,0:T(8,128)(2,1)S(1)}, u32[]{:S(2)}, u32[]{:S(2)}) collective-permute-start(bf16[1088,128]{1,0:T(8,128)(2,1)S(1)} %pack_weights.1), channel_id=1, source_target_pairs={{0,2},{1,3},{2,0},{3,1},{4,6},{5,7},{6,4},{7,5},{8,10},{9,11},{10,... | collective-permute-start | bytes 835592 | tf_op jit(solution)/shard_map/ppermute | solution.py:350
  6.1 19.0 %collective-permute-start.1 = (bf16[2,4,64,256]{3,2,1,0:T(8,128)(2,1)S(1)}, bf16[2,4,64,256]{3,2,1,0:T(8,128)(2,1)S(1)}, u32[]{:S(2)}, u32[]{:S(2)}) collective-permute-start(bf16[2,4,64,256]{3,2,1,0:T(8,128)(2,1)S(1)} %get-tuple-element.64), channel_id=1, source_target_pairs={{0,120},{8,16},{16,8},{24,32},{32,24},{40,48},{48,40},{56,64},{64,... | collective-permute-start | bytes 786440 | tf_op jit(solution)/shard_map/ppermute | solution.py:345
  12.7 12.5 %collective-permute-start = (bf16[2,4,64,256]{3,2,1,0:T(8,128)(2,1)S(1)}, bf16[2,4,64,256]{3,2,1,0:T(8,128)(2,1)S(1)}, u32[]{:S(2)}, u32[]{:S(2)}) collective-permute-start(bf16[2,4,64,256]{3,2,1,0:T(8,128)(2,1)S(1)} %get-tuple-element.65), channel_id=1, source_target_pairs={{0,8},{8,0},{16,24},{24,16},{32,40},{40,32},{48,56},{56,48},{64,72... | collective-permute-start | bytes 786440 | tf_op jit(solution)/shard_map/ppermute | solution.py:344
  25.3 6.6 %collective-permute-start.5 = (bf16[4,1088,128]{2,1,0:T(8,128)(2,1)S(1)}, bf16[4,1088,128]{2,1,0:T(8,128)(2,1)S(1)}, u32[]{:S(2)}, u32[]{:S(2)}) collective-permute-start(bf16[4,1088,128]{2,1,0:T(8,128)(2,1)S(1)} %pad_maximum_fusion.packed.weight), channel_id=1, source_target_pairs={{0,1},{1,0},{2,3},{3,2},{4,5},{5,4},{6,7},{7,6},{8,9},{9,8},{10,11... | collective-permute-start | bytes 3342344 | tf_op jit(solution)/shard_map/ppermute | solution.py:353
  26.1 11.3 %collective-permute-start.8 = (bf16[4,2,32,128]{3,2,1,0:T(8,128)(2,1)S(1)}, bf16[4,2,32,128]{3,2,1,0:T(8,128)(2,1)S(1)}, u32[]{:S(2)}, u32[]{:S(2)}) collective-permute-start(bf16[4,2,32,128]{3,2,1,0:T(8,128)(2,1)S(1)} %get-tuple-element.44), channel_id=1, source_target_pairs={{0,2},{1,3},{2,0},{3,1},{4,6},{5,7},{6,4},{7,5},{8,10},{9,11},{10,... | collective-permute-start | bytes 196616 | tf_op jit(solution)/shard_map/ppermute | solution.py:357
  27.7 9.8 %collective-permute-start.9 = (bf16[4,2,32,128]{3,2,1,0:T(8,128)(2,1)S(1)}, bf16[4,2,32,128]{3,2,1,0:T(8,128)(2,1)S(1)}, u32[]{:S(2)}, u32[]{:S(2)}) collective-permute-start(bf16[4,2,32,128]{3,2,1,0:T(8,128)(2,1)S(1)} %get-tuple-element.45), channel_id=1, source_target_pairs={{0,4},{1,5},{2,6},{3,7},{4,0},{5,1},{6,2},{7,3},{8,12},{9,13},{10,... | collective-permute-start | bytes 196616 | tf_op jit(solution)/shard_map/ppermute | solution.py:357
  30.4 7.1 %collective-permute-start.10 = (bf16[4,2,32,128]{3,2,1,0:T(8,128)(2,1)S(1)}, bf16[4,2,32,128]{3,2,1,0:T(8,128)(2,1)S(1)}, u32[]{:S(2)}, u32[]{:S(2)}) collective-permute-start(bf16[4,2,32,128]{3,2,1,0:T(8,128)(2,1)S(1)} %get-tuple-element.46), channel_id=1, source_target_pairs={{0,6},{1,7},{2,4},{3,5},{4,2},{5,3},{6,0},{7,1},{8,14},{9,15},{10,... | collective-permute-start | bytes 196616 | tf_op jit(solution)/shard_map/ppermute | solution.py:357
  36.0 8.4 %collective-permute-start.7 = (bf16[2,2,128,128]{3,2,1,0:T(8,128)(2,1)S(1)}, bf16[2,2,128,128]{3,2,1,0:T(8,128)(2,1)S(1)}, u32[]{:S(2)}, u32[]{:S(2)}) collective-permute-start(bf16[2,2,128,128]{3,2,1,0:T(8,128)(2,1)S(1)} %get-tuple-element.41.own), channel_id=1, source_target_pairs={{0,120},{8,16},{16,8},{24,32},{32,24},{40,48},{48,40},{56,64},{64,... | collective-permute-start | bytes 393224 | tf_op jit(solution)/shard_map/ppermute | solution.py:371
  37.4 7.0 %collective-permute-start.6 = (bf16[2,2,128,128]{3,2,1,0:T(8,128)(2,1)S(1)}, bf16[2,2,128,128]{3,2,1,0:T(8,128)(2,1)S(1)}, u32[]{:S(2)}, u32[]{:S(2)}) collective-permute-start(bf16[2,2,128,128]{3,2,1,0:T(8,128)(2,1)S(1)} %get-tuple-element.41.own), channel_id=1, source_target_pairs={{0,8},{8,0},{16,24},{24,16},{32,40},{40,32},{48,56},{56,48},{64,72... | collective-permute-start | bytes 393224 | tf_op jit(solution)/shard_map/ppermute | solution.py:370
  38.0 1.4 %collective-permute-start.11 = (bf16[4,2,2,32,128]{4,3,2,1,0:T(8,128)(2,1)S(1)}, bf16[4,2,2,32,128]{4,3,2,1,0:T(8,128)(2,1)S(1)}, u32[]{:S(2)}, u32[]{:S(2)}) collective-permute-start(bf16[4,2,2,32,128]{4,3,2,1,0:T(8,128)(2,1)S(1)} %get-tuple-element.48), channel_id=1, source_target_pairs={{0,1},{1,0},{2,3},{3,2},{4,5},{5,4},{6,7},{7,6},{8,9},{9,8},{10,11... | collective-permute-start | bytes 393224 | tf_op jit(solution)/shard_map/ppermute | solution.py:374
  48.5 6.0 %collective-permute-start.14 = (bf16[4,27,32,128]{3,2,1,0:T(8,128)(2,1)S(1)}, bf16[4,27,32,128]{3,2,1,0:T(8,128)(2,1)S(1)}, u32[]{:S(2)}, u32[]{:S(2)}) collective-permute-start(bf16[4,27,32,128]{3,2,1,0:T(8,128)(2,1)S(1)} %get-tuple-element.59), channel_id=1, source_target_pairs={{0,1},{1,0},{2,3},{3,2},{4,5},{5,4},{6,7},{7,6},{8,9},{9,8},{10,11... | collective-permute-start | bytes 2654216 | tf_op jit(solution)/shard_map/ppermute | solution.py:407
  48.6 5.9 %collective-permute-start.12 = (bf16[2,128,256]{2,1,0:T(8,128)(2,1)S(1)}, bf16[2,128,256]{2,1,0:T(8,128)(2,1)S(1)}, u32[]{:S(2)}, u32[]{:S(2)}) collective-permute-start(bf16[2,128,256]{2,1,0:T(8,128)(2,1)S(1)} %get-tuple-element.53), channel_id=1, source_target_pairs={{0,8},{8,0},{16,24},{24,16},{32,40},{40,32},{48,56},{56,48},{64,72... | collective-permute-start | bytes 393224 | tf_op jit(solution)/shard_map/ppermute | solution.py:397
  48.6 10.8 %collective-permute-start.13 = (bf16[2,128,256]{2,1,0:T(8,128)(2,1)S(1)}, bf16[2,128,256]{2,1,0:T(8,128)(2,1)S(1)}, u32[]{:S(2)}, u32[]{:S(2)}) collective-permute-start(bf16[2,128,256]{2,1,0:T(8,128)(2,1)S(1)} %get-tuple-element.58), channel_id=1, source_target_pairs={{0,120},{8,16},{16,8},{24,32},{32,24},{40,48},{48,40},{56,64},{64,... | collective-permute-start | bytes 393224 | tf_op jit(solution)/shard_map/ppermute | solution.py:398
  54.7 12.7 %collective-permute-start.15 = (bf16[27,32,128]{2,1,0:T(8,128)(2,1)S(1)}, bf16[27,32,128]{2,1,0:T(8,128)(2,1)S(1)}, u32[]{:S(2)}, u32[]{:S(2)}) collective-permute-start(bf16[27,32,128]{2,1,0:T(8,128)(2,1)S(1)} %get-tuple-element.61), channel_id=1, source_target_pairs={{0,2},{1,3},{2,0},{3,1},{4,6},{5,7},{6,4},{7,5},{8,10},{9,11},{10,... | collective-permute-start | bytes 663560 | tf_op jit(solution)/shard_map/ppermute | solution.py:412
  55.0 13.7 %collective-permute-start.16 = (bf16[27,32,128]{2,1,0:T(8,128)(2,1)S(1)}, bf16[27,32,128]{2,1,0:T(8,128)(2,1)S(1)}, u32[]{:S(2)}, u32[]{:S(2)}) collective-permute-start(bf16[27,32,128]{2,1,0:T(8,128)(2,1)S(1)} %get-tuple-element.62), channel_id=1, source_target_pairs={{0,4},{1,5},{2,6},{3,7},{4,0},{5,1},{6,2},{7,3},{8,12},{9,13},{10,... | collective-permute-start | bytes 663560 | tf_op jit(solution)/shard_map/ppermute | solution.py:412
  59.0 12.4 %collective-permute-start.17 = (bf16[27,32,128]{2,1,0:T(8,128)(2,1)S(1)}, bf16[27,32,128]{2,1,0:T(8,128)(2,1)S(1)}, u32[]{:S(2)}, u32[]{:S(2)}) collective-permute-start(bf16[27,32,128]{2,1,0:T(8,128)(2,1)S(1)} %get-tuple-element.63), channel_id=1, source_target_pairs={{0,6},{1,7},{2,4},{3,5},{4,2},{5,3},{6,0},{7,1},{8,14},{9,15},{10,... | collective-permute-start | bytes 663560 | tf_op jit(solution)/shard_map/ppermute | solution.py:412
  63.4 14.0 %all-to-all-start.1 = ((bf16[8,3,16,576]{3,2,1,0:T(8,128)(2,1)}), bf16[8,3,16,576]{3,2,1,0:T(8,128)(2,1)S(1)}, u32[]{:S(2)}, u32[]{:S(2)}) async-start(bf16[8,3,16,576]{3,2,1,0:T(8,128)(2,1)} %first_weights.1), calls=%async_computation.1 | async-start | bytes 983040 | tf_op jit(solution)/shard_map/all_to_all | solution.py:421
